TPU v7x, 256 devices: a whole 4x4x8 slice. The times are simulated.
256 devices in a mesh: dp: 64 (over z, x, core), group: 4 (over y).
Axes of the slice: x: 4, y: 4, z: 8, core: 2. Of those that a mesh axis runs over, the one named last changes fastest.
Arguments:
- train_grads: float32 [262144, 1024], P(('dp', 'group')), may hold values from -50 to 50
- val_grads: float32 [128, 32, 1024], P('dp', 'group'), may hold values from -6 to 6
- wanted: int32 [64, 64], replicated, may hold values from -1 to 127, as said below
- owner: int32 [64], replicated, may hold values from 0 to 63, each once
Outputs:
- scores: float32 [262144, 2048], P(('dp', 'group'))
Inputs may be any that keep to these rules, and one draw needn't show every extreme that they name: wanted[b, j] is -1 or the id of a validation block stored on index j of dp, one of j * 2 to j * 2 + 1; training blocks differ in how many slots are used.
All inputs are finite; a program needn't handle non-finite values.
Results may differ from a plain program's by a relative error of at most 0.0003.
Values sent between devices are 32-bit elements; how exact they have to be, the bound alone decides.
No kernel may reach another device: no remote copies, remote signals or barrier semaphores. Data moves between devices by JAX's collectives and lax.ppermute only.
A program may use at most 128 MiB of HBM per device.

v0:
```python
import jax
import jax.numpy as jnp
from jax import lax
from jax.sharding import PartitionSpec as P

damping = 0.1


def cholesky_apply(factor, right_side):
    middle = lax.linalg.triangular_solve(factor, right_side, left_side=True, lower=True)
    return lax.linalg.triangular_solve(factor, middle, left_side=True, lower=True, transpose_a=True)


def solve_blocks(factor, blocks_in):
    features = blocks_in.shape[-1]
    flat_rows = blocks_in.reshape(-1, features)
    return cholesky_apply(factor, flat_rows.T).T.reshape(blocks_in.shape)


def local(train_grads, val_grads, wanted, owner):
    highest = lax.Precision.HIGHEST
    partial_gram = lax.dot_general(
        train_grads, train_grads, (((0,), (0,)), ((), ())), precision=highest
    )
    summed = lax.psum(partial_gram, ("dp", "group"))
    features = summed.shape[0]
    rows_total = train_grads.shape[0] * lax.axis_size("dp") * lax.axis_size("group")
    gram_matrix = summed / rows_total + damping * jnp.eye(features, dtype=jnp.float32)
    factor = jnp.linalg.cholesky(gram_matrix)
    blocks = val_grads.shape[0]
    devices = lax.axis_size("dp")
    own_index = lax.axis_index("dp")
    positions = jnp.arange(devices, dtype=jnp.int32)
    holder = jnp.sum(jnp.where(owner[None, :] == positions[:, None], positions[None, :], 0), axis=1)
    requests = wanted[holder]
    column = lax.dynamic_slice_in_dim(requests, own_index, 1, 1)[:, 0]
    local_id = column - own_index * blocks
    chooser = (
        (local_id[:, None] == jnp.arange(blocks, dtype=jnp.int32)[None, :]) & (column[:, None] >= 0)
    ).astype(jnp.float32)
    score_scale = features ** (-0.5)
    source = solve_blocks(factor, val_grads)
    outgoing = jnp.einsum("iv,vqk->iqk", chooser, source, precision=highest)
    arrived = lax.all_to_all(outgoing, "dp", split_axis=0, concat_axis=0, tiled=True)
    tiled = (
        lax.dot_general(
            train_grads,
            lax.all_gather(arrived, "group", axis=1, tiled=True),
            (((1,), (2,)), ((), ())),
            precision=highest,
        )
        * score_scale
    )
    scores = tiled.reshape(train_grads.shape[0], -1)
    return scores


def solution(mesh):
    in_specs = (P(("dp", "group"), None), P("dp", "group", None), P(), P())
    out_specs = P(("dp", "group"), None)
    return jax.shard_map(local, mesh=mesh, in_specs=in_specs, out_specs=out_specs, check_vma=False)
```

profile of v0, /device:TPU:1, one launch (start us, length us, event | category | flops | bytes accessed | tf_op | source)
XLA Modules:
  0.0 848.0 jit_solution(1581101890622879077)
XLA Ops:
  6.5 17.8 %fusion.111 = f32[1024,1024]{0,1:T(8,128)} fusion(f32[1024,1024]{1,0:T(8,128)} %param.4), kind=kOutput, calls=%fused_computation.235 | convolution fusion | flops 12884901888 | bytes 8388608 | tf_op jit(solution)/shard_map/dot_general | solution.py:22
  26.3 269.0 %all-reduce.3.cloned.1.call-done = f32[1024,1024]{0,1:T(8,128)} async-done(((f32[1024,1024]{0,1:T(8,128)}), f32[1024,1024]{0,1:T(8,128)}) %all-reduce.3.cloned.1.call-update) | async-done | bytes 4194320 | tf_op jit(solution)/shard_map/psum | solution.py:25
  295.3 5.1 select_add_fusion
  300.4 5.5 copy.77
  305.9 4.5 fusion.3
  310.4 2.0 copy-done.3
  312.4 11.7 %cholesky.222 = f32[128,128]{1,0:T(8,128)S(1)} custom-call(f32[128,128]{1,0:T(8,128)S(1)} %cholesky.577), custom_call_target="Cholesky" | custom-call | tf_op jit(solution)/shard_map/jit(cholesky)/cholesky | solution.py:29
  324.2 9.8 %custom-call.64 = f32[1,128,128]{1,2,0:T(8,128)S(1)} custom-call(f32[1,128,128]{2,1,0:T(8,128)S(1)} %get-tuple-element.52), custom_call_target="InvertDiagBlocksLowerTriangular" | custom-call | tf_op jit(solution)/shard_map/jit(cholesky)/cholesky | solution.py:29
  334.1 1.5 fusion.16
  335.6 1.6 convolution_subtract_fusion
  337.4 11.7 %cholesky.243 = f32[128,128]{1,0:T(8,128)S(1)} custom-call(f32[128,128]{1,0:T(8,128)S(1)} %cholesky.581), custom_call_target="Cholesky" | custom-call | tf_op jit(solution)/shard_map/jit(cholesky)/cholesky | solution.py:29
  349.4 9.8 %custom-call.65 = f32[1,128,128]{1,2,0:T(8,128)S(1)} custom-call(f32[1,128,128]{2,1,0:T(8,128)S(1)} %get-tuple-element.50), custom_call_target="InvertDiagBlocksLowerTriangular" | custom-call | tf_op jit(solution)/shard_map/jit(cholesky)/cholesky | solution.py:29
  360.3 1.9 copy-done.2
  362.3 2.4 convolution_subtract_fusion.1
  364.7 11.7 %cholesky.466 = f32[128,128]{1,0:T(8,128)S(1)} custom-call(f32[128,128]{1,0:T(8,128)S(1)} %cholesky.586), custom_call_target="Cholesky" | custom-call | tf_op jit(solution)/shard_map/jit(cholesky)/cholesky | solution.py:29
  377.2 9.8 %custom-call.66 = f32[1,128,128]{1,2,0:T(8,128)S(1)} custom-call(f32[1,128,128]{2,1,0:T(8,128)S(1)} %get-tuple-element.48), custom_call_target="InvertDiagBlocksLowerTriangular" | custom-call | tf_op jit(solution)/shard_map/jit(cholesky)/cholesky | solution.py:29
  387.0 1.2 convolution_dynamic-update-slice_fusion.1
  388.2 3.5 convolution_subtract_fusion.2
  391.8 11.7 %cholesky.485 = f32[128,128]{1,0:T(8,128)S(1)} custom-call(f32[128,128]{1,0:T(8,128)S(1)} %cholesky.591), custom_call_target="Cholesky" | custom-call | tf_op jit(solution)/shard_map/jit(cholesky)/cholesky | solution.py:29
  404.3 9.8 %custom-call.67 = f32[1,128,128]{1,2,0:T(8,128)S(1)} custom-call(f32[1,128,128]{2,1,0:T(8,128)S(1)} %get-tuple-element.46), custom_call_target="InvertDiagBlocksLowerTriangular" | custom-call | tf_op jit(solution)/shard_map/jit(cholesky)/cholesky | solution.py:29
  414.1 1.1 convolution_dynamic-update-slice_fusion.2
  415.2 3.1 convolution_subtract_fusion.3
  418.4 11.9 %cholesky.504 = f32[128,128]{1,0:T(8,128)S(1)} custom-call(f32[128,128]{1,0:T(8,128)S(1)} %cholesky.596), custom_call_target="Cholesky" | custom-call | tf_op jit(solution)/shard_map/jit(cholesky)/cholesky | solution.py:29
  431.0 9.8 %custom-call.68 = f32[1,128,128]{1,2,0:T(8,128)S(1)} custom-call(f32[1,128,128]{2,1,0:T(8,128)S(1)} %get-tuple-element.44), custom_call_target="InvertDiagBlocksLowerTriangular" | custom-call | tf_op jit(solution)/shard_map/jit(cholesky)/cholesky | solution.py:29
  440.8 1.1 convolution_dynamic-update-slice_fusion.3
  441.9 3.1 convolution_subtract_fusion.4
  445.0 11.7 %cholesky.524 = f32[128,128]{1,0:T(8,128)S(1)} custom-call(f32[128,128]{1,0:T(8,128)S(1)} %cholesky.601), custom_call_target="Cholesky" | custom-call | tf_op jit(solution)/shard_map/jit(cholesky)/cholesky | solution.py:29
  457.5 9.8 %custom-call.69 = f32[1,128,128]{1,2,0:T(8,128)S(1)} custom-call(f32[1,128,128]{2,1,0:T(8,128)S(1)} %get-tuple-element.42), custom_call_target="InvertDiagBlocksLowerTriangular" | custom-call | tf_op jit(solution)/shard_map/jit(cholesky)/cholesky | solution.py:29
  468.3 2.9 convolution_subtract_fusion.5
  471.2 11.7 %cholesky.544 = f32[128,128]{1,0:T(8,128)S(1)} custom-call(f32[128,128]{1,0:T(8,128)S(1)} %cholesky.606), custom_call_target="Cholesky" | custom-call | tf_op jit(solution)/shard_map/jit(cholesky)/cholesky | solution.py:29
  483.7 9.8 %custom-call.70 = f32[1,128,128]{1,2,0:T(8,128)S(1)} custom-call(f32[1,128,128]{2,1,0:T(8,128)S(1)} %get-tuple-element.40), custom_call_target="InvertDiagBlocksLowerTriangular" | custom-call | tf_op jit(solution)/shard_map/jit(cholesky)/cholesky | solution.py:29
  494.5 2.1 convolution_subtract_fusion.6
  496.6 11.7 %cholesky.562 = f32[128,128]{1,0:T(8,128)S(1)} custom-call(f32[128,128]{1,0:T(8,128)S(1)} %convolution_subtract_fusion.6), custom_call_target="Cholesky" | custom-call | tf_op jit(solution)/shard_map/jit(cholesky)/cholesky | solution.py:29
  518.7 4.9 select_select_fusion
  523.7 24.4 %while.1 = (s32[]{:T(128)}, f32[1024,1024]{0,1:T(8,128)}, s32[8,2]{0,1:T(2,128)S(1)}, f32[8,128,128]{2,1,0:T(8,128)S(1)}, s32[]{:T(128)}) while((s32[]{:T(128)}, f32[1024,1024]{0,1:T(8,128)}, s32[8,2]{0,1:T(2,128)S(1)}, f32[8,128,128]{2,1,0:T(8,128)S(1)}, s32[]{:T(128)}) %tuple.52), condition=%wide.while_cond, body=%wide.while_body.sunk | while | flops 2 | bytes 393329 | solution.py:11
  524.3 2.2 dynamic-slice.7
  527.4 2.2 dynamic-slice.7
  530.4 2.2 dynamic-slice.7
  533.5 2.2 dynamic-slice.7
  536.6 2.2 dynamic-slice.7
  539.6 2.2 dynamic-slice.7
  542.7 2.2 dynamic-slice.7
  545.7 2.2 dynamic-slice.7
  548.0 79.0 %custom-call.71 = f32[8,128,128]{1,2,0:T(8,128)S(1)} custom-call(f32[8,128,128]{2,1,0:T(8,128)S(1)} %get-tuple-element.12), custom_call_target="InvertDiagBlocksLowerTriangular" | custom-call | tf_op jit(solution)/shard_map/triangular_solve | solution.py:11
  628.4 1.1 convolution_subtract_fusion.13
  629.7 1.2 convolution_subtract_fusion.12
  631.0 1.2 convolution_subtract_fusion.11
  632.4 1.3 convolution_subtract_fusion.20
  633.9 1.3 convolution_subtract_fusion.19
  635.4 1.4 convolution_subtract_fusion.18
  637.1 1.1 convolution_subtract_fusion.10
  638.4 1.1 convolution_subtract_fusion.9
  639.8 1.3 convolution_subtract_fusion.8
  641.2 1.3 convolution_subtract_fusion.7
  642.8 1.4 convolution_subtract_fusion.17
  644.5 1.4 convolution_subtract_fusion.16
  646.2 1.5 convolution_subtract_fusion.15
  648.0 1.0 fusion.49
  649.1 1.2 copy.95
  650.3 60.5 %all_to_all.5 = f32[64,8,1024]{2,1,0:T(8,128)S(1)} all-to-all(f32[64,8,1024]{2,1,0:T(8,128)S(1)} %copy.95), channel_id=1, replica_groups=mesh['dp'=64,'group'=4] {'dp'}, dimensions={0} | all-to-all | bytes 4194304 | tf_op jit(solution)/shard_map/all_to_all | solution.py:44
  710.8 2.5 copy.96
  713.4 82.3 %all-gather.2.cloned.1.call-done = f32[64,32,1024]{2,0,1:T(8,128)} async-done(((f32[64,8,1024]{2,0,1:T(8,128)}), f32[64,32,1024]{2,0,1:T(8,128)}) %all-gather.2.cloned.1.call-update) | async-done | bytes 8388624 | tf_op jit(solution)/shard_map/all_gather | solution.py:48
  795.7 36.2 %broadcast_multiply_fusion = f32[64,32,1024]{2,1,0:T(8,128)} fusion(f32[1024,1024]{1,0:T(8,128)} %param.4, f32[64,32,1024]{2,0,1:T(8,128)} %all-gather.2.cloned.1.call-done), kind=kOutput, calls=%fused_computation.9 | convolution fusion | flops 25771900928 | bytes 20971520 | tf_op jit(solution)/shard_map/dot_general | solution.py:46
  831.8 9.1 %copy.98 = f32[1024,2048]{1,0:T(8,128)} copy(f32[1024,2048]{0,1:T(8,128)} %bitcast.145) | data formatting | bytes 16777216 | tf_op jit(solution)/shard_map/reshape | solution.py:54
  (138 shorter events, 25.3 us)
Async XLA Ops:
  6.5 18.8 %copy-start = (s32[64,64]{1,0:T(8,128)S(1)}, s32[64,64]{1,0:T(8,128)}, u32[]{:S(2)}) copy-start(s32[64,64]{1,0:T(8,128)} %param.6) | copy-start | bytes 49156
  6.5 288.8 %all-reduce.3.cloned.1.call-start = ((), (), s32[]{:S(2)}) async-start(), calls=%async_computation.1 | async-start | bytes 8388608 | tf_op jit(solution)/shard_map/psum | solution.py:25
  24.3 0.7 copy-start.5
  24.3 771.3 %all-gather.2.cloned.1.call-start = ((), (), s32[]{:S(2)}) async-start(), calls=%async_computation.2 | async-start | bytes 10485760 | tf_op jit(solution)/shard_map/all_gather | solution.py:48
  310.4 2.0 copy-start.3
  360.3 1.9 copy-start.2
  518.7 108.4 %copy-start.4 = (f32[2,8,1024]{2,1,0:T(8,128)S(1)}, f32[2,8,1024]{2,1,0:T(8,128)}, u32[]{:S(2)}) copy-start(f32[2,8,1024]{2,1,0:T(8,128)} %param.5) | copy-start | bytes 196612
  831.8 9.1 %copy-start.1 = (s32[64,64]{1,0:T(8,128)S(1)}, s32[64,64]{1,0:T(8,128)}, u32[]{:S(2)}) copy-start(s32[64,64]{1,0:T(8,128)} %param.6) | copy-start | bytes 49156
Sparse Core Ops, SparseCore 0:
  24.5 270.8 all-reduce.2
  713.5 82.1 all-gather.1
where the time goes:
time: 856 us; the launch traced here: 848 us
  waiting for transfers between devices  351 us (41%)
  other arithmetic  261 us (30%)
  matrix products  102 us (12%)
  blocking collectives  60.5 us (7%)
  local copies, waits for them, and re-layouts  53.5 us (6%)
  between operations  19.2 us (2%)
    psum x1, waiting for transfers between devices, local(): summed = lax.psum(partial_gram, ('dp', 'group'))  269 us
    another operation x30, other arithmetic, local(): factor = jnp.linalg.cholesky(gram_matrix)  167 us
    another operation x3, other arithmetic, cholesky_apply(): lax.linalg.triangular_solve(factor, middle, left_side=True, lower=True, t...  83.9 us
    all_gather x1, waiting for transfers between devices, local(): lax.all_gather(arrived, 'group', axis=1, tiled=True)  82.3 us
    all_to_all x1, blocking collectives, local(): lax.all_to_all(outgoing, 'dp', split_axis=0, concat_axis=0, tiled=True)  60.5 us
    dot_general x1, matrix products, local(): lax.dot_general(train_grads, lax.all_gather(arrived, 'group', axis=1, til...  36.2 us
    another operation x14, matrix products, local(): factor = jnp.linalg.cholesky(gram_matrix)  26.1 us
    another operation x40, local copies, waits for them, and re-layouts  24.1 us
  transfers between devices with their start and end apart: 2, of which 2 were waited for; matrix products, arithmetic and copies ran while one was open for 0% of the time, Pallas kernels for 0%

commit v1 on v0

v1 whole, which is shorter than its diff:
```python
import functools
import jax
import jax.numpy as jnp
from jax import lax
from jax.experimental import pallas as pl
from jax.experimental.pallas import tpu as pltpu
from jax.sharding import Mesh, PartitionSpec as P

HIGHEST = lax.Precision.HIGHEST
damping = 0.1


def dot_nn(a, b):
    return lax.dot_general(a, b, (((1,), (0,)), ((), ())), precision=HIGHEST, preferred_element_type=jnp.float32)


def dot_nt(a, b):
    return lax.dot_general(a, b, (((1,), (1,)), ((), ())), precision=HIGHEST, preferred_element_type=jnp.float32)


def dot_tn(a, b):
    return lax.dot_general(a, b, (((0,), (0,)), ((), ())), precision=HIGHEST, preferred_element_type=jnp.float32)


def reciprocal(p):
    r = pl.reciprocal(p, approx=True)
    r = r * (2.0 - p * r)
    return r * (2.0 - p * r)


def inverse_128(matrix):
    rows = [matrix[8 * r:8 * r + 8, :] for r in range(16)]
    lane = lax.broadcasted_iota(jnp.int32, (8, 128), 1)
    sub = lax.broadcasted_iota(jnp.int32, (8, 128), 0)
    spread = lambda x, l: jnp.broadcast_to(x[:, l:l + 1], (8, 128))
    row_of = lambda x, i: jnp.broadcast_to(x[i:i + 1, :], (8, 128))
    for kb in range(16):
        in_block = (lane >= 8 * kb) & (lane < 8 * kb + 8)
        unit = (lane - 8 * kb == sub).astype(jnp.float32)
        held = rows[kb]
        cols = [spread(held, 8 * kb + i) for i in range(8)]
        z = jnp.where(in_block, unit, held)
        for i in range(0, 8, 2):
            first, second = cols[i], cols[i + 1]
            a, b, c = row_of(first, i), row_of(second, i), row_of(second, i + 1)
            r = reciprocal(a * c - b * b)
            at_i, at_j = sub == i, sub == i + 1
            pivots = at_i | at_j
            m0 = jnp.where(at_i, -1.0, jnp.where(at_j, 0.0, first))
            m1 = jnp.where(at_j, -1.0, jnp.where(at_i, 0.0, second))
            f0 = (m0 * c - m1 * b) * r
            f1 = (m1 * a - m0 * b) * r
            step = lambda v: jnp.where(pivots, 0.0, v) - f0 * row_of(v, i) - f1 * row_of(v, i + 1)
            z = step(z)
            for j in range(i + 2, 8):
                cols[j] = step(cols[j])
        z = jnp.where(in_block, -z, z)
        z_rows = [row_of(z, i) for i in range(8)]
        order = [(kb + 1 + r) % 16 for r in range(15)]
        for r in order:
            old = rows[r]
            acc = jnp.where(in_block, 0.0, old)
            for i in range(8):
                acc = acc - spread(old, 8 * kb + i) * z_rows[i]
            rows[r] = acc
        rows[kb] = z
    return -jnp.concatenate(rows, axis=0)


def factor_kernel(n, scale, g_ref, l_ref, d_ref, a_ref):
    place = lambda i, j: j * n - j * (j - 1) // 2 + (i - j)
    blocks = n * (n + 1) // 2
    eye = (lax.broadcasted_iota(jnp.int32, (256, 256), 0) == lax.broadcasted_iota(jnp.int32, (256, 256), 1)).astype(jnp.float32)
    diagonal = [place(j, j) for j in range(n)]
    for k in range(blocks):
        block = jnp.concatenate([g_ref[2 * k], g_ref[2 * k + 1]], axis=1) * scale
        a_ref[k] = block + damping * eye if k in diagonal else block
    def column_step(j, _):
        p = j * n - (j * (j - 1)) // 2
        d = a_ref.at[p]
        d11 = d[0:128, 0:128]
        d21 = d[128:256, 0:128]
        d22 = d[128:256, 128:256]
        i11 = inverse_128(d11)
        x = dot_nn(d21, i11)
        i22 = inverse_128(d22 - dot_nt(x, d21))
        u = dot_nn(i22, x)
        d_ref[j, 0:128, 0:128] = i11 + dot_tn(x, u)
        d_ref[j, 128:256, 0:128] = -u
        d_ref[j, 0:128, 128:256] = -u.T
        d_ref[j, 128:256, 128:256] = i22
        def panel(i, _):
            q = p + i - j
            l_ref[q] = dot_nn(a_ref[q], d_ref[j])
            return 0
        lax.fori_loop(j + 1, n, panel, 0)
        def column(c, _):
            pc = c * n - (c * (c - 1)) // 2
            def block(i, _):
                a_ref[pc + i - c] = a_ref[pc + i - c] - dot_nt(l_ref[p + i - j], a_ref[p + c - j])
                return 0
            lax.fori_loop(c, n, block, 0)
            return 0
        lax.fori_loop(j + 1, n, column, 0)
        return 0
    lax.fori_loop(0, n, column_step, 0)


def factor(g, n, scale):
    blocks = n * (n + 1) // 2
    return pl.pallas_call(
        functools.partial(factor_kernel, n, scale),
        out_shape=(
            jax.ShapeDtypeStruct((blocks, 256, 256), jnp.float32),
            jax.ShapeDtypeStruct((n, 256, 256), jnp.float32),
        ),
        in_specs=[pl.BlockSpec(memory_space=pltpu.VMEM)],
        out_specs=(pl.BlockSpec(memory_space=pltpu.VMEM),) * 2,
        scratch_shapes=[pltpu.VMEM((blocks, 256, 256), jnp.float32)],
        compiler_params=pltpu.CompilerParams(vmem_limit_bytes=40 * 1024 * 1024),
    )(g)


def split(x):
    high = x.astype(jnp.bfloat16)
    return high, (x - high.astype(jnp.float32)).astype(jnp.bfloat16)


def dot3(a, b, dims):
    d = lambda u, v: lax.dot_general(u, v, (dims, ((), ())), preferred_element_type=jnp.float32)
    return d(a[0], b[1]) + d(a[1], b[0]) + d(a[0], b[0])


NN = ((1,), (0,))
NT = ((1,), (1,))


def score_kernel(n, scale, pick_ref, t_ref, l_ref, d_ref, v_ref, out_ref, wh_ref, wl_ref):
    step = pl.program_id(0)
    place = lambda i, j: j * n - j * (j - 1) // 2 + (i - j)

    @pl.when(step == 0)
    def _():
        ys = []
        for j in range(n):
            acc = t_ref[:, 256 * j:256 * j + 256]
            for i in range(j):
                acc = acc - dot3(ys[i], split(l_ref[place(j, i)]), NT)
            ys.append(split(acc))
        ws = [None] * n
        for j in reversed(range(n)):
            acc = dot3(ys[j], split(d_ref[j]), NN)
            for i in range(j + 1, n):
                acc = acc - dot3(ws[i], split(l_ref[place(i, j)]), NN)
            ws[j] = split(acc)
        for j in range(n):
            wh_ref[:, 256 * j:256 * j + 256] = ws[j][0] * jnp.bfloat16(scale)
            wl_ref[:, 256 * j:256 * j + 256] = ws[j][1] * jnp.bfloat16(scale)

    slots = v_ref.shape[0]
    rows = []
    for s in range(slots):
        pick = pick_ref[step * slots + s]
        first = (pick == 0).astype(jnp.float32)
        second = (pick == 1).astype(jnp.float32)
        for y in range(v_ref.shape[1]):
            rows.append(v_ref[s, y, 0] * first + v_ref[s, y, 1] * second)
    v = split(jnp.concatenate(rows, axis=0))
    out_ref[...] = dot3((wh_ref[...], wl_ref[...]), v, NT)


def score(pick, t, l, d, v, n, slots):
    m, features = t.shape
    total, groups, blocks, part, _ = v.shape
    width = slots * groups * part
    whole = pl.BlockSpec(memory_space=pltpu.VMEM)
    return pl.pallas_call(
        functools.partial(score_kernel, n, features ** -0.5),
        grid=(total // slots,),
        out_shape=jax.ShapeDtypeStruct((m, total * groups * part), jnp.float32),
        in_specs=[
            pl.BlockSpec(memory_space=pltpu.SMEM),
            whole, whole, whole,
            pl.BlockSpec((slots, groups, blocks, part, features), lambda i: (i, 0, 0, 0, 0)),
        ],
        out_specs=pl.BlockSpec((m, width), lambda i: (0, i)),
        scratch_shapes=[pltpu.VMEM((m, features), jnp.bfloat16)] * 2,
        compiler_params=pltpu.CompilerParams(vmem_limit_bytes=56 * 1024 * 1024),
    )(pick, t, l, d, v)


def gram_kernel(n, t_ref, g_ref, th_ref, tl_ref):
    for j in range(n):
        at = slice(256 * j, 256 * j + 256)
        high, low = split(t_ref[:, at])
        th_ref[at, :] = high.T
        tl_ref[at, :] = low.T
    k = 0
    for j in range(n):
        at = slice(256 * j, 256 * j + 256)
        right = split(t_ref[:, at])
        for i in range(j, n):
            of = slice(256 * i, 256 * i + 256)
            block = dot3((th_ref[of, :], tl_ref[of, :]), right, NN)
            g_ref[2 * k] = block[:, 0:128]
            g_ref[2 * k + 1] = block[:, 128:256]
            k += 1


def gram(t, n):
    m, features = t.shape
    return pl.pallas_call(
        functools.partial(gram_kernel, n),
        out_shape=jax.ShapeDtypeStruct((n * (n + 1), 256, 128), jnp.float32),
        in_specs=[pl.BlockSpec(memory_space=pltpu.VMEM)],
        out_specs=pl.BlockSpec(memory_space=pltpu.VMEM),
        scratch_shapes=[pltpu.VMEM((features, m), jnp.bfloat16)] * 2,
        compiler_params=pltpu.CompilerParams(vmem_limit_bytes=40 * 1024 * 1024),
    )(t)


def swap(v, axis):
    return lax.ppermute(v, axis, [(0, 1), (1, 0)])


def scatter_pair(v, axis):
    me = lax.axis_index(axis)
    mine = lax.dynamic_index_in_dim(v, me, 0, keepdims=False)
    other = lax.dynamic_index_in_dim(v, 1 - me, 0, keepdims=False)
    return mine + swap(other, axis)


def gather_pair(v, axis):
    me = lax.axis_index(axis)
    other = swap(v, axis)
    return jnp.stack([jnp.where(me == 0, v, other), jnp.where(me == 0, other, v)])


def scatter_ring(v, axis):
    size = lax.axis_size(axis)
    me = lax.axis_index(axis)
    part = lambda k: lax.dynamic_index_in_dim(v, lax.rem(me + k, size), 0, keepdims=False)
    total = part(0)
    for k in range(1, size):
        total = total + lax.ppermute(part(k), axis, [(i, (i + k) % size) for i in range(size)])
    return total


def gather_ring(v, axis):
    size = lax.axis_size(axis)
    me = lax.axis_index(axis)
    out = jnp.zeros((size,) + v.shape, v.dtype)
    out = lax.dynamic_update_index_in_dim(out, v, me, 0)
    for k in range(1, size):
        came = lax.ppermute(v, axis, [(i, (i + k) % size) for i in range(size)])
        out = lax.dynamic_update_index_in_dim(out, came, lax.rem(me + size - k, size), 0)
    return out


def scatter_direct(v, axis):
    return lax.all_to_all(v, axis, 0, 0, tiled=True).sum(0)


def gather_direct(v, axis):
    size = lax.axis_size(axis)
    return lax.all_to_all(jnp.broadcast_to(v[None], (size,) + v.shape), axis, 0, 0, tiled=True)


def sum_all(v):
    rows, lanes = v.shape
    v = scatter_pair(v.reshape(2, -1, lanes), "core")
    v = scatter_ring(v.reshape(lax.axis_size("y"), -1, lanes), "y")
    v = scatter_ring(v.reshape(lax.axis_size("x"), -1, lanes), "x")
    v = scatter_direct(v.reshape(lax.axis_size("z"), -1, lanes), "z")
    v = gather_direct(v, "z").reshape(-1, lanes)
    v = gather_ring(v, "x").reshape(-1, lanes)
    v = gather_ring(v, "y").reshape(-1, lanes)
    return gather_pair(v, "core").reshape(rows, lanes)


def local(train_grads, val_grads, wanted, owner):
    m, features = train_grads.shape
    n = features // 256
    dp = ("z", "x", "core")
    slabs, group = lax.axis_size(dp), lax.axis_size("y")
    blocks, part, _ = val_grads.shape
    val_all = lax.all_gather(val_grads, dp + ("y",), tiled=False)
    val_all = val_all.reshape(slabs, group, blocks, part, features)

    positions = jnp.arange(slabs, dtype=jnp.int32)
    holder = jnp.sum(jnp.where(owner == lax.axis_index(dp), positions, 0))
    request = lax.dynamic_index_in_dim(wanted, holder, 0, keepdims=False)
    pick = jnp.where(request >= 0, request - positions * blocks, -1)

    g = gram(train_grads, n)
    g = sum_all(g.reshape(-1, 128)).reshape(g.shape)
    l, d = factor(g, n, 1.0 / (m * slabs * group))
    return score(pick, train_grads, l, d, val_all, n, 8)


def solution(mesh):
    axes = ("z", "x", "core", "y")
    fine = Mesh(mesh.devices.reshape(8, 4, 2, 4), axes)
    dp = P(("z", "x", "core"), "y", None)
    in_specs = (P(axes, None), dp, P(), P())
    return jax.shard_map(local, mesh=fine, in_specs=in_specs, out_specs=P(axes, None), check_vma=False)
```

time: 856 us -> 189 us (0.22)
  waiting for transfers between devices: 351 us -> 43.4 us
  other arithmetic: 261 us -> 4.76 us
  matrix products: 102 us -> 0 us
  Pallas kernels: 0 us -> 74.8 us
  local copies, waits for them, and re-layouts: 53.5 us -> 7.88 us
  blocking collectives: 60.5 us -> 15.7 us
  starting transfers between devices: 0.04 us -> 26.1 us
    psum x1 -> x0, waiting for transfers between devices: 269 us -> none  [local(): summed = lax.psum(partial_gram, ('dp', 'group'))]
    another operation x33 -> x2, other arithmetic: 251 us -> 0.34 us  [gather_pair(): jnp.stack([jnp.where(me == 0, v, other), jnp.where(me == 0, other, v)])]
    all_gather x1, waiting for transfers between devices: 82.3 us -> 0.01 us  [local(): val_all = lax.all_gather(val_grads, dp + ('y',), tiled=False)]
    pallas_call x0 -> x3, Pallas kernels: none -> 74.8 us  [the longest x1 43.5 us: factor(): pl.pallas_call(functools.partial(factor_kernel, n, scale), out_shape=(jax...]
    dot_general x3 -> x0, matrix products: 55 us -> none  [the longest x1 36.2 us: local(): lax.dot_general(train_grads, lax.all_gather(arrived, 'group', axis=1, til...]
    another operation x44 -> x0, matrix products: 46.7 us -> none  [the longest x14 26.1 us: local(): factor = jnp.linalg.cholesky(gram_matrix)]
    all_to_all x1, blocking collectives: 60.5 us -> 15.7 us  [scatter_direct(): return lax.all_to_all(v, axis, 0, 0, tiled=True).sum(0)]
    ppermute x0 -> x14, waiting for transfers between devices: none -> 34.3 us  [the longest x6 18.3 us: scatter_ring(): lax.ppermute(part(k), axis, [(i, (i + k) % size) for i in range(size)])]
  transfers between devices with their start and end apart: 2 -> 16, of which waited for: 2 -> 8; matrix products, arithmetic and copies ran while one was open for 0% -> 4% of each run, Pallas kernels for 0% -> 25%
where the time goes in v1:
time: 189 us; the launch traced here: 188 us
  Pallas kernels  74.8 us (40%)
  waiting for transfers between devices  43.4 us (23%)
  starting transfers between devices  26.1 us (14%)
  blocking collectives  15.7 us (8%)
  between operations  15.6 us (8%)
  local copies, waits for them, and re-layouts  7.88 us (4%)
  other arithmetic  4.76 us (3%)
    pallas_call x1, Pallas kernels, factor(): pl.pallas_call(functools.partial(factor_kernel, n, scale), out_shape=(jax...  43.5 us
    pallas_call x1, Pallas kernels, score(): pl.pallas_call(functools.partial(score_kernel, n, features ** (-0.5)), gr...  27 us
    ppermute x6, waiting for transfers between devices, scatter_ring(): lax.ppermute(part(k), axis, [(i, (i + k) % size) for i in range(size)])  18.3 us
    all_to_all x1, blocking collectives, scatter_direct(): return lax.all_to_all(v, axis, 0, 0, tiled=True).sum(0)  15.7 us
    ppermute x6, waiting for transfers between devices, gather_ring(): came = lax.ppermute(v, axis, [(i, (i + k) % size) for i in range(size)])  13 us
    ppermute x2, starting transfers between devices, swap(): return lax.ppermute(v, axis, [(0, 1), (1, 0)])  10.5 us
    all_to_all x1, waiting for transfers between devices, gather_direct(): lax.all_to_all(jnp.broadcast_to(v[None], (size,) + v.shape), axis, 0, 0,...  8.41 us
    ppermute x6, starting transfers between devices, scatter_ring(): lax.ppermute(part(k), axis, [(i, (i + k) % size) for i in range(size)])  7.06 us
  transfers between devices with their start and end apart: 16, of which 8 were waited for; matrix products, arithmetic and copies ran while one was open for 4% of the time, Pallas kernels for 25%

profile of v1, /device:TPU:1, one launch (start us, length us, event | category | flops | bytes accessed | tf_op | source)
XLA Modules:
  0.0 188.2 jit_solution(7805710253470193759)
XLA Ops:
  6.5 0.0 all-gather.3.cloned.1.call-start
  6.5 0.7 all-gather.3.cloned.1.call-update
  7.3 0.0 copy-start
  7.3 2.2 %copy-done = f32[1024,1024]{1,0:T(8,128)S(1)} copy-done((f32[1024,1024]{1,0:T(8,128)S(1)}, f32[1024,1024]{1,0:T(8,128)}, u32[]{:S(2)}) %copy-start) | copy-done | bytes 4194328
  9.5 4.3 %shard_map.46 = f32[20,256,128]{2,1,0:T(8,128)S(1)} custom-call(f32[1024,1024]{1,0:T(8,128)S(1)} %copy-done), custom_call_target="tpu_custom_call" | custom-call | tf_op jit(solution)/shard_map/pallas_call | solution.py:212
  13.7 1.2 dynamic-slice_bitcast_fusion
  14.9 3.2 %collective-permute-start = (f32[2560,128]{1,0:T(8,128)}, f32[2560,128]{1,0:T(8,128)}, u32[]{:S(2)}, u32[]{:S(2)}) collective-permute-start(f32[2560,128]{1,0:T(8,128)} %dynamic-slice_bitcast_fusion), channel_id=1, source_target_pairs={{0,4},{4,0},{1,5},{5,1},{2,6},{6,2},{3,7},{7,3},{8,12},{12,8},{9,1... | collective-permute-start | bytes 3932168 | tf_op jit(solution)/shard_map/ppermute | solution.py:223
  18.1 3.0 %collective-permute-done = f32[2560,128]{1,0:T(8,128)} collective-permute-done((f32[2560,128]{1,0:T(8,128)}, f32[2560,128]{1,0:T(8,128)}, u32[]{:S(2)}, u32[]{:S(2)}) %collective-permute-start) | collective-permute-done | bytes 1310752 | tf_op jit(solution)/shard_map/ppermute | solution.py:223
  21.1 1.4 bitcast_add_fusion
  22.6 0.0 copy-start.3
  22.6 1.0 copy-done.3
  23.6 0.1 dynamic-slice_bitcast_fusion.3
  23.7 0.1 collective-permute-start.1
  23.8 2.7 %collective-permute-start.3 = (f32[640,128]{1,0:T(8,128)S(1)}, f32[640,128]{1,0:T(8,128)S(1)}, u32[]{:S(2)}, u32[]{:S(2)}) collective-permute-start(f32[640,128]{1,0:T(8,128)S(1)} %get-tuple-element.12), channel_id=1, source_target_pairs={{0,3},{1,0},{2,1},{3,2},{4,7},{5,4},{6,5},{7,6},{8,11},{9,8},{10,9... | collective-permute-start | bytes 983048 | tf_op jit(solution)/shard_map/ppermute | solution.py:245
  26.5 0.0 collective-permute-start.2
  26.5 8.2 %collective-permute-done.1 = f32[640,128]{1,0:T(8,128)S(1)} collective-permute-done((f32[640,128]{1,0:T(8,128)S(1)}, f32[640,128]{1,0:T(8,128)S(1)}, u32[]{:S(2)}, u32[]{:S(2)}) %collective-permute-start.1) | collective-permute-done | bytes 327712 | tf_op jit(solution)/shard_map/ppermute | solution.py:245
  34.6 0.0 collective-permute-done.3
  34.6 6.3 %collective-permute-done.2 = f32[640,128]{1,0:T(8,128)S(1)} collective-permute-done((f32[640,128]{1,0:T(8,128)S(1)}, f32[640,128]{1,0:T(8,128)S(1)}, u32[]{:S(2)}, u32[]{:S(2)}) %collective-permute-start.2) | collective-permute-done | bytes 327712 | tf_op jit(solution)/shard_map/ppermute | solution.py:245
  40.9 1.0 fusion.1
  42.0 1.3 collective-permute-start.4
  43.3 1.4 collective-permute-start.6
  44.7 1.6 collective-permute-start.5
  46.3 0.3 collective-permute-done.4
  46.6 0.0 collective-permute-done.6
  46.6 3.5 %collective-permute-done.5 = f32[160,128]{1,0:T(8,128)S(1)} collective-permute-done((f32[160,128]{1,0:T(8,128)S(1)}, f32[160,128]{1,0:T(8,128)S(1)}, u32[]{:S(2)}, u32[]{:S(2)}) %collective-permute-start.5) | collective-permute-done | bytes 81952 | tf_op jit(solution)/shard_map/ppermute | solution.py:245
  50.2 15.7 %all_to_all.10 = f32[8,20,128]{2,1,0:T(8,128)S(1)} all-to-all(f32[8,20,128]{2,1,0:T(8,128)S(1)} %reshape.26), channel_id=1, replica_groups=mesh['z'=8,'x'=4,'core'=2,'y'=4] {'z'}, dimensions={0} | all-to-all | bytes 163840 | tf_op jit(solution)/shard_map/all_to_all | solution.py:261
  65.9 0.6 broadcast_in_dim.49
  66.6 3.4 %all-to-all-start.1 = ((f32[8,20,128]{2,1,0:T(8,128)}), f32[8,20,128]{2,1,0:T(8,128)S(1)}, u32[]{:S(2)}, u32[]{:S(2)}) async-start(f32[8,20,128]{2,1,0:T(8,128)} %broadcast_in_dim.49), calls=%async_computation.1 | async-start | bytes 196608 | tf_op jit(solution)/shard_map/all_to_all | solution.py:266
  69.9 8.4 %all-to-all-done.1 = f32[8,20,128]{2,1,0:T(8,128)S(1)} async-done(((f32[8,20,128]{2,1,0:T(8,128)}), f32[8,20,128]{2,1,0:T(8,128)S(1)}, u32[]{:S(2)}, u32[]{:S(2)}) %all-to-all-start.1) | async-done | bytes 81952 | tf_op jit(solution)/shard_map/all_to_all | solution.py:266
  78.4 0.8 collective-permute-start.9
  79.1 0.8 collective-permute-start.8
  79.9 0.6 collective-permute-start.7
  80.6 4.7 %collective-permute-done.7 = f32[160,128]{1,0:T(8,128)S(1)} collective-permute-done((f32[160,128]{1,0:T(8,128)S(1)}, f32[160,128]{1,0:T(8,128)S(1)}, u32[]{:S(2)}, u32[]{:S(2)}) %collective-permute-start.7) | collective-permute-done | bytes 81952 | tf_op jit(solution)/shard_map/ppermute | solution.py:255
  85.2 0.0 collective-permute-done.8
  85.3 0.0 collective-permute-done.9
  85.3 1.1 collective-permute-start.10
  86.4 1.8 collective-permute-start.12
  88.2 0.1 collective-permute-start.11
  88.3 0.1 broadcast_in_dim.47
  88.4 0.0 copy-start.4
  88.4 8.3 %collective-permute-done.10 = f32[640,128]{1,0:T(8,128)S(1)} collective-permute-done((f32[640,128]{1,0:T(8,128)S(1)}, f32[640,128]{1,0:T(8,128)S(1)}, u32[]{:S(2)}, u32[]{:S(2)}) %collective-permute-start.10) | collective-permute-done | bytes 327712 | tf_op jit(solution)/shard_map/ppermute | solution.py:255
  96.7 0.0 collective-permute-done.11
  96.8 0.0 collective-permute-done.12
  96.8 7.3 %collective-permute-start.13 = (f32[2560,128]{1,0:T(8,128)S(1)}, f32[2560,128]{1,0:T(8,128)S(1)}, u32[]{:S(2)}, u32[]{:S(2)}) collective-permute-start(f32[2560,128]{1,0:T(8,128)S(1)} %bitcast.66), channel_id=1, source_target_pairs={{0,4},{4,0},{1,5},{5,1},{2,6},{6,2},{3,7},{7,3},{8,12},{12,8},{9,1... | collective-permute-start | bytes 3932168 | tf_op jit(solution)/shard_map/ppermute | solution.py:223
  104.1 0.0 copy-done.4
  104.1 0.6 fusion.4
  106.7 1.3 compare_select_fusion.pick_ref
  108.0 0.0 collective-permute-done.13
  108.0 0.2 select_bitcast_fusion.1
  108.2 0.2 pad_maximum_fusion
  108.3 43.5 %shard_map.47 = (f32[10,256,256]{2,1,0:T(8,128)S(1)}, f32[4,256,256]{2,1,0:T(8,128)S(1)}) custom-call(f32[20,256,128]{2,1,0:T(8,128)S(1)} %bitcast.62), custom_call_target="tpu_custom_call" | custom-call | tf_op jit(solution)/shard_map/pallas_call | solution.py:111
  151.9 0.0 copy-start.1
  151.9 1.5 copy-done.1
  153.4 0.0 copy-start.2
  153.4 1.0 copy-done.2
  154.3 0.0 all-gather.3.cloned.1.call-done
  154.3 27.0 %shard_map.48 = f32[1024,2048]{1,0:T(8,128)} custom-call(s32[64]{0:T(128)} %compare_select_fusion.pick_ref, f32[1024,1024]{1,0:T(8,128)} %t_ref.3, f32[10,256,256]{2,1,0:T(8,128)} %copy-done.1, f32[4,256,256]{2,1,0:T(8,128)} %copy-done.2, f32[64,4,2,8,1024]{4,3,2,1,0:T(8,128)} %bitcast.63), custom_call_target="tpu_custom_call" | custom-call | tf_op jit(solution)/shard_map/pallas_call | solution.py:177
  (15 shorter events, 0.3 us)
Async XLA Ops:
  6.5 147.8 %all-gather.3.cloned.1.call-start = ((), (), s32[]{:S(2)}) async-start(), calls=%async_computation.2 | async-start | bytes 16842752 | tf_op jit(solution)/shard_map/all_gather | solution.py:287
  7.3 2.2 %copy-start = (f32[1024,1024]{1,0:T(8,128)S(1)}, f32[1024,1024]{1,0:T(8,128)}, u32[]{:S(2)}) copy-start(f32[1024,1024]{1,0:T(8,128)} %t_ref.3) | copy-start | bytes 12582916
  14.9 6.2 %collective-permute-start = (f32[2560,128]{1,0:T(8,128)}, f32[2560,128]{1,0:T(8,128)}, u32[]{:S(2)}, u32[]{:S(2)}) collective-permute-start(f32[2560,128]{1,0:T(8,128)} %dynamic-slice_bitcast_fusion), channel_id=1, source_target_pairs={{0,4},{4,0},{1,5},{5,1},{2,6},{6,2},{3,7},{7,3},{8,12},{12,8},{9,1... | collective-permute-start | bytes 3932168 | tf_op jit(solution)/shard_map/ppermute | solution.py:223
  22.6 1.1 copy-start.3
  23.7 10.9 %collective-permute-start.1 = (f32[640,128]{1,0:T(8,128)S(1)}, f32[640,128]{1,0:T(8,128)S(1)}, u32[]{:S(2)}, u32[]{:S(2)}) collective-permute-start(f32[640,128]{1,0:T(8,128)S(1)} %get-tuple-element.11), channel_id=1, source_target_pairs={{0,1},{1,2},{2,3},{3,0},{4,5},{5,6},{6,7},{7,4},{8,9},{9,10},{10,1... | collective-permute-start | bytes 983048 | tf_op jit(solution)/shard_map/ppermute | solution.py:245
  23.8 10.8 %collective-permute-start.3 = (f32[640,128]{1,0:T(8,128)S(1)}, f32[640,128]{1,0:T(8,128)S(1)}, u32[]{:S(2)}, u32[]{:S(2)}) collective-permute-start(f32[640,128]{1,0:T(8,128)S(1)} %get-tuple-element.12), channel_id=1, source_target_pairs={{0,3},{1,0},{2,1},{3,2},{4,7},{5,4},{6,5},{7,6},{8,11},{9,8},{10,9... | collective-permute-start | bytes 983048 | tf_op jit(solution)/shard_map/ppermute | solution.py:245
  26.5 14.5 %collective-permute-start.2 = (f32[640,128]{1,0:T(8,128)S(1)}, f32[640,128]{1,0:T(8,128)S(1)}, u32[]{:S(2)}, u32[]{:S(2)}) collective-permute-start(f32[640,128]{1,0:T(8,128)S(1)} %get-tuple-element.13), channel_id=1, source_target_pairs={{0,2},{1,3},{2,0},{3,1},{4,6},{5,7},{6,4},{7,5},{8,10},{9,11},{10,... | collective-permute-start | bytes 983048 | tf_op jit(solution)/shard_map/ppermute | solution.py:245
  42.0 4.6 %collective-permute-start.4 = (f32[160,128]{1,0:T(8,128)S(1)}, f32[160,128]{1,0:T(8,128)S(1)}, u32[]{:S(2)}, u32[]{:S(2)}) collective-permute-start(f32[160,128]{1,0:T(8,128)S(1)} %get-tuple-element.14), channel_id=1, source_target_pairs={{0,8},{8,16},{16,24},{24,0},{1,9},{9,17},{17,25},{25,1},{2,10},{10... | collective-permute-start | bytes 245768 | tf_op jit(solution)/shard_map/ppermute | solution.py:245
  43.3 3.3 %collective-permute-start.6 = (f32[160,128]{1,0:T(8,128)S(1)}, f32[160,128]{1,0:T(8,128)S(1)}, u32[]{:S(2)}, u32[]{:S(2)}) collective-permute-start(f32[160,128]{1,0:T(8,128)S(1)} %get-tuple-element.15), channel_id=1, source_target_pairs={{0,24},{8,0},{16,8},{24,16},{1,25},{9,1},{17,9},{25,17},{2,26},{10... | collective-permute-start | bytes 245768 | tf_op jit(solution)/shard_map/ppermute | solution.py:245
  44.7 5.4 %collective-permute-start.5 = (f32[160,128]{1,0:T(8,128)S(1)}, f32[160,128]{1,0:T(8,128)S(1)}, u32[]{:S(2)}, u32[]{:S(2)}) collective-permute-start(f32[160,128]{1,0:T(8,128)S(1)} %get-tuple-element.16), channel_id=1, source_target_pairs={{0,16},{8,24},{16,0},{24,8},{1,17},{9,25},{17,1},{25,9},{2,18},{10... | collective-permute-start | bytes 245768 | tf_op jit(solution)/shard_map/ppermute | solution.py:245
  66.6 11.8 %all-to-all-start.1 = ((f32[8,20,128]{2,1,0:T(8,128)}), f32[8,20,128]{2,1,0:T(8,128)S(1)}, u32[]{:S(2)}, u32[]{:S(2)}) async-start(f32[8,20,128]{2,1,0:T(8,128)} %broadcast_in_dim.49), calls=%async_computation.1 | async-start | bytes 196608 | tf_op jit(solution)/shard_map/all_to_all | solution.py:266
  78.4 6.9 %collective-permute-start.9 = (f32[160,128]{1,0:T(8,128)S(1)}, f32[160,128]{1,0:T(8,128)S(1)}, u32[]{:S(2)}, u32[]{:S(2)}) collective-permute-start(f32[160,128]{1,0:T(8,128)S(1)} %reshape.27), channel_id=1, source_target_pairs={{0,24},{8,0},{16,8},{24,16},{1,25},{9,1},{17,9},{25,17},{2,26},{10... | collective-permute-start | bytes 245768 | tf_op jit(solution)/shard_map/ppermute | solution.py:255
  79.1 6.1 %collective-permute-start.8 = (f32[160,128]{1,0:T(8,128)S(1)}, f32[160,128]{1,0:T(8,128)S(1)}, u32[]{:S(2)}, u32[]{:S(2)}) collective-permute-start(f32[160,128]{1,0:T(8,128)S(1)} %reshape.27), channel_id=1, source_target_pairs={{0,16},{8,24},{16,0},{24,8},{1,17},{9,25},{17,1},{25,9},{2,18},{10... | collective-permute-start | bytes 245768 | tf_op jit(solution)/shard_map/ppermute | solution.py:255
  79.9 5.3 %collective-permute-start.7 = (f32[160,128]{1,0:T(8,128)S(1)}, f32[160,128]{1,0:T(8,128)S(1)}, u32[]{:S(2)}, u32[]{:S(2)}) collective-permute-start(f32[160,128]{1,0:T(8,128)S(1)} %reshape.27), channel_id=1, source_target_pairs={{0,8},{8,16},{16,24},{24,0},{1,9},{9,17},{17,25},{25,1},{2,10},{10... | collective-permute-start | bytes 245768 | tf_op jit(solution)/shard_map/ppermute | solution.py:255
  85.3 11.4 %collective-permute-start.10 = (f32[640,128]{1,0:T(8,128)S(1)}, f32[640,128]{1,0:T(8,128)S(1)}, u32[]{:S(2)}, u32[]{:S(2)}) collective-permute-start(f32[640,128]{1,0:T(8,128)S(1)} %bitcast.67), channel_id=1, source_target_pairs={{0,1},{1,2},{2,3},{3,0},{4,5},{5,6},{6,7},{7,4},{8,9},{9,10},{10,1... | collective-permute-start | bytes 983048 | tf_op jit(solution)/shard_map/ppermute | solution.py:255
  86.4 10.4 %collective-permute-start.12 = (f32[640,128]{1,0:T(8,128)S(1)}, f32[640,128]{1,0:T(8,128)S(1)}, u32[]{:S(2)}, u32[]{:S(2)}) collective-permute-start(f32[640,128]{1,0:T(8,128)S(1)} %bitcast.68), channel_id=1, source_target_pairs={{0,3},{1,0},{2,1},{3,2},{4,7},{5,4},{6,5},{7,6},{8,11},{9,8},{10,9... | collective-permute-start | bytes 983048 | tf_op jit(solution)/shard_map/ppermute | solution.py:255
  88.2 8.5 %collective-permute-start.11 = (f32[640,128]{1,0:T(8,128)S(1)}, f32[640,128]{1,0:T(8,128)S(1)}, u32[]{:S(2)}, u32[]{:S(2)}) collective-permute-start(f32[640,128]{1,0:T(8,128)S(1)} %bitcast.69), channel_id=1, source_target_pairs={{0,2},{1,3},{2,0},{3,1},{4,6},{5,7},{6,4},{7,5},{8,10},{9,11},{10,... | collective-permute-start | bytes 983048 | tf_op jit(solution)/shard_map/ppermute | solution.py:255
  88.4 15.7 %copy-start.4 = (s32[64]{0:T(128)S(1)}, s32[64]{0:T(128)}, u32[]{:S(2)}) copy-start(s32[64]{0:T(128)} %param.7) | copy-start | bytes 772
  96.8 11.1 %collective-permute-start.13 = (f32[2560,128]{1,0:T(8,128)S(1)}, f32[2560,128]{1,0:T(8,128)S(1)}, u32[]{:S(2)}, u32[]{:S(2)}) collective-permute-start(f32[2560,128]{1,0:T(8,128)S(1)} %bitcast.66), channel_id=1, source_target_pairs={{0,4},{4,0},{1,5},{5,1},{2,6},{6,2},{3,7},{7,3},{8,12},{12,8},{9,1... | collective-permute-start | bytes 3932168 | tf_op jit(solution)/shard_map/ppermute | solution.py:223
  151.9 1.5 copy-start.1
  153.4 1.0 copy-start.2
Sparse Core Ops, SparseCore 0:
  11.0 129.3 all-gather.2

commit v2 on v0

v2 whole, which is shorter than its diff:
```python
import functools
import jax
import jax.numpy as jnp
from jax import lax
from jax.experimental import pallas as pl
from jax.experimental.pallas import tpu as pltpu
from jax.sharding import Mesh, PartitionSpec as P

HIGHEST = lax.Precision.HIGHEST
damping = 0.1
NN = ((1,), (0,))
NT = ((1,), (1,))
TN = ((0,), (0,))
MIB = 1024 * 1024


def dot(a, b, dims):
    return lax.dot_general(a, b, (dims, ((), ())), precision=HIGHEST, preferred_element_type=jnp.float32)


def split(x):
    high = x.astype(jnp.bfloat16)
    return high, (x - high.astype(jnp.float32)).astype(jnp.bfloat16)


def dot3(a, b, dims):
    d = lambda u, v: lax.dot_general(u, v, (dims, ((), ())), preferred_element_type=jnp.float32)
    return d(a[0], b[1]) + d(a[1], b[0]) + d(a[0], b[0])


def thirds(x):
    high = x.astype(jnp.bfloat16).astype(jnp.float32)
    rest = x - high
    middle = rest.astype(jnp.bfloat16).astype(jnp.float32)
    return high, middle, rest - middle


def inverse_128(matrix):
    width = 2
    pivots = 8 * width
    rows = [matrix[8 * r:8 * r + 8, :] for r in range(16)]
    lane = lax.broadcasted_iota(jnp.int32, (8, 128), 1)
    sub = lax.broadcasted_iota(jnp.int32, (8, 128), 0)
    spread = lambda x, l: jnp.broadcast_to(x[:, l:l + 1], (8, 128))
    row_of = lambda v, i: jnp.broadcast_to(v[i // 8][i % 8:i % 8 + 1, :], (8, 128))
    stack = lambda v: jnp.concatenate(v, axis=0)
    for lo in range(0, 128, pivots):
        first_row = lo // 8
        in_block = (lane >= lo) & (lane < lo + pivots)
        held = rows[first_row:first_row + width]
        cols = [[spread(h, lo + i) for h in held] for i in range(pivots)]
        z = [jnp.where(in_block, (lane - lo == sub + 8 * t).astype(jnp.float32), held[t]) for t in range(width)]
        for i in range(0, pivots, 2):
            one, two = cols[i], cols[i + 1]
            a, b, c = row_of(one, i), row_of(two, i), row_of(two, i + 1)
            r = pl.reciprocal(a * c - b * b)
            at = i // 8
            at_i, at_j = sub == i % 8, sub == i % 8 + 1
            both = at_i | at_j
            m0, m1 = list(one), list(two)
            m0[at] = jnp.where(at_i, -1.0, jnp.where(at_j, 0.0, one[at]))
            m1[at] = jnp.where(at_j, -1.0, jnp.where(at_i, 0.0, two[at]))
            e0 = [x * c - y * b for x, y in zip(m0, m1)]
            e1 = [y * a - x * b for x, y in zip(m0, m1)]

            def step(v):
                ri, rj = row_of(v, i) * r, row_of(v, i + 1) * r
                kept = [jnp.where(both, 0.0, v[t]) if t == at else v[t] for t in range(width)]
                return [kept[t] - (e0[t] * ri + e1[t] * rj) for t in range(width)]

            z = step(z)
            for j in range(i + 2, pivots):
                cols[j] = step(cols[j])
        z = [jnp.where(in_block, -v, v) for v in z]
        z_rows = [row_of(z, i) for i in range(pivots)]
        order = [(first_row + width + r) % 16 for r in range(16 - width)]
        for r in order[:width]:
            terms = [spread(rows[r], lo + i) * z_rows[i] for i in range(pivots)]
            while len(terms) > 1:
                terms = [terms[2 * t] + terms[2 * t + 1] for t in range(len(terms) // 2)]
            rows[r] = jnp.where(in_block, 0.0, rows[r]) - terms[0]
        h, m, l = thirds(stack(held))
        zh, zm, zl = thirds(stack(z))
        left = stack([h, h, m, m, h, l]).astype(jnp.bfloat16)
        right = stack([zh, zm, zh, zm, zl, zh]).astype(jnp.bfloat16)
        change = lax.dot_general(left, right, (TN, ((), ())), preferred_element_type=jnp.float32)
        for r in order[width:]:
            rows[r] = jnp.where(in_block, 0.0, rows[r]) - change[8 * r:8 * r + 8]
        rows[first_row:first_row + width] = z
    return -stack(rows)


def small_blocks(n):
    out, place = [], 0
    for j in range(n):
        for i in range(j, n):
            out += [(place, 0, 0), (place, 128, 0)] + ([(place, 0, 128)] if i > j else []) + [(place, 128, 128)]
            place += 1
    return out


def gram_kernel(n, core_ref, t_ref, mine_ref, other_ref, th_ref, tl_ref):
    core = core_ref[0]
    for j in range(n):
        at = slice(256 * j, 256 * j + 256)
        high, low = split(t_ref[:, at])
        th_ref[at, :] = high.T
        tl_ref[at, :] = low.T
    list_of = small_blocks(n)
    half = len(list_of) // 2
    place = 0
    for j in range(n):
        right = split(t_ref[:, 256 * j:256 * j + 256])
        for i in range(j, n):
            of = slice(256 * i, 256 * i + 256)
            block = dot3((th_ref[of, :], tl_ref[of, :]), right, NN)
            for k, (p, row, column) in enumerate(list_of):
                if p == place:
                    part = block[row:row + 128, column:column + 128]
                    at = k % half

                    @pl.when(core == k // half)
                    def _():
                        mine_ref[at] = part

                    @pl.when(core != k // half)
                    def _():
                        other_ref[at] = part
            place += 1


def gram(core, t, n):
    m, features = t.shape
    half = len(small_blocks(n)) // 2
    whole = pl.BlockSpec(memory_space=pltpu.VMEM)
    return pl.pallas_call(
        functools.partial(gram_kernel, n),
        out_shape=(jax.ShapeDtypeStruct((half, 128, 128), jnp.float32),) * 2,
        in_specs=[pl.BlockSpec(memory_space=pltpu.SMEM), whole],
        out_specs=(whole,) * 2,
        scratch_shapes=[pltpu.VMEM((features, m), jnp.bfloat16)] * 2,
        compiler_params=pltpu.CompilerParams(vmem_limit_bytes=28 * MIB),
    )(core, t)


def factor_kernel(n, scale, core_ref, mine_ref, other_ref, l_ref, d_ref, a_ref):
    core = core_ref[0]
    list_of = small_blocks(n)
    half = len(list_of) // 2
    eye = lax.broadcasted_iota(jnp.int32, (128, 128), 0) == lax.broadcasted_iota(jnp.int32, (128, 128), 1)
    damp = damping * eye.astype(jnp.float32)
    diagonal = [j * n - j * (j - 1) // 2 for j in range(n)]
    for k, (p, row, column) in enumerate(list_of):
        block = jnp.where(core == k // half, mine_ref[k % half], other_ref[k % half]) * scale
        a_ref[p, row:row + 128, column:column + 128] = block + damp if p in diagonal and row == column else block

    def column_step(j, _):
        p = j * n - (j * (j - 1)) // 2
        d = a_ref.at[p]
        d21 = d[128:256, 0:128]
        i11 = inverse_128(d[0:128, 0:128])
        x = dot(d21, i11, NN)
        i22 = inverse_128(d[128:256, 128:256] - dot(x, d21, NT))
        u = dot(i22, x, NN)
        d_ref[j, 0:128, 0:128] = i11 + dot(x, u, TN)
        d_ref[j, 128:256, 0:128] = -u
        d_ref[j, 0:128, 128:256] = -u.T
        d_ref[j, 128:256, 128:256] = i22

        def row_step(i, _):
            panel = dot(a_ref[p + i - j], d_ref[j], NN)
            l_ref[p + i - j] = panel

            def block_step(c, _):
                q = c * n - (c * (c - 1)) // 2 + i - c
                a_ref[q] = a_ref[q] - dot(panel, a_ref[p + c - j], NT)
                return 0

            lax.fori_loop(j + 1, i + 1, block_step, 0)
            return 0

        lax.fori_loop(j + 1, n, row_step, 0)
        return 0

    lax.fori_loop(0, n, column_step, 0)


def factor(core, mine, other, n, scale):
    blocks = n * (n + 1) // 2
    whole = pl.BlockSpec(memory_space=pltpu.VMEM)
    return pl.pallas_call(
        functools.partial(factor_kernel, n, scale),
        out_shape=(
            jax.ShapeDtypeStruct((blocks, 256, 256), jnp.float32),
            jax.ShapeDtypeStruct((n, 256, 256), jnp.float32),
        ),
        in_specs=[pl.BlockSpec(memory_space=pltpu.SMEM), whole, whole],
        out_specs=(whole,) * 2,
        scratch_shapes=[pltpu.VMEM((blocks, 256, 256), jnp.float32)],
        compiler_params=pltpu.CompilerParams(vmem_limit_bytes=20 * MIB),
    )(core, mine, other)


def solve_kernel(n, scale, t_ref, l_ref, d_ref, wh_ref, wl_ref):
    place = lambda i, j: j * n - j * (j - 1) // 2 + (i - j)
    at = lambda j: slice(256 * j, 256 * j + 256)
    ys = []
    for j in range(n):
        acc = t_ref[:, at(j)]
        for i in range(j):
            acc = acc - dot3(ys[i], split(l_ref[place(j, i)]), NT)
        ys.append(split(acc))
    ws = [None] * n
    for j in reversed(range(n)):
        acc = dot3(ys[j], split(d_ref[j]), NN)
        for i in range(j + 1, n):
            acc = acc - dot3(ws[i], split(l_ref[place(i, j)]), NN)
        ws[j] = split(acc)
        wh_ref[:, at(j)] = ws[j][0] * jnp.bfloat16(scale)
        wl_ref[:, at(j)] = ws[j][1] * jnp.bfloat16(scale)


def solve(t, l, d, n):
    m, features = t.shape
    whole = pl.BlockSpec(memory_space=pltpu.VMEM)
    return pl.pallas_call(
        functools.partial(solve_kernel, n, features ** -0.5),
        out_shape=(jax.ShapeDtypeStruct((m, features), jnp.bfloat16),) * 2,
        in_specs=[whole] * 3,
        out_specs=(whole,) * 2,
        compiler_params=pltpu.CompilerParams(vmem_limit_bytes=36 * MIB),
    )(t, l, d)


def score_kernel(pick_ref, wh_ref, wl_ref, v_ref, out_ref):
    step = pl.program_id(0)
    slots = v_ref.shape[0]
    rows = []
    for s in range(slots):
        pick = pick_ref[step * slots + s]
        first = (pick == 0).astype(jnp.float32)
        second = (pick == 1).astype(jnp.float32)
        for y in range(v_ref.shape[1]):
            rows.append(v_ref[s, y, 0] * first + v_ref[s, y, 1] * second)
    v = split(jnp.concatenate(rows, axis=0))
    out_ref[...] = dot3((wh_ref[...], wl_ref[...]), v, NT)


def score(pick, wh, wl, v, slots):
    m, features = wh.shape
    total, groups, blocks, part, _ = v.shape
    width = slots * groups * part
    whole = pl.BlockSpec(memory_space=pltpu.VMEM)
    return pl.pallas_call(
        score_kernel,
        grid=(total // slots,),
        out_shape=jax.ShapeDtypeStruct((m, total * groups * part), jnp.float32),
        in_specs=[
            pl.BlockSpec(memory_space=pltpu.SMEM),
            whole, whole,
            pl.BlockSpec((slots, groups, blocks, part, features), lambda i: (i, 0, 0, 0, 0)),
        ],
        out_specs=pl.BlockSpec((m, width), lambda i: (0, i)),
        compiler_params=pltpu.CompilerParams(vmem_limit_bytes=32 * MIB),
    )(pick, wh, wl, v)


def swap(v):
    return lax.ppermute(v, "core", [(0, 1), (1, 0)])


def ring(v, axis, k):
    size = lax.axis_size(axis)
    return lax.ppermute(v, axis, [(i, (i + k) % size) for i in range(size)])


def scatter(v, axis, dim):
    size, me = lax.axis_size(axis), lax.axis_index(axis)
    part = lambda k: lax.dynamic_index_in_dim(v, lax.rem(me + k, size), dim, keepdims=False)
    came = [ring(part(k), axis, k) for k in range(1, size)]
    return part(0), came


def gather(v, axis):
    size, me = lax.axis_size(axis), lax.axis_index(axis)
    came = [ring(v, axis, k) for k in range(1, size)]
    out = lax.dynamic_update_index_in_dim(jnp.zeros((size,) + v.shape, v.dtype), v, me, 0)
    for k in range(1, size):
        out = lax.dynamic_update_index_in_dim(out, came[k - 1], lax.rem(me + size - k, size), 0)
    return out


def add(parts):
    total = parts[0]
    for c in parts[1]:
        total = total + c
    return total


def sum_all(mine, other, beside):
    shape = mine.shape
    ny, nx, nz = lax.axis_size("y"), lax.axis_size("x"), lax.axis_size("z")
    v = (mine + swap(other)).reshape(ny, nx, 2, -1, 128)
    by_y, by_x = scatter(v[:, :, 0], "y", 0), scatter(v[:, :, 1], "x", 1)
    left, right = add(by_y), add(by_x)
    left, beside = lax.optimization_barrier((left, beside))
    by_x, by_y = scatter(left, "x", 0), scatter(right, "y", 0)
    s = jnp.stack([add(by_x), add(by_y)])
    hop = 1
    while hop < nz:
        s = s + lax.ppermute(s, "z", [(i, i ^ hop) for i in range(nz)])
        hop *= 2
    return gather(gather(s, "x"), "y").reshape(shape), beside


def local(train_grads, val_grads, wanted, owner):
    m, features = train_grads.shape
    n = features // 256
    dp = ("z", "x", "core")
    slabs, group = lax.axis_size(dp), lax.axis_size("y")
    blocks, part, _ = val_grads.shape
    val_all = lax.all_gather(val_grads, dp + ("y",), tiled=False)
    val_all = val_all.reshape(slabs, group, blocks, part, features)

    positions = jnp.arange(slabs, dtype=jnp.int32)
    holder = jnp.sum(jnp.where(owner == lax.axis_index(dp), positions, 0))
    request = lax.dynamic_index_in_dim(wanted, holder, 0, keepdims=False)
    pick = jnp.where(request >= 0, request - positions * blocks, -1)

    core = lax.axis_index("core").reshape(1)
    mine, other = gram(core, train_grads, n)
    mine, pick = sum_all(mine, other, pick)
    l, d = factor(core, mine, swap(mine), n, 1.0 / (m * slabs * group))
    wh, wl = solve(train_grads, l, d, n)
    return score(pick, wh, wl, val_all, 8)


def solution(mesh):
    axes = ("z", "x", "core", "y")
    fine = Mesh(mesh.devices.reshape(8, 4, 2, 4), axes)
    dp = P(("z", "x", "core"), "y", None)
    in_specs = (P(axes, None), dp, P(), P())
    return jax.shard_map(local, mesh=fine, in_specs=in_specs, out_specs=P(axes, None), check_vma=False)
```

time: 856 us -> 172 us (0.20)
  waiting for transfers between devices: 351 us -> 30.4 us
  other arithmetic: 261 us -> 1.67 us
  matrix products: 102 us -> 0 us
  Pallas kernels: 0 us -> 66.3 us
  blocking collectives: 60.5 us -> 0 us
  starting transfers between devices: 0.04 us -> 46.2 us
  local copies, waits for them, and re-layouts: 53.5 us -> 11.3 us
    psum x1 -> x0, waiting for transfers between devices: 269 us -> none  [local(): summed = lax.psum(partial_gram, ('dp', 'group'))]
    another operation x33 -> x3, other arithmetic: 251 us -> 0.03 us  [sum_all(): s = jnp.stack([add(by_x), add(by_y)])]
    all_gather x1, waiting for transfers between devices: 82.3 us -> 4.63 us  [local(): val_all = lax.all_gather(val_grads, dp + ('y',), tiled=False)]
    pallas_call x0 -> x4, Pallas kernels: none -> 66.3 us  [the longest x1 32.5 us: factor(): pl.pallas_call(functools.partial(factor_kernel, n, scale), out_shape=(jax...]
    all_to_all x1 -> x0, blocking collectives: 60.5 us -> none  [local(): lax.all_to_all(outgoing, 'dp', split_axis=0, concat_axis=0, tiled=True)]
    dot_general x3 -> x0, matrix products: 55 us -> none  [the longest x1 36.2 us: local(): lax.dot_general(train_grads, lax.all_gather(arrived, 'group', axis=1, til...]
    another operation x44 -> x0, matrix products: 46.7 us -> none  [the longest x14 26.1 us: local(): factor = jnp.linalg.cholesky(gram_matrix)]
    ppermute x0 -> x23, starting transfers between devices: none -> 46.2 us  [the longest x18 20.8 us: ring(): return lax.ppermute(v, axis, [(i, (i + k) % size) for i in range(size)])]
  transfers between devices with their start and end apart: 2 -> 24, of which waited for: 2 -> 13; matrix products, arithmetic and copies ran while one was open for 0% -> 1% of each run, Pallas kernels for 0% -> 29%
where the time goes in v2:
time: 172 us
  Pallas kernels  66.3 us (39%)
  starting transfers between devices  46.2 us (27%)
  waiting for transfers between devices  30.4 us (18%)
  between operations  15.7 us (9%)
  local copies, waits for them, and re-layouts  11.3 us (7%)
    pallas_call x1, Pallas kernels, factor(): pl.pallas_call(functools.partial(factor_kernel, n, scale), out_shape=(jax...  32.5 us
    ppermute x18, starting transfers between devices, ring(): return lax.ppermute(v, axis, [(i, (i + k) % size) for i in range(size)])  20.8 us
    ppermute x18, waiting for transfers between devices, ring(): return lax.ppermute(v, axis, [(i, (i + k) % size) for i in range(size)])  16.9 us
    pallas_call x1, Pallas kernels, score(): pl.pallas_call(score_kernel, grid=(total // slots,), out_shape=jax.ShapeD...  16.7 us
    ppermute x2, starting transfers between devices, swap(): return lax.ppermute(v, 'core', [(0, 1), (1, 0)])  13.7 us
    ppermute x3, starting transfers between devices, sum_all(): s = s + lax.ppermute(s, 'z', [(i, i ^ hop) for i in range(nz)])  11.7 us
    unnamed x12, local copies, waits for them, and re-layouts  10.9 us
    pallas_call x1, Pallas kernels, gram(): pl.pallas_call(functools.partial(gram_kernel, n), out_shape=(jax.ShapeDty...  10.3 us
  transfers between devices with their start and end apart: 24, of which 13 were waited for; matrix products, arithmetic and copies ran while one was open for 1% of the time, Pallas kernels for 29%

profile of v2, /device:TPU:1, one launch (start us, length us, event | category | flops | bytes accessed | tf_op | source)
XLA Modules:
  0.0 171.6 jit_solution(1501708049991638760)
XLA Ops:
  6.5 0.7 all-gather.3.cloned.1.call-update
  7.3 0.0 copy-start.1
  7.3 2.2 %copy-done.1 = f32[1024,1024]{1,0:T(8,128)S(1)} copy-done((f32[1024,1024]{1,0:T(8,128)S(1)}, f32[1024,1024]{1,0:T(8,128)}, u32[]{:S(2)}) %copy-start.1) | copy-done | bytes 4194328
  9.5 10.3 %shard_map.46 = (f32[18,128,128]{2,1,0:T(8,128)S(1)}, f32[18,128,128]{2,1,0:T(8,128)S(1)}) custom-call(s32[1]{0:T(128)} %bitcast.core_ref, f32[1024,1024]{1,0:T(8,128)S(1)} %copy-done.1), custom_call_target="tpu_custom_call" | custom-call | tf_op jit(solution)/shard_map/pallas_call | solution.py:136
  19.8 3.3 %collective-permute-start = (f32[18,128,128]{2,1,0:T(8,128)S(1)}, f32[18,128,128]{2,1,0:T(8,128)S(1)}, u32[]{:S(2)}, u32[]{:S(2)}) collective-permute-start(f32[18,128,128]{2,1,0:T(8,128)S(1)} %get-tuple-element.14), channel_id=1, source_target_pairs={{0,4},{4,0},{1,5},{5,1},{2,6},{6,2},{3,7},{7,3},{8,12},{12,8},{9,1... | collective-permute-start | bytes 3538952 | tf_op jit(solution)/shard_map/ppermute | solution.py:269
  23.1 0.7 fusion.10
  25.9 0.0 collective-permute-done
  25.9 0.1 add.155
  26.0 0.1 fusion.13
  26.2 0.1 collective-permute-start.7
  26.3 2.7 %collective-permute-start.9 = (f32[4,72,128]{2,1,0:T(8,128)S(1)}, f32[4,72,128]{2,1,0:T(8,128)S(1)}, u32[]{:S(2)}, u32[]{:S(2)}) collective-permute-start(f32[4,72,128]{2,1,0:T(8,128)S(1)} %get-tuple-element.26), channel_id=1, source_target_pairs={{0,24},{8,0},{16,8},{24,16},{1,25},{9,1},{17,9},{25,17},{2,26},{10... | collective-permute-start | bytes 442376 | tf_op jit(solution)/shard_map/ppermute | solution.py:274
  28.9 0.0 collective-permute-start.8
  28.9 0.7 compare_select_fusion.pick_ref
  29.6 1.2 collective-permute-start.1
  30.8 1.6 collective-permute-start.3
  32.4 0.8 collective-permute-done.7
  33.2 0.9 collective-permute-start.2
  34.0 1.0 collective-permute-done.9
  35.1 0.2 collective-permute-done.8
  35.4 1.8 %collective-permute-start.10 = (f32[72,128]{1,0:T(8,128)S(1)}, f32[72,128]{1,0:T(8,128)S(1)}, u32[]{:S(2)}, u32[]{:S(2)}) collective-permute-start(f32[72,128]{1,0:T(8,128)S(1)} %get-tuple-element.34), channel_id=1, source_target_pairs={{0,1},{1,2},{2,3},{3,0},{4,5},{5,6},{6,7},{7,4},{8,9},{9,10},{10,1... | collective-permute-start | bytes 110600 | tf_op jit(solution)/shard_map/ppermute | solution.py:274
  37.2 1.5 collective-permute-start.12
  38.7 0.0 collective-permute-done.1
  38.7 1.6 collective-permute-start.11
  40.3 0.0 collective-permute-done.3
  40.3 0.0 collective-permute-done.2
  40.4 0.6 collective-permute-start.4
  41.0 2.1 %collective-permute-start.6 = (f32[72,128]{1,0:T(8,128)S(1)}, f32[72,128]{1,0:T(8,128)S(1)}, u32[]{:S(2)}, u32[]{:S(2)}) collective-permute-start(f32[72,128]{1,0:T(8,128)S(1)} %get-tuple-element.32), channel_id=1, source_target_pairs={{0,24},{8,0},{16,8},{24,16},{1,25},{9,1},{17,9},{25,17},{2,26},{10... | collective-permute-start | bytes 110600 | tf_op jit(solution)/shard_map/ppermute | solution.py:274
  43.1 0.0 collective-permute-done.10
  43.1 0.7 collective-permute-start.5
  43.8 0.0 collective-permute-done.12
  43.8 0.0 collective-permute-done.11
  43.8 0.6 collective-permute-done.4
  44.4 0.0 collective-permute-done.6
  44.5 3.0 %collective-permute-done.5 = f32[72,128]{1,0:T(8,128)S(1)} collective-permute-done((f32[72,128]{1,0:T(8,128)S(1)}, f32[72,128]{1,0:T(8,128)S(1)}, u32[]{:S(2)}, u32[]{:S(2)}) %collective-permute-start.5) | collective-permute-done | bytes 36896 | tf_op jit(solution)/shard_map/ppermute | solution.py:274
  47.5 1.8 %collective-permute-start.13 = (f32[2,72,128]{2,1,0:T(8,128)S(1)}, f32[2,72,128]{2,1,0:T(8,128)S(1)}, u32[]{:S(2)}, u32[]{:S(2)}) collective-permute-start(f32[2,72,128]{2,1,0:T(8,128)S(1)} %pad_maximum_fusion), channel_id=1, source_target_pairs={{0,32},{32,0},{64,96},{96,64},{128,160},{160,128},{192,224},{224,1... | collective-permute-start | bytes 221192 | tf_op jit(solution)/shard_map/ppermute | solution.py:311
  49.3 2.3 %collective-permute-done.13 = f32[2,72,128]{2,1,0:T(8,128)S(1)} collective-permute-done((f32[2,72,128]{2,1,0:T(8,128)S(1)}, f32[2,72,128]{2,1,0:T(8,128)S(1)}, u32[]{:S(2)}, u32[]{:S(2)}) %collective-permute-start.13) | collective-permute-done | bytes 73760 | tf_op jit(solution)/shard_map/ppermute | solution.py:311
  51.5 3.0 %collective-permute-start.14 = (f32[2,72,128]{2,1,0:T(8,128)S(1)}, f32[2,72,128]{2,1,0:T(8,128)S(1)}, u32[]{:S(2)}, u32[]{:S(2)}) collective-permute-start(f32[2,72,128]{2,1,0:T(8,128)S(1)} %fusion.12), channel_id=1, source_target_pairs={{0,64},{32,96},{64,0},{96,32},{128,192},{160,224},{192,128},{224,1... | collective-permute-start | bytes 221192 | tf_op jit(solution)/shard_map/ppermute | solution.py:311
  54.5 1.7 %collective-permute-done.14 = f32[2,72,128]{2,1,0:T(8,128)S(1)} collective-permute-done((f32[2,72,128]{2,1,0:T(8,128)S(1)}, f32[2,72,128]{2,1,0:T(8,128)S(1)}, u32[]{:S(2)}, u32[]{:S(2)}) %collective-permute-start.14) | collective-permute-done | bytes 73760 | tf_op jit(solution)/shard_map/ppermute | solution.py:311
  56.3 6.9 %collective-permute-start.15 = (f32[2,72,128]{2,1,0:T(8,128)S(1)}, f32[2,72,128]{2,1,0:T(8,128)S(1)}, u32[]{:S(2)}, u32[]{:S(2)}) collective-permute-start(f32[2,72,128]{2,1,0:T(8,128)S(1)} %fusion.14), channel_id=1, source_target_pairs={{0,128},{32,160},{64,192},{96,224},{128,0},{160,32},{192,64},{224,... | collective-permute-start | bytes 221192 | tf_op jit(solution)/shard_map/ppermute | solution.py:311
  63.2 1.8 %collective-permute-done.15 = f32[2,72,128]{2,1,0:T(8,128)S(1)} collective-permute-done((f32[2,72,128]{2,1,0:T(8,128)S(1)}, f32[2,72,128]{2,1,0:T(8,128)S(1)}, u32[]{:S(2)}, u32[]{:S(2)}) %collective-permute-start.15) | collective-permute-done | bytes 73760 | tf_op jit(solution)/shard_map/ppermute | solution.py:311
  65.0 0.1 collective-permute-start.16
  65.1 1.3 collective-permute-start.17
  66.4 1.5 collective-permute-start.18
  67.9 3.8 %collective-permute-done.16 = f32[2,72,128]{2,1,0:T(8,128)S(1)} collective-permute-done((f32[2,72,128]{2,1,0:T(8,128)S(1)}, f32[2,72,128]{2,1,0:T(8,128)S(1)}, u32[]{:S(2)}, u32[]{:S(2)}) %collective-permute-start.16) | collective-permute-done | bytes 73760 | tf_op jit(solution)/shard_map/ppermute | solution.py:274
  71.7 0.0 collective-permute-done.17
  71.8 0.0 collective-permute-done.18
  71.8 0.2 collective-permute-start.19
  72.0 2.5 %collective-permute-start.21 = (f32[4,2,72,128]{3,2,1,0:T(8,128)S(1)}, f32[4,2,72,128]{3,2,1,0:T(8,128)S(1)}, u32[]{:S(2)}, u32[]{:S(2)}) collective-permute-start(f32[4,2,72,128]{3,2,1,0:T(8,128)S(1)} %bitcast_dynamic-update-slice_fusion.4), channel_id=1, source_target_pairs={{0,3},{1,0},{2,1},{3,2},{4,7},{5,4},{6,5},{7,6},{8,11},{9,8},{10,9... | collective-permute-start | bytes 884744 | tf_op jit(solution)/shard_map/ppermute | solution.py:274
  74.6 0.4 collective-permute-start.20
  74.9 0.1 broadcast_in_dim.41
  75.0 0.0 copy-start.2
  75.1 4.6 %collective-permute-done.19 = f32[4,2,72,128]{3,2,1,0:T(8,128)S(1)} collective-permute-done((f32[4,2,72,128]{3,2,1,0:T(8,128)S(1)}, f32[4,2,72,128]{3,2,1,0:T(8,128)S(1)}, u32[]{:S(2)}, u32[]{:S(2)}) %collective-permute-start.19) | collective-permute-done | bytes 294944 | tf_op jit(solution)/shard_map/ppermute | solution.py:274
  79.7 2.8 %collective-permute-done.20 = f32[4,2,72,128]{3,2,1,0:T(8,128)S(1)} collective-permute-done((f32[4,2,72,128]{3,2,1,0:T(8,128)S(1)}, f32[4,2,72,128]{3,2,1,0:T(8,128)S(1)}, u32[]{:S(2)}, u32[]{:S(2)}) %collective-permute-start.20) | collective-permute-done | bytes 294944 | tf_op jit(solution)/shard_map/ppermute | solution.py:274
  82.5 0.0 collective-permute-done.21
  82.6 10.4 %collective-permute-start.22 = (f32[18,128,128]{2,1,0:T(8,128)S(1)}, f32[18,128,128]{2,1,0:T(8,128)S(1)}, u32[]{:S(2)}, u32[]{:S(2)}) collective-permute-start(f32[18,128,128]{2,1,0:T(8,128)S(1)} %bitcast.81), channel_id=1, source_target_pairs={{0,4},{4,0},{1,5},{5,1},{2,6},{6,2},{3,7},{7,3},{8,12},{12,8},{9,1... | collective-permute-start | bytes 3538952 | tf_op jit(solution)/shard_map/ppermute | solution.py:269
  92.9 2.5 %collective-permute-done.22.other_ref = f32[18,128,128]{2,1,0:T(8,128)S(1)} collective-permute-done((f32[18,128,128]{2,1,0:T(8,128)S(1)}, f32[18,128,128]{2,1,0:T(8,128)S(1)}, u32[]{:S(2)}, u32[]{:S(2)}) %collective-permute-start.22) | collective-permute-done | bytes 1179680 | tf_op jit(solution)/shard_map/ppermute | solution.py:269
  95.4 32.5 %shard_map.47 = (f32[10,256,256]{2,1,0:T(8,128)S(1)}, f32[4,256,256]{2,1,0:T(8,128)S(1)}) custom-call(s32[1]{0:T(128)} %bitcast.core_ref, f32[18,128,128]{2,1,0:T(8,128)S(1)} %bitcast.82, f32[18,128,128]{2,1,0:T(8,128)S(1)} %collective-permute-done.22.other_ref), custom_call_target="tpu_custom_call" | custom-call | tf_op jit(solution)/shard_map/pallas_call | solution.py:191
  127.9 6.8 %shard_map.48 = (bf16[1024,1024]{1,0:T(8,128)(2,1)S(1)}, bf16[1024,1024]{1,0:T(8,128)(2,1)S(1)}) custom-call(f32[1024,1024]{1,0:T(8,128)S(1)} %copy-done.2, f32[10,256,256]{2,1,0:T(8,128)S(1)} %get-tuple-element.17.l_ref, f32[4,256,256]{2,1,0:T(8,128)S(1)} %get-tuple-element.18.d_ref), custom_call_target="tpu_custom_call" | custom-call | tf_op jit(solution)/shard_map/pallas_call | solution.py:226
  134.7 0.0 copy-start.3
  134.7 1.3 copy-done.3
  136.0 4.6 %all-gather.3.cloned.1.call-done = f32[512,8,1024]{2,1,0:T(8,128)} async-done(((f32[2,8,1024]{2,1,0:T(8,128)}), f32[512,8,1024]{2,1,0:T(8,128)}) %all-gather.3.cloned.1.call-update) | async-done | bytes 16777232 | tf_op jit(solution)/shard_map/all_gather | solution.py:322
  140.6 5.8 %copy-done = f32[512,8,1024]{2,1,0:T(8,128)S(1)} copy-done((f32[512,8,1024]{2,1,0:T(8,128)S(1)}, f32[512,8,1024]{2,1,0:T(8,128)}, u32[]{:S(2)}) %copy-start) | copy-done | bytes 16777240
  146.4 1.6 copy-done.4
  148.0 16.7 %shard_map.49 = f32[1024,2048]{1,0:T(8,128)} custom-call(s32[64]{0:T(128)S(1)} %compare_select_fusion.pick_ref, bf16[1024,1024]{1,0:T(8,128)(2,1)S(1)} %get-tuple-element.19.wh_ref, bf16[1024,1024]{1,0:T(8,128)(2,1)S(1)} %copy-done.4, f32[64,4,2,8,1024]{4,3,2,1,0:T(8,128)S(1)} %bitcast.80), custom_call_target="tpu_custom_call" | custom-call | tf_op jit(solution)/shard_map/pallas_call | solution.py:254
  (26 shorter events, 0.4 us)
Async XLA Ops:
  6.5 134.1 %all-gather.3.cloned.1.call-start = ((), (), s32[]{:S(2)}) async-start(), calls=%async_computation | async-start | bytes 16842752 | tf_op jit(solution)/shard_map/all_gather | solution.py:322
  7.3 2.2 %copy-start.1 = (f32[1024,1024]{1,0:T(8,128)S(1)}, f32[1024,1024]{1,0:T(8,128)}, u32[]{:S(2)}) copy-start(f32[1024,1024]{1,0:T(8,128)} %t_ref.3) | copy-start | bytes 12582916
  9.5 13.7 %copy-start.5 = (s32[64]{0:T(128)S(1)}, s32[64]{0:T(128)}, u32[]{:S(2)}) copy-start(s32[64]{0:T(128)} %param.7) | copy-start | bytes 772
  19.8 6.1 %collective-permute-start = (f32[18,128,128]{2,1,0:T(8,128)S(1)}, f32[18,128,128]{2,1,0:T(8,128)S(1)}, u32[]{:S(2)}, u32[]{:S(2)}) collective-permute-start(f32[18,128,128]{2,1,0:T(8,128)S(1)} %get-tuple-element.14), channel_id=1, source_target_pairs={{0,4},{4,0},{1,5},{5,1},{2,6},{6,2},{3,7},{7,3},{8,12},{12,8},{9,1... | collective-permute-start | bytes 3538952 | tf_op jit(solution)/shard_map/ppermute | solution.py:269
  26.2 7.0 %collective-permute-start.7 = (f32[4,72,128]{2,1,0:T(8,128)S(1)}, f32[4,72,128]{2,1,0:T(8,128)S(1)}, u32[]{:S(2)}, u32[]{:S(2)}) collective-permute-start(f32[4,72,128]{2,1,0:T(8,128)S(1)} %get-tuple-element.25), channel_id=1, source_target_pairs={{0,8},{8,16},{16,24},{24,0},{1,9},{9,17},{17,25},{25,1},{2,10},{10... | collective-permute-start | bytes 442376 | tf_op jit(solution)/shard_map/ppermute | solution.py:274
  26.3 8.8 %collective-permute-start.9 = (f32[4,72,128]{2,1,0:T(8,128)S(1)}, f32[4,72,128]{2,1,0:T(8,128)S(1)}, u32[]{:S(2)}, u32[]{:S(2)}) collective-permute-start(f32[4,72,128]{2,1,0:T(8,128)S(1)} %get-tuple-element.26), channel_id=1, source_target_pairs={{0,24},{8,0},{16,8},{24,16},{1,25},{9,1},{17,9},{25,17},{2,26},{10... | collective-permute-start | bytes 442376 | tf_op jit(solution)/shard_map/ppermute | solution.py:274
  28.9 6.4 %collective-permute-start.8 = (f32[4,72,128]{2,1,0:T(8,128)S(1)}, f32[4,72,128]{2,1,0:T(8,128)S(1)}, u32[]{:S(2)}, u32[]{:S(2)}) collective-permute-start(f32[4,72,128]{2,1,0:T(8,128)S(1)} %get-tuple-element.27), channel_id=1, source_target_pairs={{0,16},{8,24},{16,0},{24,8},{1,17},{9,25},{17,1},{25,9},{2,18},{10... | collective-permute-start | bytes 442376 | tf_op jit(solution)/shard_map/ppermute | solution.py:274
  29.6 9.1 %collective-permute-start.1 = (f32[4,72,128]{2,1,0:T(8,128)S(1)}, f32[4,72,128]{2,1,0:T(8,128)S(1)}, u32[]{:S(2)}, u32[]{:S(2)}) collective-permute-start(f32[4,72,128]{2,1,0:T(8,128)S(1)} %get-tuple-element.28), channel_id=1, source_target_pairs={{0,1},{1,2},{2,3},{3,0},{4,5},{5,6},{6,7},{7,4},{8,9},{9,10},{10,1... | collective-permute-start | bytes 442376 | tf_op jit(solution)/shard_map/ppermute | solution.py:274
  30.8 9.5 %collective-permute-start.3 = (f32[4,72,128]{2,1,0:T(8,128)S(1)}, f32[4,72,128]{2,1,0:T(8,128)S(1)}, u32[]{:S(2)}, u32[]{:S(2)}) collective-permute-start(f32[4,72,128]{2,1,0:T(8,128)S(1)} %get-tuple-element.29), channel_id=1, source_target_pairs={{0,3},{1,0},{2,1},{3,2},{4,7},{5,4},{6,5},{7,6},{8,11},{9,8},{10,9... | collective-permute-start | bytes 442376 | tf_op jit(solution)/shard_map/ppermute | solution.py:274
  33.2 7.1 %collective-permute-start.2 = (f32[4,72,128]{2,1,0:T(8,128)S(1)}, f32[4,72,128]{2,1,0:T(8,128)S(1)}, u32[]{:S(2)}, u32[]{:S(2)}) collective-permute-start(f32[4,72,128]{2,1,0:T(8,128)S(1)} %get-tuple-element.30), channel_id=1, source_target_pairs={{0,2},{1,3},{2,0},{3,1},{4,6},{5,7},{6,4},{7,5},{8,10},{9,11},{10,... | collective-permute-start | bytes 442376 | tf_op jit(solution)/shard_map/ppermute | solution.py:274
  35.4 7.7 %collective-permute-start.10 = (f32[72,128]{1,0:T(8,128)S(1)}, f32[72,128]{1,0:T(8,128)S(1)}, u32[]{:S(2)}, u32[]{:S(2)}) collective-permute-start(f32[72,128]{1,0:T(8,128)S(1)} %get-tuple-element.34), channel_id=1, source_target_pairs={{0,1},{1,2},{2,3},{3,0},{4,5},{5,6},{6,7},{7,4},{8,9},{9,10},{10,1... | collective-permute-start | bytes 110600 | tf_op jit(solution)/shard_map/ppermute | solution.py:274
  37.2 6.6 %collective-permute-start.12 = (f32[72,128]{1,0:T(8,128)S(1)}, f32[72,128]{1,0:T(8,128)S(1)}, u32[]{:S(2)}, u32[]{:S(2)}) collective-permute-start(f32[72,128]{1,0:T(8,128)S(1)} %get-tuple-element.35), channel_id=1, source_target_pairs={{0,3},{1,0},{2,1},{3,2},{4,7},{5,4},{6,5},{7,6},{8,11},{9,8},{10,9... | collective-permute-start | bytes 110600 | tf_op jit(solution)/shard_map/ppermute | solution.py:274
  38.7 5.1 %collective-permute-start.11 = (f32[72,128]{1,0:T(8,128)S(1)}, f32[72,128]{1,0:T(8,128)S(1)}, u32[]{:S(2)}, u32[]{:S(2)}) collective-permute-start(f32[72,128]{1,0:T(8,128)S(1)} %get-tuple-element.36), channel_id=1, source_target_pairs={{0,2},{1,3},{2,0},{3,1},{4,6},{5,7},{6,4},{7,5},{8,10},{9,11},{10,... | collective-permute-start | bytes 110600 | tf_op jit(solution)/shard_map/ppermute | solution.py:274
  40.4 4.1 %collective-permute-start.4 = (f32[72,128]{1,0:T(8,128)S(1)}, f32[72,128]{1,0:T(8,128)S(1)}, u32[]{:S(2)}, u32[]{:S(2)}) collective-permute-start(f32[72,128]{1,0:T(8,128)S(1)} %get-tuple-element.31), channel_id=1, source_target_pairs={{0,8},{8,16},{16,24},{24,0},{1,9},{9,17},{17,25},{25,1},{2,10},{10... | collective-permute-start | bytes 110600 | tf_op jit(solution)/shard_map/ppermute | solution.py:274
  41.0 3.5 %collective-permute-start.6 = (f32[72,128]{1,0:T(8,128)S(1)}, f32[72,128]{1,0:T(8,128)S(1)}, u32[]{:S(2)}, u32[]{:S(2)}) collective-permute-start(f32[72,128]{1,0:T(8,128)S(1)} %get-tuple-element.32), channel_id=1, source_target_pairs={{0,24},{8,0},{16,8},{24,16},{1,25},{9,1},{17,9},{25,17},{2,26},{10... | collective-permute-start | bytes 110600 | tf_op jit(solution)/shard_map/ppermute | solution.py:274
  43.1 4.3 %collective-permute-start.5 = (f32[72,128]{1,0:T(8,128)S(1)}, f32[72,128]{1,0:T(8,128)S(1)}, u32[]{:S(2)}, u32[]{:S(2)}) collective-permute-start(f32[72,128]{1,0:T(8,128)S(1)} %get-tuple-element.33), channel_id=1, source_target_pairs={{0,16},{8,24},{16,0},{24,8},{1,17},{9,25},{17,1},{25,9},{2,18},{10... | collective-permute-start | bytes 110600 | tf_op jit(solution)/shard_map/ppermute | solution.py:274
  47.5 4.1 %collective-permute-start.13 = (f32[2,72,128]{2,1,0:T(8,128)S(1)}, f32[2,72,128]{2,1,0:T(8,128)S(1)}, u32[]{:S(2)}, u32[]{:S(2)}) collective-permute-start(f32[2,72,128]{2,1,0:T(8,128)S(1)} %pad_maximum_fusion), channel_id=1, source_target_pairs={{0,32},{32,0},{64,96},{96,64},{128,160},{160,128},{192,224},{224,1... | collective-permute-start | bytes 221192 | tf_op jit(solution)/shard_map/ppermute | solution.py:311
  51.5 4.7 %collective-permute-start.14 = (f32[2,72,128]{2,1,0:T(8,128)S(1)}, f32[2,72,128]{2,1,0:T(8,128)S(1)}, u32[]{:S(2)}, u32[]{:S(2)}) collective-permute-start(f32[2,72,128]{2,1,0:T(8,128)S(1)} %fusion.12), channel_id=1, source_target_pairs={{0,64},{32,96},{64,0},{96,32},{128,192},{160,224},{192,128},{224,1... | collective-permute-start | bytes 221192 | tf_op jit(solution)/shard_map/ppermute | solution.py:311
  56.3 8.6 %collective-permute-start.15 = (f32[2,72,128]{2,1,0:T(8,128)S(1)}, f32[2,72,128]{2,1,0:T(8,128)S(1)}, u32[]{:S(2)}, u32[]{:S(2)}) collective-permute-start(f32[2,72,128]{2,1,0:T(8,128)S(1)} %fusion.14), channel_id=1, source_target_pairs={{0,128},{32,160},{64,192},{96,224},{128,0},{160,32},{192,64},{224,... | collective-permute-start | bytes 221192 | tf_op jit(solution)/shard_map/ppermute | solution.py:311
  65.0 6.8 %collective-permute-start.16 = (f32[2,72,128]{2,1,0:T(8,128)S(1)}, f32[2,72,128]{2,1,0:T(8,128)S(1)}, u32[]{:S(2)}, u32[]{:S(2)}) collective-permute-start(f32[2,72,128]{2,1,0:T(8,128)S(1)} %get-tuple-element.22), channel_id=1, source_target_pairs={{0,8},{8,16},{16,24},{24,0},{1,9},{9,17},{17,25},{25,1},{2,10},{10... | collective-permute-start | bytes 221192 | tf_op jit(solution)/shard_map/ppermute | solution.py:274
  65.1 6.7 %collective-permute-start.17 = (f32[2,72,128]{2,1,0:T(8,128)S(1)}, f32[2,72,128]{2,1,0:T(8,128)S(1)}, u32[]{:S(2)}, u32[]{:S(2)}) collective-permute-start(f32[2,72,128]{2,1,0:T(8,128)S(1)} %get-tuple-element.22), channel_id=1, source_target_pairs={{0,16},{8,24},{16,0},{24,8},{1,17},{9,25},{17,1},{25,9},{2,18},{10... | collective-permute-start | bytes 221192 | tf_op jit(solution)/shard_map/ppermute | solution.py:274
  66.4 5.4 %collective-permute-start.18 = (f32[2,72,128]{2,1,0:T(8,128)S(1)}, f32[2,72,128]{2,1,0:T(8,128)S(1)}, u32[]{:S(2)}, u32[]{:S(2)}) collective-permute-start(f32[2,72,128]{2,1,0:T(8,128)S(1)} %get-tuple-element.22), channel_id=1, source_target_pairs={{0,24},{8,0},{16,8},{24,16},{1,25},{9,1},{17,9},{25,17},{2,26},{10... | collective-permute-start | bytes 221192 | tf_op jit(solution)/shard_map/ppermute | solution.py:274
  71.8 7.9 %collective-permute-start.19 = (f32[4,2,72,128]{3,2,1,0:T(8,128)S(1)}, f32[4,2,72,128]{3,2,1,0:T(8,128)S(1)}, u32[]{:S(2)}, u32[]{:S(2)}) collective-permute-start(f32[4,2,72,128]{3,2,1,0:T(8,128)S(1)} %bitcast_dynamic-update-slice_fusion.4), channel_id=1, source_target_pairs={{0,1},{1,2},{2,3},{3,0},{4,5},{5,6},{6,7},{7,4},{8,9},{9,10},{10,1... | collective-permute-start | bytes 884744 | tf_op jit(solution)/shard_map/ppermute | solution.py:274
  72.0 10.5 %collective-permute-start.21 = (f32[4,2,72,128]{3,2,1,0:T(8,128)S(1)}, f32[4,2,72,128]{3,2,1,0:T(8,128)S(1)}, u32[]{:S(2)}, u32[]{:S(2)}) collective-permute-start(f32[4,2,72,128]{3,2,1,0:T(8,128)S(1)} %bitcast_dynamic-update-slice_fusion.4), channel_id=1, source_target_pairs={{0,3},{1,0},{2,1},{3,2},{4,7},{5,4},{6,5},{7,6},{8,11},{9,8},{10,9... | collective-permute-start | bytes 884744 | tf_op jit(solution)/shard_map/ppermute | solution.py:274
  74.6 7.9 %collective-permute-start.20 = (f32[4,2,72,128]{3,2,1,0:T(8,128)S(1)}, f32[4,2,72,128]{3,2,1,0:T(8,128)S(1)}, u32[]{:S(2)}, u32[]{:S(2)}) collective-permute-start(f32[4,2,72,128]{3,2,1,0:T(8,128)S(1)} %bitcast_dynamic-update-slice_fusion.4), channel_id=1, source_target_pairs={{0,2},{1,3},{2,0},{3,1},{4,6},{5,7},{6,4},{7,5},{8,10},{9,11},{10,... | collective-permute-start | bytes 884744 | tf_op jit(solution)/shard_map/ppermute | solution.py:274
  75.0 52.8 %copy-start.2 = (f32[1024,1024]{1,0:T(8,128)S(1)}, f32[1024,1024]{1,0:T(8,128)}, u32[]{:S(2)}) copy-start(f32[1024,1024]{1,0:T(8,128)} %t_ref.3) | copy-start | bytes 12582916
  82.6 12.8 %collective-permute-start.22 = (f32[18,128,128]{2,1,0:T(8,128)S(1)}, f32[18,128,128]{2,1,0:T(8,128)S(1)}, u32[]{:S(2)}, u32[]{:S(2)}) collective-permute-start(f32[18,128,128]{2,1,0:T(8,128)S(1)} %bitcast.81), channel_id=1, source_target_pairs={{0,4},{4,0},{1,5},{5,1},{2,6},{6,2},{3,7},{7,3},{8,12},{12,8},{9,1... | collective-permute-start | bytes 3538952 | tf_op jit(solution)/shard_map/ppermute | solution.py:269
  134.7 1.3 copy-start.3
  140.6 5.8 %copy-start = (f32[512,8,1024]{2,1,0:T(8,128)S(1)}, f32[512,8,1024]{2,1,0:T(8,128)}, u32[]{:S(2)}) copy-start(f32[512,8,1024]{2,1,0:T(8,128)} %all-gather.3.cloned.1.call-done) | copy-start | bytes 50331652
  146.4 1.6 copy-start.4
Sparse Core Ops, SparseCore 0:
  11.0 129.6 all-gather.2

commit v3 on v2

--- a/solution.py
+++ b/solution.py
@@ -12,6 +12,10 @@
 NT = ((1,), (1,))
 TN = ((0,), (0,))
 MIB = 1024 * 1024
+
+
+def cost(flops, size):
+    return pl.CostEstimate(flops=flops, bytes_accessed=size, transcendentals=0)
 
 
 def dot(a, b, dims):
@@ -99,7 +103,7 @@
     return out
 
 
-def gram_kernel(n, core_ref, t_ref, mine_ref, other_ref, th_ref, tl_ref):
+def gram_kernel(n, core_ref, t_ref, mine_ref, other_ref, th_ref, tl_ref, halves_ref):
     core = core_ref[0]
     for j in range(n):
         at = slice(256 * j, 256 * j + 256)
@@ -116,17 +120,10 @@
             block = dot3((th_ref[of, :], tl_ref[of, :]), right, NN)
             for k, (p, row, column) in enumerate(list_of):
                 if p == place:
-                    part = block[row:row + 128, column:column + 128]
-                    at = k % half
-
-                    @pl.when(core == k // half)
-                    def _():
-                        mine_ref[at] = part
-
-                    @pl.when(core != k // half)
-                    def _():
-                        other_ref[at] = part
+                    halves_ref[core ^ (k // half), k % half] = block[row:row + 128, column:column + 128]
             place += 1
+    mine_ref[...] = halves_ref[0]
+    other_ref[...] = halves_ref[1]
 
 
 def gram(core, t, n):
@@ -138,8 +135,9 @@
         out_shape=(jax.ShapeDtypeStruct((half, 128, 128), jnp.float32),) * 2,
         in_specs=[pl.BlockSpec(memory_space=pltpu.SMEM), whole],
         out_specs=(whole,) * 2,
-        scratch_shapes=[pltpu.VMEM((features, m), jnp.bfloat16)] * 2,
+        scratch_shapes=[pltpu.VMEM((features, m), jnp.bfloat16)] * 2 + [pltpu.VMEM((2, half, 128, 128), jnp.float32)],
         compiler_params=pltpu.CompilerParams(vmem_limit_bytes=28 * MIB),
+        cost_estimate=cost(6 * m * features * features, 7 * MIB),
     )(core, t)
 
 
@@ -198,6 +196,7 @@
         out_specs=(whole,) * 2,
         scratch_shapes=[pltpu.VMEM((blocks, 256, 256), jnp.float32)],
         compiler_params=pltpu.CompilerParams(vmem_limit_bytes=20 * MIB),
+        cost_estimate=cost(32 * (256 * n) ** 3, 6 * MIB),
     )(core, mine, other)
 
 
@@ -229,40 +228,45 @@
         in_specs=[whole] * 3,
         out_specs=(whole,) * 2,
         compiler_params=pltpu.CompilerParams(vmem_limit_bytes=36 * MIB),
+        cost_estimate=cost(6 * m * features * features, 12 * MIB),
     )(t, l, d)
 
 
-def score_kernel(pick_ref, wh_ref, wl_ref, v_ref, out_ref):
+def score_kernel(slots, pick_ref, wh_ref, wl_ref, *refs):
     step = pl.program_id(0)
-    slots = v_ref.shape[0]
     rows = []
     for s in range(slots):
-        pick = pick_ref[step * slots + s]
-        first = (pick == 0).astype(jnp.float32)
-        second = (pick == 1).astype(jnp.float32)
-        for y in range(v_ref.shape[1]):
-            rows.append(v_ref[s, y, 0] * first + v_ref[s, y, 1] * second)
+        live = (pick_ref[step * slots + s] >= 0).astype(jnp.float32)
+        block = refs[s][...]
+        rows.append(block.reshape(-1, block.shape[-1]) * live)
     v = split(jnp.concatenate(rows, axis=0))
-    out_ref[...] = dot3((wh_ref[...], wl_ref[...]), v, NT)
+    refs[slots][...] = dot3((wh_ref[...], wl_ref[...]), v, NT)
 
 
 def score(pick, wh, wl, v, slots):
     m, features = wh.shape
-    total, groups, blocks, part, _ = v.shape
+    total, groups, part = pick.shape[0], v.shape[1], v.shape[3]
     width = slots * groups * part
     whole = pl.BlockSpec(memory_space=pltpu.VMEM)
+
+    def slot(s):
+        def index(i, pick_ref):
+            j = i * slots + s
+            return lax.rem(j, v.shape[0]), 0, jnp.maximum(pick_ref[j], 0), 0, 0
+        return pl.BlockSpec((1, groups, 1, part, features), index)
+
     return pl.pallas_call(
-        score_kernel,
-        grid=(total // slots,),
+        functools.partial(score_kernel, slots),
+        grid_spec=pltpu.PrefetchScalarGridSpec(
+            num_scalar_prefetch=1,
+            grid=(total // slots,),
+            in_specs=[whole, whole] + [slot(s) for s in range(slots)],
+            out_specs=pl.BlockSpec((m, width), lambda i, pick_ref: (0, i)),
+        ),
         out_shape=jax.ShapeDtypeStruct((m, total * groups * part), jnp.float32),
-        in_specs=[
-            pl.BlockSpec(memory_space=pltpu.SMEM),
-            whole, whole,
-            pl.BlockSpec((slots, groups, blocks, part, features), lambda i: (i, 0, 0, 0, 0)),
-        ],
-        out_specs=pl.BlockSpec((m, width), lambda i: (0, i)),
-        compiler_params=pltpu.CompilerParams(vmem_limit_bytes=32 * MIB),
-    )(pick, wh, wl, v)
+        compiler_params=pltpu.CompilerParams(vmem_limit_bytes=48 * MIB),
+        cost_estimate=cost(6 * m * width * total // slots * features, 20 * MIB),
+    )(pick, wh, wl, *([v] * slots))
 
 
 def swap(v):
@@ -303,7 +307,7 @@
     v = (mine + swap(other)).reshape(ny, nx, 2, -1, 128)
     by_y, by_x = scatter(v[:, :, 0], "y", 0), scatter(v[:, :, 1], "x", 1)
     left, right = add(by_y), add(by_x)
-    left, beside = lax.optimization_barrier((left, beside))
+    left, right, beside = lax.optimization_barrier((left, right, beside))
     by_x, by_y = scatter(left, "x", 0), scatter(right, "y", 0)
     s = jnp.stack([add(by_x), add(by_y)])
     hop = 1
@@ -313,26 +317,37 @@
     return gather(gather(s, "x"), "y").reshape(shape), beside
 
 
+def beside_z(v, hops):
+    size = lax.axis_size("z")
+    return jnp.concatenate([v] + [lax.ppermute(v, "z", [(i, i ^ h) for i in range(size)]) for h in hops])
+
+
 def local(train_grads, val_grads, wanted, owner):
     m, features = train_grads.shape
     n = features // 256
     dp = ("z", "x", "core")
     slabs, group = lax.axis_size(dp), lax.axis_size("y")
     blocks, part, _ = val_grads.shape
-    val_all = lax.all_gather(val_grads, dp + ("y",), tiled=False)
-    val_all = val_all.reshape(slabs, group, blocks, part, features)
+    size = lax.axis_size("z")
+    held = beside_z(val_grads, range(2, size, 2))
 
     positions = jnp.arange(slabs, dtype=jnp.int32)
     holder = jnp.sum(jnp.where(owner == lax.axis_index(dp), positions, 0))
     request = lax.dynamic_index_in_dim(wanted, holder, 0, keepdims=False)
-    pick = jnp.where(request >= 0, request - positions * blocks, -1)
+    plane = slabs // size
+    apart = (positions // plane) ^ lax.axis_index("z")
+    at = (apart & 1) * (size // 2) + (apart >> 1)
+    pick = jnp.where(request >= 0, at * blocks + request - positions * blocks, -1)
 
     core = lax.axis_index("core").reshape(1)
     mine, other = gram(core, train_grads, n)
-    mine, pick = sum_all(mine, other, pick)
+    mine, other, held = lax.optimization_barrier((mine, other, held))
+    mine, (pick, held) = sum_all(mine, other, (pick, beside_z(held, [1])))
+    val_all = lax.all_gather(held, ("x", "core", "y"), tiled=False)
+    val_all = val_all.reshape(plane, group, size * blocks, part, features)
     l, d = factor(core, mine, swap(mine), n, 1.0 / (m * slabs * group))
     wh, wl = solve(train_grads, l, d, n)
-    return score(pick, wh, wl, val_all, 8)
+    return score(pick, wh, wl, val_all, 16)
 
 
 def solution(mesh):

time: 172 us -> 185 us (1.076); the launches traced: 172 us -> 182 us
  starting transfers between devices: 46.2 us -> 62.9 us
  local copies, waits for them, and re-layouts: 11.3 us -> 5.52 us
  Pallas kernels: 66.3 us -> 62.8 us
  other arithmetic: 1.67 us -> 3.79 us
    ppermute x0 -> x4, starting transfers between devices: none -> 10.1 us  [beside_z(): lax.ppermute(v, 'z', [(i, i ^ h) for i in range(size)])]
    ppermute x2, starting transfers between devices: 13.7 us -> 21.9 us  [swap(): return lax.ppermute(v, 'core', [(0, 1), (1, 0)])]
    unnamed x12, local copies, waits for them, and re-layouts: 10.9 us -> 5.11 us
    pallas_call x1, Pallas kernels: 10.3 us -> 4.62 us  [gram(): pl.pallas_call(functools.partial(gram_kernel, n), out_shape=(jax.ShapeDty...]
    ppermute x18, waiting for transfers between devices: 16.9 us -> 21.7 us  [ring(): return lax.ppermute(v, axis, [(i, (i + k) % size) for i in range(size)])]
    all_gather x1, waiting for transfers between devices: 4.63 us -> 0.01 us  [local(): val_all = lax.all_gather(held, ('x', 'core', 'y'), tiled=False)]
    ppermute x3, starting transfers between devices: 11.7 us -> 8.64 us  [sum_all(): s = s + lax.ppermute(s, 'z', [(i, i ^ hop) for i in range(nz)])]
    pallas_call x1, Pallas kernels: 16.7 us -> 19 us  [score(): pl.pallas_call(functools.partial(score_kernel, slots), grid_spec=pltpu.Pr...]
  transfers between devices with their start and end apart: 24 -> 28, of which waited for: 13 -> 14; matrix products, arithmetic and copies ran while one was open for 1% -> 2% of each run, Pallas kernels for 29% -> 24%
where the time goes in v3:
time: 185 us; the launch traced here: 182 us
  starting transfers between devices  62.9 us (34%)
  Pallas kernels  62.8 us (34%)
  waiting for transfers between devices  31.9 us (17%)
  between operations  15.6 us (8%)
  local copies, waits for them, and re-layouts  5.52 us (3%)
  other arithmetic  3.79 us (2%)
    pallas_call x1, Pallas kernels, factor(): pl.pallas_call(functools.partial(factor_kernel, n, scale), out_shape=(jax...  32.5 us
    ppermute x18, starting transfers between devices, ring(): return lax.ppermute(v, axis, [(i, (i + k) % size) for i in range(size)])  22.3 us
    ppermute x2, starting transfers between devices, swap(): return lax.ppermute(v, 'core', [(0, 1), (1, 0)])  21.9 us
    ppermute x18, waiting for transfers between devices, ring(): return lax.ppermute(v, axis, [(i, (i + k) % size) for i in range(size)])  21.7 us
    pallas_call x1, Pallas kernels, score(): pl.pallas_call(functools.partial(score_kernel, slots), grid_spec=pltpu.Pr...  19 us
    ppermute x4, starting transfers between devices, beside_z(): lax.ppermute(v, 'z', [(i, i ^ h) for i in range(size)])  10.1 us
    ppermute x3, starting transfers between devices, sum_all(): s = s + lax.ppermute(s, 'z', [(i, i ^ hop) for i in range(nz)])  8.64 us
    pallas_call x1, Pallas kernels, solve(): pl.pallas_call(functools.partial(solve_kernel, n, features ** (-0.5)), ou...  6.8 us
  transfers between devices with their start and end apart: 28, of which 14 were waited for; matrix products, arithmetic and copies ran while one was open for 2% of the time, Pallas kernels for 24%

profile of v3, /device:TPU:1, one launch (start us, length us, event | category | flops | bytes accessed | tf_op | source)
XLA Modules:
  0.0 182.5 jit_solution(772950817485535622)
XLA Ops:
  6.5 7.7 %collective-permute-start.1 = (f32[2,8,1024]{2,1,0:T(8,128)}, f32[2,8,1024]{2,1,0:T(8,128)S(1)}, u32[]{:S(2)}, u32[]{:S(2)}) collective-permute-start(f32[2,8,1024]{2,1,0:T(8,128)} %param.5), channel_id=1, source_target_pairs={{0,128},{32,160},{64,192},{96,224},{128,0},{160,32},{192,64},{224,... | collective-permute-start | bytes 196616 | tf_op jit(solution)/shard_map/ppermute | solution.py:322
  14.3 1.2 collective-permute-start
  15.5 0.0 collective-permute-start.2
  15.5 2.2 %copy-done.2 = f32[1024,1024]{1,0:T(8,128)S(1)} copy-done((f32[1024,1024]{1,0:T(8,128)S(1)}, f32[1024,1024]{1,0:T(8,128)}, u32[]{:S(2)}) %copy-start.2) | copy-done | bytes 4194328
  17.7 4.6 %shard_map.46 = (f32[18,128,128]{2,1,0:T(8,128)S(1)}, f32[18,128,128]{2,1,0:T(8,128)S(1)}) custom-call(s32[1]{0:T(128)} %bitcast.core_ref, f32[1024,1024]{1,0:T(8,128)S(1)} %copy-done.2), custom_call_target="tpu_custom_call" | custom-call | flops 6442450944 | bytes 7340032 | tf_op jit(solution)/shard_map/pallas_call | solution.py:133
  22.3 0.0 collective-permute-done.1
  22.3 0.0 collective-permute-done
  22.3 0.0 collective-permute-done.2
  22.4 1.3 collective-permute-start.3
  23.7 0.7 fusion.11
  26.3 0.7 compare_select_fusion.pick_ref
  27.0 1.2 collective-permute-start.10
  28.1 0.0 collective-permute-done.3
  28.1 1.4 add.162
  29.5 0.1 fusion.14
  29.7 1.3 collective-permute-start.7
  31.0 1.5 collective-permute-start.9
  32.4 1.5 collective-permute-start.8
  34.0 0.9 collective-permute-done.10
  34.8 0.8 pad_maximum_fusion
  35.7 1.4 collective-permute-start.4
  37.1 1.5 collective-permute-start.6
  38.6 0.0 collective-permute-done.7
  38.6 1.6 collective-permute-start.5
  40.2 0.0 collective-permute-done.8
  40.3 1.4 collective-permute-done.4
  41.6 4.3 %collective-permute-done.5 = f32[4,72,128]{2,1,0:T(8,128)S(1)} collective-permute-done((f32[4,72,128]{2,1,0:T(8,128)S(1)}, f32[4,72,128]{2,1,0:T(8,128)S(1)}, u32[]{:S(2)}, u32[]{:S(2)}) %collective-permute-start.5) | collective-permute-done | bytes 147488 | tf_op jit(solution)/shard_map/ppermute | solution.py:278
  46.0 0.0 all-gather.3.cloned.1.call-update
  46.1 1.5 collective-permute-start.11
  47.5 1.5 collective-permute-start.13
  49.0 1.5 collective-permute-start.12
  50.5 0.3 collective-permute-start.14
  50.8 2.5 %collective-permute-start.16 = (f32[72,128]{1,0:T(8,128)S(1)}, f32[72,128]{1,0:T(8,128)S(1)}, u32[]{:S(2)}, u32[]{:S(2)}) collective-permute-start(f32[72,128]{1,0:T(8,128)S(1)} %get-tuple-element.45), channel_id=1, source_target_pairs={{0,3},{1,0},{2,1},{3,2},{4,7},{5,4},{6,5},{7,6},{8,11},{9,8},{10,9... | collective-permute-start | bytes 110600 | tf_op jit(solution)/shard_map/ppermute | solution.py:278
  53.3 0.3 collective-permute-done.12
  53.6 1.1 collective-permute-done.14
  54.6 0.0 collective-permute-done.16
  54.6 3.3 %collective-permute-done.15 = f32[72,128]{1,0:T(8,128)S(1)} collective-permute-done((f32[72,128]{1,0:T(8,128)S(1)}, f32[72,128]{1,0:T(8,128)S(1)}, u32[]{:S(2)}, u32[]{:S(2)}) %collective-permute-start.15) | collective-permute-done | bytes 36896 | tf_op jit(solution)/shard_map/ppermute | solution.py:278
  58.0 1.2 collective-permute-start.17
  59.2 2.2 %collective-permute-done.17 = f32[2,72,128]{2,1,0:T(8,128)S(1)} collective-permute-done((f32[2,72,128]{2,1,0:T(8,128)S(1)}, f32[2,72,128]{2,1,0:T(8,128)S(1)}, u32[]{:S(2)}, u32[]{:S(2)}) %collective-permute-start.17) | collective-permute-done | bytes 73760 | tf_op jit(solution)/shard_map/ppermute | solution.py:315
  61.5 1.9 %collective-permute-start.18 = (f32[2,72,128]{2,1,0:T(8,128)S(1)}, f32[2,72,128]{2,1,0:T(8,128)S(1)}, u32[]{:S(2)}, u32[]{:S(2)}) collective-permute-start(f32[2,72,128]{2,1,0:T(8,128)S(1)} %fusion.13), channel_id=1, source_target_pairs={{0,64},{32,96},{64,0},{96,32},{128,192},{160,224},{192,128},{224,1... | collective-permute-start | bytes 221192 | tf_op jit(solution)/shard_map/ppermute | solution.py:315
  63.4 2.7 %collective-permute-done.18 = f32[2,72,128]{2,1,0:T(8,128)S(1)} collective-permute-done((f32[2,72,128]{2,1,0:T(8,128)S(1)}, f32[2,72,128]{2,1,0:T(8,128)S(1)}, u32[]{:S(2)}, u32[]{:S(2)}) %collective-permute-start.18) | collective-permute-done | bytes 73760 | tf_op jit(solution)/shard_map/ppermute | solution.py:315
  66.1 5.5 %collective-permute-start.19 = (f32[2,72,128]{2,1,0:T(8,128)S(1)}, f32[2,72,128]{2,1,0:T(8,128)S(1)}, u32[]{:S(2)}, u32[]{:S(2)}) collective-permute-start(f32[2,72,128]{2,1,0:T(8,128)S(1)} %fusion.15), channel_id=1, source_target_pairs={{0,128},{32,160},{64,192},{96,224},{128,0},{160,32},{192,64},{224,... | collective-permute-start | bytes 221192 | tf_op jit(solution)/shard_map/ppermute | solution.py:315
  71.6 1.8 collective-permute-done.19
  73.4 0.4 collective-permute-start.20
  73.8 1.7 collective-permute-start.21
  75.6 1.5 collective-permute-start.22
  77.0 1.7 collective-permute-done.20
  78.7 0.0 collective-permute-done.21
  78.7 0.8 collective-permute-done.22
  79.6 0.1 collective-permute-start.23
  79.7 2.7 %collective-permute-start.25 = (f32[4,2,72,128]{3,2,1,0:T(8,128)S(1)}, f32[4,2,72,128]{3,2,1,0:T(8,128)S(1)}, u32[]{:S(2)}, u32[]{:S(2)}) collective-permute-start(f32[4,2,72,128]{3,2,1,0:T(8,128)S(1)} %bitcast_dynamic-update-slice_fusion.4), channel_id=1, source_target_pairs={{0,3},{1,0},{2,1},{3,2},{4,7},{5,4},{6,5},{7,6},{8,11},{9,8},{10,9... | collective-permute-start | bytes 884744 | tf_op jit(solution)/shard_map/ppermute | solution.py:278
  82.3 0.1 broadcast_in_dim.38
  82.5 6.8 %collective-permute-done.23 = f32[4,2,72,128]{3,2,1,0:T(8,128)S(1)} collective-permute-done((f32[4,2,72,128]{3,2,1,0:T(8,128)S(1)}, f32[4,2,72,128]{3,2,1,0:T(8,128)S(1)}, u32[]{:S(2)}, u32[]{:S(2)}) %collective-permute-start.23) | collective-permute-done | bytes 294944 | tf_op jit(solution)/shard_map/ppermute | solution.py:278
  89.3 2.0 %collective-permute-done.24 = f32[4,2,72,128]{3,2,1,0:T(8,128)S(1)} collective-permute-done((f32[4,2,72,128]{3,2,1,0:T(8,128)S(1)}, f32[4,2,72,128]{3,2,1,0:T(8,128)S(1)}, u32[]{:S(2)}, u32[]{:S(2)}) %collective-permute-start.24) | collective-permute-done | bytes 294944 | tf_op jit(solution)/shard_map/ppermute | solution.py:278
  91.4 0.0 collective-permute-done.25
  91.4 0.0 copy-start.3
  91.4 20.6 %collective-permute-start.26 = (f32[18,128,128]{2,1,0:T(8,128)S(1)}, f32[18,128,128]{2,1,0:T(8,128)S(1)}, u32[]{:S(2)}, u32[]{:S(2)}) collective-permute-start(f32[18,128,128]{2,1,0:T(8,128)S(1)} %bitcast.80), channel_id=1, source_target_pairs={{0,4},{4,0},{1,5},{5,1},{2,6},{6,2},{3,7},{7,3},{8,12},{12,8},{9,1... | collective-permute-start | bytes 3538952 | tf_op jit(solution)/shard_map/ppermute | solution.py:273
  112.0 2.5 %collective-permute-done.26.other_ref = f32[18,128,128]{2,1,0:T(8,128)S(1)} collective-permute-done((f32[18,128,128]{2,1,0:T(8,128)S(1)}, f32[18,128,128]{2,1,0:T(8,128)S(1)}, u32[]{:S(2)}, u32[]{:S(2)}) %collective-permute-start.26) | collective-permute-done | bytes 1179680 | tf_op jit(solution)/shard_map/ppermute | solution.py:273
  114.5 32.5 %shard_map.47 = (f32[10,256,256]{2,1,0:T(8,128)S(1)}, f32[4,256,256]{2,1,0:T(8,128)S(1)}) custom-call(s32[1]{0:T(128)} %bitcast.core_ref, f32[18,128,128]{2,1,0:T(8,128)S(1)} %bitcast.81, f32[18,128,128]{2,1,0:T(8,128)S(1)} %collective-permute-done.26.other_ref), custom_call_target="tpu_custom_call" | custom-call | flops 34359738368 | bytes 6291456 | tf_op jit(solution)/shard_map/pallas_call | solution.py:189
  147.0 6.8 %shard_map.48 = (bf16[1024,1024]{1,0:T(8,128)(2,1)S(1)}, bf16[1024,1024]{1,0:T(8,128)(2,1)S(1)}) custom-call(f32[1024,1024]{1,0:T(8,128)S(1)} %copy-done.3, f32[10,256,256]{2,1,0:T(8,128)S(1)} %get-tuple-element.26.l_ref, f32[4,256,256]{2,1,0:T(8,128)S(1)} %get-tuple-element.27.d_ref), custom_call_target="tpu_custom_call" | custom-call | flops 6442450944 | bytes 12582912 | tf_op jit(solution)/shard_map/pallas_call | solution.py:225
  153.8 0.0 copy-start
  153.8 1.3 copy-done
  155.1 1.6 copy-done.1
  156.7 19.0 %shard_map.49 = f32[1024,2048]{1,0:T(8,128)} custom-call(s32[64]{0:T(128)S(1)} %compare_select_fusion.pick_ref, bf16[1024,1024]{1,0:T(8,128)(2,1)S(1)} %get-tuple-element.28.wh_ref, bf16[1024,1024]{1,0:T(8,128)(2,1)S(1)} %copy-done.1, f32[8,4,16,8,1024]{4,3,2,1,0:T(8,128)} %bitcast.82, f32[8,4,16,8,1024]{4,3,2,1,0:T(8,128)} %bitcast.83, ...), custom_call_target="tpu_custom_call" | custom-call | flops 12884901888 | bytes 20971520 | tf_op jit(solution)/shard_map/pallas_call | solution.py:258
  (36 shorter events, 0.5 us)
Async XLA Ops:
  6.5 148.5 %all-gather.3.cloned.1.call-start = ((), (), s32[]{:S(2)}) async-start(), calls=%async_computation | async-start | bytes 17301504 | tf_op jit(solution)/shard_map/all_gather | solution.py:346
  6.5 15.8 %collective-permute-start.1 = (f32[2,8,1024]{2,1,0:T(8,128)}, f32[2,8,1024]{2,1,0:T(8,128)S(1)}, u32[]{:S(2)}, u32[]{:S(2)}) collective-permute-start(f32[2,8,1024]{2,1,0:T(8,128)} %param.5), channel_id=1, source_target_pairs={{0,128},{32,160},{64,192},{96,224},{128,0},{160,32},{192,64},{224,... | collective-permute-start | bytes 196616 | tf_op jit(solution)/shard_map/ppermute | solution.py:322
  14.3 8.0 %collective-permute-start = (f32[2,8,1024]{2,1,0:T(8,128)}, f32[2,8,1024]{2,1,0:T(8,128)S(1)}, u32[]{:S(2)}, u32[]{:S(2)}) collective-permute-start(f32[2,8,1024]{2,1,0:T(8,128)} %param.5), channel_id=1, source_target_pairs={{0,64},{32,96},{64,0},{96,32},{128,192},{160,224},{192,128},{224,1... | collective-permute-start | bytes 196616 | tf_op jit(solution)/shard_map/ppermute | solution.py:322
  15.5 6.9 %collective-permute-start.2 = (f32[2,8,1024]{2,1,0:T(8,128)}, f32[2,8,1024]{2,1,0:T(8,128)S(1)}, u32[]{:S(2)}, u32[]{:S(2)}) collective-permute-start(f32[2,8,1024]{2,1,0:T(8,128)} %param.5), channel_id=1, source_target_pairs={{0,192},{32,224},{64,128},{96,160},{128,64},{160,96},{192,0},{224,... | collective-permute-start | bytes 196616 | tf_op jit(solution)/shard_map/ppermute | solution.py:322
  15.5 2.2 %copy-start.2 = (f32[1024,1024]{1,0:T(8,128)S(1)}, f32[1024,1024]{1,0:T(8,128)}, u32[]{:S(2)}) copy-start(f32[1024,1024]{1,0:T(8,128)} %t_ref.3) | copy-start | bytes 12582916
  17.7 4.7 %copy-start.4 = (f32[2,8,1024]{2,1,0:T(8,128)S(1)}, f32[2,8,1024]{2,1,0:T(8,128)}, u32[]{:S(2)}) copy-start(f32[2,8,1024]{2,1,0:T(8,128)} %param.5) | copy-start | bytes 196612
  17.7 6.0 %copy-start.5 = (s32[64]{0:T(128)S(1)}, s32[64]{0:T(128)}, u32[]{:S(2)}) copy-start(s32[64]{0:T(128)} %param.7) | copy-start | bytes 772
  22.4 5.8 %collective-permute-start.3 = (f32[18,128,128]{2,1,0:T(8,128)S(1)}, f32[18,128,128]{2,1,0:T(8,128)}, u32[]{:S(2)}, u32[]{:S(2)}) collective-permute-start(f32[18,128,128]{2,1,0:T(8,128)S(1)} %get-tuple-element.21), channel_id=1, source_target_pairs={{0,4},{4,0},{1,5},{5,1},{2,6},{6,2},{3,7},{7,3},{8,12},{12,8},{9,1... | collective-permute-start | bytes 3538952 | tf_op jit(solution)/shard_map/ppermute | solution.py:273
  27.0 7.9 %collective-permute-start.10 = (f32[8,8,1024]{2,1,0:T(8,128)S(1)}, f32[8,8,1024]{2,1,0:T(8,128)S(1)}, u32[]{:S(2)}, u32[]{:S(2)}) collective-permute-start(f32[8,8,1024]{2,1,0:T(8,128)S(1)} %pad_maximum_fusion.1), channel_id=1, source_target_pairs={{0,32},{32,0},{64,96},{96,64},{128,160},{160,128},{192,224},{224,1... | collective-permute-start | bytes 786440 | tf_op jit(solution)/shard_map/ppermute | solution.py:322
  29.7 8.9 %collective-permute-start.7 = (f32[4,72,128]{2,1,0:T(8,128)S(1)}, f32[4,72,128]{2,1,0:T(8,128)S(1)}, u32[]{:S(2)}, u32[]{:S(2)}) collective-permute-start(f32[4,72,128]{2,1,0:T(8,128)S(1)} %get-tuple-element.35), channel_id=1, source_target_pairs={{0,8},{8,16},{16,24},{24,0},{1,9},{9,17},{17,25},{25,1},{2,10},{10... | collective-permute-start | bytes 442376 | tf_op jit(solution)/shard_map/ppermute | solution.py:278
  31.0 9.2 %collective-permute-start.9 = (f32[4,72,128]{2,1,0:T(8,128)S(1)}, f32[4,72,128]{2,1,0:T(8,128)S(1)}, u32[]{:S(2)}, u32[]{:S(2)}) collective-permute-start(f32[4,72,128]{2,1,0:T(8,128)S(1)} %get-tuple-element.36), channel_id=1, source_target_pairs={{0,24},{8,0},{16,8},{24,16},{1,25},{9,1},{17,9},{25,17},{2,26},{10... | collective-permute-start | bytes 442376 | tf_op jit(solution)/shard_map/ppermute | solution.py:278
  32.4 7.8 %collective-permute-start.8 = (f32[4,72,128]{2,1,0:T(8,128)S(1)}, f32[4,72,128]{2,1,0:T(8,128)S(1)}, u32[]{:S(2)}, u32[]{:S(2)}) collective-permute-start(f32[4,72,128]{2,1,0:T(8,128)S(1)} %get-tuple-element.37), channel_id=1, source_target_pairs={{0,16},{8,24},{16,0},{24,8},{1,17},{9,25},{17,1},{25,9},{2,18},{10... | collective-permute-start | bytes 442376 | tf_op jit(solution)/shard_map/ppermute | solution.py:278
  35.7 5.9 %collective-permute-start.4 = (f32[4,72,128]{2,1,0:T(8,128)S(1)}, f32[4,72,128]{2,1,0:T(8,128)S(1)}, u32[]{:S(2)}, u32[]{:S(2)}) collective-permute-start(f32[4,72,128]{2,1,0:T(8,128)S(1)} %get-tuple-element.38), channel_id=1, source_target_pairs={{0,1},{1,2},{2,3},{3,0},{4,5},{5,6},{6,7},{7,4},{8,9},{9,10},{10,1... | collective-permute-start | bytes 442376 | tf_op jit(solution)/shard_map/ppermute | solution.py:278
  37.1 4.6 %collective-permute-start.6 = (f32[4,72,128]{2,1,0:T(8,128)S(1)}, f32[4,72,128]{2,1,0:T(8,128)S(1)}, u32[]{:S(2)}, u32[]{:S(2)}) collective-permute-start(f32[4,72,128]{2,1,0:T(8,128)S(1)} %get-tuple-element.39), channel_id=1, source_target_pairs={{0,3},{1,0},{2,1},{3,2},{4,7},{5,4},{6,5},{7,6},{8,11},{9,8},{10,9... | collective-permute-start | bytes 442376 | tf_op jit(solution)/shard_map/ppermute | solution.py:278
  38.6 7.4 %collective-permute-start.5 = (f32[4,72,128]{2,1,0:T(8,128)S(1)}, f32[4,72,128]{2,1,0:T(8,128)S(1)}, u32[]{:S(2)}, u32[]{:S(2)}) collective-permute-start(f32[4,72,128]{2,1,0:T(8,128)S(1)} %get-tuple-element.40), channel_id=1, source_target_pairs={{0,2},{1,3},{2,0},{3,1},{4,6},{5,7},{6,4},{7,5},{8,10},{9,11},{10,... | collective-permute-start | bytes 442376 | tf_op jit(solution)/shard_map/ppermute | solution.py:278
  46.1 7.2 %collective-permute-start.11 = (f32[72,128]{1,0:T(8,128)S(1)}, f32[72,128]{1,0:T(8,128)S(1)}, u32[]{:S(2)}, u32[]{:S(2)}) collective-permute-start(f32[72,128]{1,0:T(8,128)S(1)} %get-tuple-element.41), channel_id=1, source_target_pairs={{0,8},{8,16},{16,24},{24,0},{1,9},{9,17},{17,25},{25,1},{2,10},{10... | collective-permute-start | bytes 110600 | tf_op jit(solution)/shard_map/ppermute | solution.py:278
  47.5 5.8 %collective-permute-start.13 = (f32[72,128]{1,0:T(8,128)S(1)}, f32[72,128]{1,0:T(8,128)S(1)}, u32[]{:S(2)}, u32[]{:S(2)}) collective-permute-start(f32[72,128]{1,0:T(8,128)S(1)} %get-tuple-element.42), channel_id=1, source_target_pairs={{0,24},{8,0},{16,8},{24,16},{1,25},{9,1},{17,9},{25,17},{2,26},{10... | collective-permute-start | bytes 110600 | tf_op jit(solution)/shard_map/ppermute | solution.py:278
  49.0 4.6 %collective-permute-start.12 = (f32[72,128]{1,0:T(8,128)S(1)}, f32[72,128]{1,0:T(8,128)S(1)}, u32[]{:S(2)}, u32[]{:S(2)}) collective-permute-start(f32[72,128]{1,0:T(8,128)S(1)} %get-tuple-element.43), channel_id=1, source_target_pairs={{0,16},{8,24},{16,0},{24,8},{1,17},{9,25},{17,1},{25,9},{2,18},{10... | collective-permute-start | bytes 110600 | tf_op jit(solution)/shard_map/ppermute | solution.py:278
  50.5 4.1 %collective-permute-start.14 = (f32[72,128]{1,0:T(8,128)S(1)}, f32[72,128]{1,0:T(8,128)S(1)}, u32[]{:S(2)}, u32[]{:S(2)}) collective-permute-start(f32[72,128]{1,0:T(8,128)S(1)} %get-tuple-element.44), channel_id=1, source_target_pairs={{0,1},{1,2},{2,3},{3,0},{4,5},{5,6},{6,7},{7,4},{8,9},{9,10},{10,1... | collective-permute-start | bytes 110600 | tf_op jit(solution)/shard_map/ppermute | solution.py:278
  50.8 3.8 %collective-permute-start.16 = (f32[72,128]{1,0:T(8,128)S(1)}, f32[72,128]{1,0:T(8,128)S(1)}, u32[]{:S(2)}, u32[]{:S(2)}) collective-permute-start(f32[72,128]{1,0:T(8,128)S(1)} %get-tuple-element.45), channel_id=1, source_target_pairs={{0,3},{1,0},{2,1},{3,2},{4,7},{5,4},{6,5},{7,6},{8,11},{9,8},{10,9... | collective-permute-start | bytes 110600 | tf_op jit(solution)/shard_map/ppermute | solution.py:278
  53.3 4.6 %collective-permute-start.15 = (f32[72,128]{1,0:T(8,128)S(1)}, f32[72,128]{1,0:T(8,128)S(1)}, u32[]{:S(2)}, u32[]{:S(2)}) collective-permute-start(f32[72,128]{1,0:T(8,128)S(1)} %get-tuple-element.46), channel_id=1, source_target_pairs={{0,2},{1,3},{2,0},{3,1},{4,6},{5,7},{6,4},{7,5},{8,10},{9,11},{10,... | collective-permute-start | bytes 110600 | tf_op jit(solution)/shard_map/ppermute | solution.py:278
  58.0 3.5 %collective-permute-start.17 = (f32[2,72,128]{2,1,0:T(8,128)S(1)}, f32[2,72,128]{2,1,0:T(8,128)S(1)}, u32[]{:S(2)}, u32[]{:S(2)}) collective-permute-start(f32[2,72,128]{2,1,0:T(8,128)S(1)} %pad_maximum_fusion.2), channel_id=1, source_target_pairs={{0,32},{32,0},{64,96},{96,64},{128,160},{160,128},{192,224},{224,1... | collective-permute-start | bytes 221192 | tf_op jit(solution)/shard_map/ppermute | solution.py:315
  61.5 4.6 %collective-permute-start.18 = (f32[2,72,128]{2,1,0:T(8,128)S(1)}, f32[2,72,128]{2,1,0:T(8,128)S(1)}, u32[]{:S(2)}, u32[]{:S(2)}) collective-permute-start(f32[2,72,128]{2,1,0:T(8,128)S(1)} %fusion.13), channel_id=1, source_target_pairs={{0,64},{32,96},{64,0},{96,32},{128,192},{160,224},{192,128},{224,1... | collective-permute-start | bytes 221192 | tf_op jit(solution)/shard_map/ppermute | solution.py:315
  66.1 7.3 %collective-permute-start.19 = (f32[2,72,128]{2,1,0:T(8,128)S(1)}, f32[2,72,128]{2,1,0:T(8,128)S(1)}, u32[]{:S(2)}, u32[]{:S(2)}) collective-permute-start(f32[2,72,128]{2,1,0:T(8,128)S(1)} %fusion.15), channel_id=1, source_target_pairs={{0,128},{32,160},{64,192},{96,224},{128,0},{160,32},{192,64},{224,... | collective-permute-start | bytes 221192 | tf_op jit(solution)/shard_map/ppermute | solution.py:315
  73.4 5.3 %collective-permute-start.20 = (f32[2,72,128]{2,1,0:T(8,128)S(1)}, f32[2,72,128]{2,1,0:T(8,128)S(1)}, u32[]{:S(2)}, u32[]{:S(2)}) collective-permute-start(f32[2,72,128]{2,1,0:T(8,128)S(1)} %get-tuple-element.32), channel_id=1, source_target_pairs={{0,8},{8,16},{16,24},{24,0},{1,9},{9,17},{17,25},{25,1},{2,10},{10... | collective-permute-start | bytes 221192 | tf_op jit(solution)/shard_map/ppermute | solution.py:278
  73.8 4.9 %collective-permute-start.21 = (f32[2,72,128]{2,1,0:T(8,128)S(1)}, f32[2,72,128]{2,1,0:T(8,128)S(1)}, u32[]{:S(2)}, u32[]{:S(2)}) collective-permute-start(f32[2,72,128]{2,1,0:T(8,128)S(1)} %get-tuple-element.32), channel_id=1, source_target_pairs={{0,16},{8,24},{16,0},{24,8},{1,17},{9,25},{17,1},{25,9},{2,18},{10... | collective-permute-start | bytes 221192 | tf_op jit(solution)/shard_map/ppermute | solution.py:278
  75.6 4.0 %collective-permute-start.22 = (f32[2,72,128]{2,1,0:T(8,128)S(1)}, f32[2,72,128]{2,1,0:T(8,128)S(1)}, u32[]{:S(2)}, u32[]{:S(2)}) collective-permute-start(f32[2,72,128]{2,1,0:T(8,128)S(1)} %get-tuple-element.32), channel_id=1, source_target_pairs={{0,24},{8,0},{16,8},{24,16},{1,25},{9,1},{17,9},{25,17},{2,26},{10... | collective-permute-start | bytes 221192 | tf_op jit(solution)/shard_map/ppermute | solution.py:278
  79.6 9.7 %collective-permute-start.23 = (f32[4,2,72,128]{3,2,1,0:T(8,128)S(1)}, f32[4,2,72,128]{3,2,1,0:T(8,128)S(1)}, u32[]{:S(2)}, u32[]{:S(2)}) collective-permute-start(f32[4,2,72,128]{3,2,1,0:T(8,128)S(1)} %bitcast_dynamic-update-slice_fusion.4), channel_id=1, source_target_pairs={{0,1},{1,2},{2,3},{3,0},{4,5},{5,6},{6,7},{7,4},{8,9},{9,10},{10,1... | collective-permute-start | bytes 884744 | tf_op jit(solution)/shard_map/ppermute | solution.py:278
  79.7 11.7 %collective-permute-start.25 = (f32[4,2,72,128]{3,2,1,0:T(8,128)S(1)}, f32[4,2,72,128]{3,2,1,0:T(8,128)S(1)}, u32[]{:S(2)}, u32[]{:S(2)}) collective-permute-start(f32[4,2,72,128]{3,2,1,0:T(8,128)S(1)} %bitcast_dynamic-update-slice_fusion.4), channel_id=1, source_target_pairs={{0,3},{1,0},{2,1},{3,2},{4,7},{5,4},{6,5},{7,6},{8,11},{9,8},{10,9... | collective-permute-start | bytes 884744 | tf_op jit(solution)/shard_map/ppermute | solution.py:278
  82.3 9.0 %collective-permute-start.24 = (f32[4,2,72,128]{3,2,1,0:T(8,128)S(1)}, f32[4,2,72,128]{3,2,1,0:T(8,128)S(1)}, u32[]{:S(2)}, u32[]{:S(2)}) collective-permute-start(f32[4,2,72,128]{3,2,1,0:T(8,128)S(1)} %bitcast_dynamic-update-slice_fusion.4), channel_id=1, source_target_pairs={{0,2},{1,3},{2,0},{3,1},{4,6},{5,7},{6,4},{7,5},{8,10},{9,11},{10,... | collective-permute-start | bytes 884744 | tf_op jit(solution)/shard_map/ppermute | solution.py:278
  91.4 55.5 %copy-start.3 = (f32[1024,1024]{1,0:T(8,128)S(1)}, f32[1024,1024]{1,0:T(8,128)}, u32[]{:S(2)}) copy-start(f32[1024,1024]{1,0:T(8,128)} %t_ref.3) | copy-start | bytes 12582916
  91.4 23.0 %collective-permute-start.26 = (f32[18,128,128]{2,1,0:T(8,128)S(1)}, f32[18,128,128]{2,1,0:T(8,128)S(1)}, u32[]{:S(2)}, u32[]{:S(2)}) collective-permute-start(f32[18,128,128]{2,1,0:T(8,128)S(1)} %bitcast.80), channel_id=1, source_target_pairs={{0,4},{4,0},{1,5},{5,1},{2,6},{6,2},{3,7},{7,3},{8,12},{12,8},{9,1... | collective-permute-start | bytes 3538952 | tf_op jit(solution)/shard_map/ppermute | solution.py:273
  153.8 1.3 copy-start
  155.1 1.6 copy-start.1
Sparse Core Ops, SparseCore 0:
  46.2 86.0 all-gather.2

commit v4 on v2

--- a/solution.py
+++ b/solution.py
@@ -12,6 +12,11 @@
 NT = ((1,), (1,))
 TN = ((0,), (0,))
 MIB = 1024 * 1024
+Z = ("z_high", "z_low")
+
+
+def cost(flops, size):
+    return pl.CostEstimate(flops=flops, bytes_accessed=size, transcendentals=0)
 
 
 def dot(a, b, dims):
@@ -99,7 +104,7 @@
     return out
 
 
-def gram_kernel(n, core_ref, t_ref, mine_ref, other_ref, th_ref, tl_ref):
+def gram_kernel(n, core_ref, t_ref, mine_ref, other_ref, th_ref, tl_ref, halves_ref):
     core = core_ref[0]
     for j in range(n):
         at = slice(256 * j, 256 * j + 256)
@@ -116,17 +121,10 @@
             block = dot3((th_ref[of, :], tl_ref[of, :]), right, NN)
             for k, (p, row, column) in enumerate(list_of):
                 if p == place:
-                    part = block[row:row + 128, column:column + 128]
-                    at = k % half
-
-                    @pl.when(core == k // half)
-                    def _():
-                        mine_ref[at] = part
-
-                    @pl.when(core != k // half)
-                    def _():
-                        other_ref[at] = part
+                    halves_ref[core ^ (k // half), k % half] = block[row:row + 128, column:column + 128]
             place += 1
+    mine_ref[...] = halves_ref[0]
+    other_ref[...] = halves_ref[1]
 
 
 def gram(core, t, n):
@@ -138,8 +136,9 @@
         out_shape=(jax.ShapeDtypeStruct((half, 128, 128), jnp.float32),) * 2,
         in_specs=[pl.BlockSpec(memory_space=pltpu.SMEM), whole],
         out_specs=(whole,) * 2,
-        scratch_shapes=[pltpu.VMEM((features, m), jnp.bfloat16)] * 2,
+        scratch_shapes=[pltpu.VMEM((features, m), jnp.bfloat16)] * 2 + [pltpu.VMEM((2, half, 128, 128), jnp.float32)],
         compiler_params=pltpu.CompilerParams(vmem_limit_bytes=28 * MIB),
+        cost_estimate=cost(6 * m * features * features, 7 * MIB),
     )(core, t)
 
 
@@ -198,6 +197,7 @@
         out_specs=(whole,) * 2,
         scratch_shapes=[pltpu.VMEM((blocks, 256, 256), jnp.float32)],
         compiler_params=pltpu.CompilerParams(vmem_limit_bytes=20 * MIB),
+        cost_estimate=cost(32 * (256 * n) ** 3, 6 * MIB),
     )(core, mine, other)
 
 
@@ -229,39 +229,40 @@
         in_specs=[whole] * 3,
         out_specs=(whole,) * 2,
         compiler_params=pltpu.CompilerParams(vmem_limit_bytes=36 * MIB),
+        cost_estimate=cost(6 * m * features * features, 12 * MIB),
     )(t, l, d)
 
 
 def score_kernel(pick_ref, wh_ref, wl_ref, v_ref, out_ref):
     step = pl.program_id(0)
-    slots = v_ref.shape[0]
+    leads, groups = v_ref.shape[:2]
     rows = []
-    for s in range(slots):
-        pick = pick_ref[step * slots + s]
-        first = (pick == 0).astype(jnp.float32)
-        second = (pick == 1).astype(jnp.float32)
-        for y in range(v_ref.shape[1]):
-            rows.append(v_ref[s, y, 0] * first + v_ref[s, y, 1] * second)
+    for s in range(2 * leads):
+        pick = pick_ref[step * 2 * leads + s]
+        live = (pick >= 0).astype(jnp.float32)
+        for y in range(groups):
+            rows.append(v_ref[s % leads, y, jnp.maximum(pick, 0)] * live)
     v = split(jnp.concatenate(rows, axis=0))
     out_ref[...] = dot3((wh_ref[...], wl_ref[...]), v, NT)
 
 
-def score(pick, wh, wl, v, slots):
+def score(pick, wh, wl, v, leads):
     m, features = wh.shape
-    total, groups, blocks, part, _ = v.shape
-    width = slots * groups * part
+    total, groups, both, part, _ = v.shape
+    width = 2 * leads * groups * part
     whole = pl.BlockSpec(memory_space=pltpu.VMEM)
     return pl.pallas_call(
         score_kernel,
-        grid=(total // slots,),
-        out_shape=jax.ShapeDtypeStruct((m, total * groups * part), jnp.float32),
+        grid=(total // leads,),
+        out_shape=jax.ShapeDtypeStruct((m, total * 2 * groups * part), jnp.float32),
         in_specs=[
             pl.BlockSpec(memory_space=pltpu.SMEM),
             whole, whole,
-            pl.BlockSpec((slots, groups, blocks, part, features), lambda i: (i, 0, 0, 0, 0)),
+            pl.BlockSpec((leads, groups, both, part, features), lambda i: (i, 0, 0, 0, 0)),
         ],
         out_specs=pl.BlockSpec((m, width), lambda i: (0, i)),
-        compiler_params=pltpu.CompilerParams(vmem_limit_bytes=32 * MIB),
+        compiler_params=pltpu.CompilerParams(vmem_limit_bytes=44 * MIB),
+        cost_estimate=cost(12 * m * total * groups * part * features, 20 * MIB),
     )(pick, wh, wl, v)
 
 
@@ -274,11 +275,13 @@
     return lax.ppermute(v, axis, [(i, (i + k) % size) for i in range(size)])
 
 
-def scatter(v, axis, dim):
+def scatter(v, axis):
     size, me = lax.axis_size(axis), lax.axis_index(axis)
-    part = lambda k: lax.dynamic_index_in_dim(v, lax.rem(me + k, size), dim, keepdims=False)
-    came = [ring(part(k), axis, k) for k in range(1, size)]
-    return part(0), came
+    part = lambda k: lax.dynamic_index_in_dim(v, lax.rem(me + k, size), 0, keepdims=False)
+    total = part(0)
+    for k in range(1, size):
+        total = total + ring(part(k), axis, k)
+    return total
 
 
 def gather(v, axis):
@@ -290,54 +293,49 @@
     return out
 
 
-def add(parts):
-    total = parts[0]
-    for c in parts[1]:
-        total = total + c
-    return total
-
-
 def sum_all(mine, other, beside):
     shape = mine.shape
-    ny, nx, nz = lax.axis_size("y"), lax.axis_size("x"), lax.axis_size("z")
-    v = (mine + swap(other)).reshape(ny, nx, 2, -1, 128)
-    by_y, by_x = scatter(v[:, :, 0], "y", 0), scatter(v[:, :, 1], "x", 1)
-    left, right = add(by_y), add(by_x)
-    left, beside = lax.optimization_barrier((left, beside))
-    by_x, by_y = scatter(left, "x", 0), scatter(right, "y", 0)
-    s = jnp.stack([add(by_x), add(by_y)])
+    ny, nx, nz = lax.axis_size("y"), lax.axis_size("x"), lax.axis_size(Z)
+    v = (mine + swap(other)).reshape(ny, nx, -1, 128)
+    v, beside = lax.optimization_barrier((scatter(v, "y"), beside))
+    v = scatter(v, "x")
     hop = 1
     while hop < nz:
-        s = s + lax.ppermute(s, "z", [(i, i ^ hop) for i in range(nz)])
+        v = v + lax.ppermute(v, Z, [(i, i ^ hop) for i in range(nz)])
         hop *= 2
-    return gather(gather(s, "x"), "y").reshape(shape), beside
+    return gather(gather(v, "x"), "y").reshape(shape), beside
 
 
 def local(train_grads, val_grads, wanted, owner):
     m, features = train_grads.shape
     n = features // 256
-    dp = ("z", "x", "core")
+    dp = Z + ("x", "core")
     slabs, group = lax.axis_size(dp), lax.axis_size("y")
+    plane = slabs // lax.axis_size(Z)
     blocks, part, _ = val_grads.shape
-    val_all = lax.all_gather(val_grads, dp + ("y",), tiled=False)
-    val_all = val_all.reshape(slabs, group, blocks, part, features)
+
+    near = lax.ppermute(val_grads, "z_low", [(0, 1), (1, 0)])
+    held = jnp.concatenate([val_grads, near])
 
     positions = jnp.arange(slabs, dtype=jnp.int32)
     holder = jnp.sum(jnp.where(owner == lax.axis_index(dp), positions, 0))
     request = lax.dynamic_index_in_dim(wanted, holder, 0, keepdims=False)
-    pick = jnp.where(request >= 0, request - positions * blocks, -1)
+    apart = ((positions // plane) & 1) ^ lax.axis_index("z_low")
+    pick = jnp.where(request >= 0, apart * blocks + request - positions * blocks, -1)
 
     core = lax.axis_index("core").reshape(1)
     mine, other = gram(core, train_grads, n)
+    mine, other, held = lax.optimization_barrier((mine, other, held))
+    val_all = lax.all_gather(held, ("z_high", "x", "core", "y"), tiled=False)
+    val_all = val_all.reshape(slabs // 2, group, 2 * blocks, part, features)
     mine, pick = sum_all(mine, other, pick)
     l, d = factor(core, mine, swap(mine), n, 1.0 / (m * slabs * group))
     wh, wl = solve(train_grads, l, d, n)
-    return score(pick, wh, wl, val_all, 8)
+    return score(pick, wh, wl, val_all, plane)
 
 
 def solution(mesh):
-    axes = ("z", "x", "core", "y")
-    fine = Mesh(mesh.devices.reshape(8, 4, 2, 4), axes)
-    dp = P(("z", "x", "core"), "y", None)
-    in_specs = (P(axes, None), dp, P(), P())
+    axes = Z + ("x", "core", "y")
+    fine = Mesh(mesh.devices.reshape(4, 2, 4, 2, 4), axes)
+    in_specs = (P(axes, None), P(Z + ("x", "core"), "y", None), P(), P())
     return jax.shard_map(local, mesh=fine, in_specs=in_specs, out_specs=P(axes, None), check_vma=False)

time: 172 us -> 164 us (0.953)
  the two profiles are of different devices: /device:TPU:1 before, /device:TPU:35 now
where the time goes in v4:
time: 164 us
  Pallas kernels  61.4 us (37%)
  waiting for transfers between devices  41.3 us (25%)
  starting transfers between devices  38.2 us (23%)
  between operations  15.7 us (10%)
  local copies, waits for them, and re-layouts  5.43 us (3%)
  other arithmetic  2.32 us (1%)
    pallas_call x1, Pallas kernels, factor(): pl.pallas_call(functools.partial(factor_kernel, n, scale), out_shape=(jax...  32.5 us
    ppermute x12, waiting for transfers between devices, ring(): return lax.ppermute(v, axis, [(i, (i + k) % size) for i in range(size)])  22.4 us
    pallas_call x1, Pallas kernels, score(): pl.pallas_call(score_kernel, grid=(total // leads,), out_shape=jax.ShapeD...  17.5 us
    ppermute x12, starting transfers between devices, ring(): return lax.ppermute(v, axis, [(i, (i + k) % size) for i in range(size)])  15.9 us
    ppermute x2, starting transfers between devices, swap(): return lax.ppermute(v, 'core', [(0, 1), (1, 0)])  11.3 us
    ppermute x3, starting transfers between devices, sum_all(): v = v + lax.ppermute(v, Z, [(i, i ^ hop) for i in range(nz)])  10.9 us
    ppermute x3, waiting for transfers between devices, sum_all(): v = v + lax.ppermute(v, Z, [(i, i ^ hop) for i in range(nz)])  8.31 us
    pallas_call x1, Pallas kernels, solve(): pl.pallas_call(functools.partial(solve_kernel, n, features ** (-0.5)), ou...  6.77 us
  transfers between devices with their start and end apart: 19, of which 14 were waited for; matrix products, arithmetic and copies ran while one was open for 1% of the time, Pallas kernels for 27%

profile of v4, /device:TPU:35, one launch (start us, length us, event | category | flops | bytes accessed | tf_op | source)
XLA Modules:
  0.0 164.2 jit_solution(5099215722948239240)
XLA Ops:
  6.5 0.0 all-gather.3.cloned.1.call-start
  6.5 0.0 collective-permute-start
  6.5 0.0 copy-start
  6.5 2.2 %copy-done = f32[1024,1024]{1,0:T(8,128)S(1)} copy-done((f32[1024,1024]{1,0:T(8,128)S(1)}, f32[1024,1024]{1,0:T(8,128)}, u32[]{:S(2)}) %copy-start) | copy-done | bytes 4194328
  8.7 0.0 copy-start.4
  8.7 4.6 %shard_map.46 = (f32[18,128,128]{2,1,0:T(8,128)S(1)}, f32[18,128,128]{2,1,0:T(8,128)S(1)}) custom-call(s32[1]{0:T(128)} %bitcast.core_ref, f32[1024,1024]{1,0:T(8,128)S(1)} %copy-done), custom_call_target="tpu_custom_call" | custom-call | flops 6442450944 | bytes 7340032 | tf_op jit(solution)/shard_map/pallas_call | solution.py:134
  13.4 0.0 collective-permute-done
  13.4 0.0 copy-done.4
  13.4 0.7 pad_maximum_fusion
  14.0 0.0 all-gather.3.cloned.1.call-update
  14.1 0.9 collective-permute-start.1
  14.9 2.5 %collective-permute-done.1 = f32[18,128,128]{2,1,0:T(8,128)S(1)} collective-permute-done((f32[18,128,128]{2,1,0:T(8,128)S(1)}, f32[18,128,128]{2,1,0:T(8,128)S(1)}, u32[]{:S(2)}, u32[]{:S(2)}) %collective-permute-start.1) | collective-permute-done | bytes 1179680 | tf_op jit(solution)/shard_map/ppermute | solution.py:270
  17.4 0.1 add.129
  17.6 0.0 copy-start.5
  17.6 0.1 dynamic-slice_bitcast_fusion.2
  17.7 1.4 collective-permute-start.2
  19.0 1.5 collective-permute-start.4
  20.6 1.6 collective-permute-start.3
  22.1 0.0 copy-done.5
  22.1 0.7 fusion.9
  24.9 0.7 compare_select_fusion.pick_ref
  25.6 1.7 %collective-permute-done.2 = f32[4,144,128]{2,1,0:T(8,128)S(1)} collective-permute-done((f32[4,144,128]{2,1,0:T(8,128)S(1)}, f32[4,144,128]{2,1,0:T(8,128)S(1)}, u32[]{:S(2)}, u32[]{:S(2)}) %collective-permute-start.2) | collective-permute-done | bytes 294944 | tf_op jit(solution)/shard_map/ppermute | solution.py:275
  27.3 0.0 collective-permute-done.4
  27.3 7.4 %collective-permute-done.3 = f32[4,144,128]{2,1,0:T(8,128)S(1)} collective-permute-done((f32[4,144,128]{2,1,0:T(8,128)S(1)}, f32[4,144,128]{2,1,0:T(8,128)S(1)}, u32[]{:S(2)}, u32[]{:S(2)}) %collective-permute-start.3) | collective-permute-done | bytes 294944 | tf_op jit(solution)/shard_map/ppermute | solution.py:275
  34.7 0.1 fusion.1
  34.8 1.3 collective-permute-start.5
  36.1 0.3 collective-permute-start.7
  36.4 1.8 %collective-permute-start.6 = (f32[144,128]{1,0:T(8,128)S(1)}, f32[144,128]{1,0:T(8,128)S(1)}, u32[]{:S(2)}, u32[]{:S(2)}) collective-permute-start(f32[144,128]{1,0:T(8,128)S(1)} %get-tuple-element.34), channel_id=1, source_target_pairs={{0,16},{8,24},{16,0},{24,8},{1,17},{9,25},{17,1},{25,9},{2,18},{10... | collective-permute-start | bytes 221192 | tf_op jit(solution)/shard_map/ppermute | solution.py:275
  38.2 0.6 collective-permute-done.5
  38.8 1.2 collective-permute-done.7
  40.0 1.5 collective-permute-done.6
  41.5 1.9 %collective-permute-start.8 = (f32[144,128]{1,0:T(8,128)S(1)}, f32[144,128]{1,0:T(8,128)S(1)}, u32[]{:S(2)}, u32[]{:S(2)}) collective-permute-start(f32[144,128]{1,0:T(8,128)S(1)} %fusion.3), channel_id=1, source_target_pairs={{0,32},{32,0},{64,96},{96,64},{128,160},{160,128},{192,224},{224,1... | collective-permute-start | bytes 221192 | tf_op jit(solution)/shard_map/ppermute | solution.py:304
  43.4 2.4 %collective-permute-done.8 = f32[144,128]{1,0:T(8,128)S(1)} collective-permute-done((f32[144,128]{1,0:T(8,128)S(1)}, f32[144,128]{1,0:T(8,128)S(1)}, u32[]{:S(2)}, u32[]{:S(2)}) %collective-permute-start.8) | collective-permute-done | bytes 73760 | tf_op jit(solution)/shard_map/ppermute | solution.py:304
  45.7 2.8 %collective-permute-start.9 = (f32[144,128]{1,0:T(8,128)S(1)}, f32[144,128]{1,0:T(8,128)S(1)}, u32[]{:S(2)}, u32[]{:S(2)}) collective-permute-start(f32[144,128]{1,0:T(8,128)S(1)} %add.155), channel_id=1, source_target_pairs={{0,64},{32,96},{64,0},{96,32},{128,192},{160,224},{192,128},{224,1... | collective-permute-start | bytes 221192 | tf_op jit(solution)/shard_map/ppermute | solution.py:304
  48.6 1.8 %collective-permute-done.9 = f32[144,128]{1,0:T(8,128)S(1)} collective-permute-done((f32[144,128]{1,0:T(8,128)S(1)}, f32[144,128]{1,0:T(8,128)S(1)}, u32[]{:S(2)}, u32[]{:S(2)}) %collective-permute-start.9) | collective-permute-done | bytes 73760 | tf_op jit(solution)/shard_map/ppermute | solution.py:304
  50.4 6.2 %collective-permute-start.10 = (f32[144,128]{1,0:T(8,128)S(1)}, f32[144,128]{1,0:T(8,128)S(1)}, u32[]{:S(2)}, u32[]{:S(2)}) collective-permute-start(f32[144,128]{1,0:T(8,128)S(1)} %add.156), channel_id=1, source_target_pairs={{0,128},{32,160},{64,192},{96,224},{128,0},{160,32},{192,64},{224,... | collective-permute-start | bytes 221192 | tf_op jit(solution)/shard_map/ppermute | solution.py:304
  56.6 4.1 %collective-permute-done.10 = f32[144,128]{1,0:T(8,128)S(1)} collective-permute-done((f32[144,128]{1,0:T(8,128)S(1)}, f32[144,128]{1,0:T(8,128)S(1)}, u32[]{:S(2)}, u32[]{:S(2)}) %collective-permute-start.10) | collective-permute-done | bytes 73760 | tf_op jit(solution)/shard_map/ppermute | solution.py:304
  60.8 1.4 collective-permute-start.11
  62.2 0.9 collective-permute-start.12
  63.0 2.0 %collective-permute-start.13 = (f32[144,128]{1,0:T(8,128)S(1)}, f32[144,128]{1,0:T(8,128)S(1)}, u32[]{:S(2)}, u32[]{:S(2)}) collective-permute-start(f32[144,128]{1,0:T(8,128)S(1)} %get-tuple-element.28), channel_id=1, source_target_pairs={{0,24},{8,0},{16,8},{24,16},{1,25},{9,1},{17,9},{25,17},{2,26},{10... | collective-permute-start | bytes 221192 | tf_op jit(solution)/shard_map/ppermute | solution.py:275
  65.0 0.0 collective-permute-done.11
  65.0 2.5 %collective-permute-done.12 = f32[144,128]{1,0:T(8,128)S(1)} collective-permute-done((f32[144,128]{1,0:T(8,128)S(1)}, f32[144,128]{1,0:T(8,128)S(1)}, u32[]{:S(2)}, u32[]{:S(2)}) %collective-permute-start.12) | collective-permute-done | bytes 73760 | tf_op jit(solution)/shard_map/ppermute | solution.py:275
  67.5 0.0 collective-permute-done.13
  67.5 2.0 %collective-permute-start.14 = (f32[4,144,128]{2,1,0:T(8,128)S(1)}, f32[4,144,128]{2,1,0:T(8,128)S(1)}, u32[]{:S(2)}, u32[]{:S(2)}) collective-permute-start(f32[4,144,128]{2,1,0:T(8,128)S(1)} %bitcast_dynamic-update-slice_fusion.4), channel_id=1, source_target_pairs={{0,1},{1,2},{2,3},{3,0},{4,5},{5,6},{6,7},{7,4},{8,9},{9,10},{10,1... | collective-permute-start | bytes 884744 | tf_op jit(solution)/shard_map/ppermute | solution.py:275
  69.5 0.8 collective-permute-start.16
  70.3 1.1 collective-permute-start.15
  71.4 0.1 broadcast_in_dim.38
  71.5 4.2 %collective-permute-done.14 = f32[4,144,128]{2,1,0:T(8,128)S(1)} collective-permute-done((f32[4,144,128]{2,1,0:T(8,128)S(1)}, f32[4,144,128]{2,1,0:T(8,128)S(1)}, u32[]{:S(2)}, u32[]{:S(2)}) %collective-permute-start.14) | collective-permute-done | bytes 294944 | tf_op jit(solution)/shard_map/ppermute | solution.py:275
  75.7 3.3 %collective-permute-done.15 = f32[4,144,128]{2,1,0:T(8,128)S(1)} collective-permute-done((f32[4,144,128]{2,1,0:T(8,128)S(1)}, f32[4,144,128]{2,1,0:T(8,128)S(1)}, u32[]{:S(2)}, u32[]{:S(2)}) %collective-permute-start.15) | collective-permute-done | bytes 294944 | tf_op jit(solution)/shard_map/ppermute | solution.py:275
  79.1 0.0 collective-permute-done.16
  79.1 0.0 copy-start.1
  79.2 10.5 %collective-permute-start.17 = (f32[18,128,128]{2,1,0:T(8,128)S(1)}, f32[18,128,128]{2,1,0:T(8,128)S(1)}, u32[]{:S(2)}, u32[]{:S(2)}) collective-permute-start(f32[18,128,128]{2,1,0:T(8,128)S(1)} %bitcast.48), channel_id=1, source_target_pairs={{0,4},{4,0},{1,5},{5,1},{2,6},{6,2},{3,7},{7,3},{8,12},{12,8},{9,1... | collective-permute-start | bytes 3538952 | tf_op jit(solution)/shard_map/ppermute | solution.py:270
  89.6 2.5 %collective-permute-done.17.other_ref = f32[18,128,128]{2,1,0:T(8,128)S(1)} collective-permute-done((f32[18,128,128]{2,1,0:T(8,128)S(1)}, f32[18,128,128]{2,1,0:T(8,128)S(1)}, u32[]{:S(2)}, u32[]{:S(2)}) %collective-permute-start.17) | collective-permute-done | bytes 1179680 | tf_op jit(solution)/shard_map/ppermute | solution.py:270
  92.1 32.5 %shard_map.47 = (f32[10,256,256]{2,1,0:T(8,128)S(1)}, f32[4,256,256]{2,1,0:T(8,128)S(1)}) custom-call(s32[1]{0:T(128)} %bitcast.core_ref, f32[18,128,128]{2,1,0:T(8,128)S(1)} %bitcast.49, f32[18,128,128]{2,1,0:T(8,128)S(1)} %collective-permute-done.17.other_ref), custom_call_target="tpu_custom_call" | custom-call | flops 34359738368 | bytes 6291456 | tf_op jit(solution)/shard_map/pallas_call | solution.py:190
  124.6 0.0 copy-done.1
  124.6 6.8 %shard_map.48 = (bf16[1024,1024]{1,0:T(8,128)(2,1)S(1)}, bf16[1024,1024]{1,0:T(8,128)(2,1)S(1)}) custom-call(f32[1024,1024]{1,0:T(8,128)S(1)} %copy-done.1, f32[10,256,256]{2,1,0:T(8,128)S(1)} %get-tuple-element.22.l_ref, f32[4,256,256]{2,1,0:T(8,128)S(1)} %get-tuple-element.23.d_ref), custom_call_target="tpu_custom_call" | custom-call | flops 6442450944 | bytes 12582912 | tf_op jit(solution)/shard_map/pallas_call | solution.py:226
  131.4 0.0 copy-start.2
  131.4 1.3 copy-done.2
  132.7 5.6 %all-gather.3.cloned.1.call-done = f32[512,8,1024]{2,1,0:T(8,128)} async-done(((f32[4,8,1024]{2,1,0:T(8,128)}), f32[512,8,1024]{2,1,0:T(8,128)}) %all-gather.3.cloned.1.call-update) | async-done | bytes 16777232 | tf_op jit(solution)/shard_map/all_gather | solution.py:329
  138.3 0.0 copy-start.3
  138.3 1.6 copy-done.3
  139.9 17.5 %shard_map.49 = f32[1024,2048]{1,0:T(8,128)} custom-call(s32[64]{0:T(128)S(1)} %compare_select_fusion.pick_ref, bf16[1024,1024]{1,0:T(8,128)(2,1)S(1)} %get-tuple-element.24.wh_ref, bf16[1024,1024]{1,0:T(8,128)(2,1)S(1)} %copy-done.3, f32[32,4,4,8,1024]{4,3,2,1,0:T(8,128)} %bitcast.52), custom_call_target="tpu_custom_call" | custom-call | flops 12884901888 | bytes 20971520 | tf_op jit(solution)/shard_map/pallas_call | solution.py:254
  (13 shorter events, 0.2 us)
Async XLA Ops:
  6.5 131.8 %all-gather.3.cloned.1.call-start = ((), (), s32[]{:S(2)}) async-start(), calls=%async_computation | async-start | bytes 16908288 | tf_op jit(solution)/shard_map/all_gather | solution.py:329
  6.5 6.8 %collective-permute-start = (f32[2,8,1024]{2,1,0:T(8,128)}, f32[2,8,1024]{2,1,0:T(8,128)S(1)}, u32[]{:S(2)}, u32[]{:S(2)}) collective-permute-start(f32[2,8,1024]{2,1,0:T(8,128)} %param.5), channel_id=1, source_target_pairs={{0,32},{32,0},{1,33},{33,1},{2,34},{34,2},{3,35},{35,3},{4,36},{36... | collective-permute-start | bytes 196616 | tf_op jit(solution)/shard_map/ppermute | solution.py:317
  6.5 2.2 %copy-start = (f32[1024,1024]{1,0:T(8,128)S(1)}, f32[1024,1024]{1,0:T(8,128)}, u32[]{:S(2)}) copy-start(f32[1024,1024]{1,0:T(8,128)} %t_ref.3) | copy-start | bytes 12582916
  8.7 4.6 %copy-start.4 = (f32[2,8,1024]{2,1,0:T(8,128)S(1)}, f32[2,8,1024]{2,1,0:T(8,128)}, u32[]{:S(2)}) copy-start(f32[2,8,1024]{2,1,0:T(8,128)} %param.5) | copy-start | bytes 196612
  14.1 3.3 %collective-permute-start.1 = (f32[18,128,128]{2,1,0:T(8,128)S(1)}, f32[18,128,128]{2,1,0:T(8,128)S(1)}, u32[]{:S(2)}, u32[]{:S(2)}) collective-permute-start(f32[18,128,128]{2,1,0:T(8,128)S(1)} %get-tuple-element.19), channel_id=1, source_target_pairs={{0,4},{4,0},{1,5},{5,1},{2,6},{6,2},{3,7},{7,3},{8,12},{12,8},{9,1... | collective-permute-start | bytes 3538952 | tf_op jit(solution)/shard_map/ppermute | solution.py:270
  17.6 4.6 %copy-start.5 = (s32[64]{0:T(128)S(1)}, s32[64]{0:T(128)}, u32[]{:S(2)}) copy-start(s32[64]{0:T(128)} %param.7) | copy-start | bytes 772
  17.7 9.6 %collective-permute-start.2 = (f32[4,144,128]{2,1,0:T(8,128)S(1)}, f32[4,144,128]{2,1,0:T(8,128)S(1)}, u32[]{:S(2)}, u32[]{:S(2)}) collective-permute-start(f32[4,144,128]{2,1,0:T(8,128)S(1)} %get-tuple-element.29), channel_id=1, source_target_pairs={{0,1},{1,2},{2,3},{3,0},{4,5},{5,6},{6,7},{7,4},{8,9},{9,10},{10,1... | collective-permute-start | bytes 884744 | tf_op jit(solution)/shard_map/ppermute | solution.py:275
  19.0 8.3 %collective-permute-start.4 = (f32[4,144,128]{2,1,0:T(8,128)S(1)}, f32[4,144,128]{2,1,0:T(8,128)S(1)}, u32[]{:S(2)}, u32[]{:S(2)}) collective-permute-start(f32[4,144,128]{2,1,0:T(8,128)S(1)} %get-tuple-element.30), channel_id=1, source_target_pairs={{0,3},{1,0},{2,1},{3,2},{4,7},{5,4},{6,5},{7,6},{8,11},{9,8},{10,9... | collective-permute-start | bytes 884744 | tf_op jit(solution)/shard_map/ppermute | solution.py:275
  20.6 14.2 %collective-permute-start.3 = (f32[4,144,128]{2,1,0:T(8,128)S(1)}, f32[4,144,128]{2,1,0:T(8,128)S(1)}, u32[]{:S(2)}, u32[]{:S(2)}) collective-permute-start(f32[4,144,128]{2,1,0:T(8,128)S(1)} %get-tuple-element.31), channel_id=1, source_target_pairs={{0,2},{1,3},{2,0},{3,1},{4,6},{5,7},{6,4},{7,5},{8,10},{9,11},{10,... | collective-permute-start | bytes 884744 | tf_op jit(solution)/shard_map/ppermute | solution.py:275
  34.8 4.0 %collective-permute-start.5 = (f32[144,128]{1,0:T(8,128)S(1)}, f32[144,128]{1,0:T(8,128)S(1)}, u32[]{:S(2)}, u32[]{:S(2)}) collective-permute-start(f32[144,128]{1,0:T(8,128)S(1)} %get-tuple-element.32), channel_id=1, source_target_pairs={{0,8},{8,16},{16,24},{24,0},{1,9},{9,17},{17,25},{25,1},{2,10},{10... | collective-permute-start | bytes 221192 | tf_op jit(solution)/shard_map/ppermute | solution.py:275
  36.1 3.9 %collective-permute-start.7 = (f32[144,128]{1,0:T(8,128)S(1)}, f32[144,128]{1,0:T(8,128)S(1)}, u32[]{:S(2)}, u32[]{:S(2)}) collective-permute-start(f32[144,128]{1,0:T(8,128)S(1)} %get-tuple-element.33), channel_id=1, source_target_pairs={{0,24},{8,0},{16,8},{24,16},{1,25},{9,1},{17,9},{25,17},{2,26},{10... | collective-permute-start | bytes 221192 | tf_op jit(solution)/shard_map/ppermute | solution.py:275
  36.4 5.1 %collective-permute-start.6 = (f32[144,128]{1,0:T(8,128)S(1)}, f32[144,128]{1,0:T(8,128)S(1)}, u32[]{:S(2)}, u32[]{:S(2)}) collective-permute-start(f32[144,128]{1,0:T(8,128)S(1)} %get-tuple-element.34), channel_id=1, source_target_pairs={{0,16},{8,24},{16,0},{24,8},{1,17},{9,25},{17,1},{25,9},{2,18},{10... | collective-permute-start | bytes 221192 | tf_op jit(solution)/shard_map/ppermute | solution.py:275
  41.5 4.2 %collective-permute-start.8 = (f32[144,128]{1,0:T(8,128)S(1)}, f32[144,128]{1,0:T(8,128)S(1)}, u32[]{:S(2)}, u32[]{:S(2)}) collective-permute-start(f32[144,128]{1,0:T(8,128)S(1)} %fusion.3), channel_id=1, source_target_pairs={{0,32},{32,0},{64,96},{96,64},{128,160},{160,128},{192,224},{224,1... | collective-permute-start | bytes 221192 | tf_op jit(solution)/shard_map/ppermute | solution.py:304
  45.7 4.6 %collective-permute-start.9 = (f32[144,128]{1,0:T(8,128)S(1)}, f32[144,128]{1,0:T(8,128)S(1)}, u32[]{:S(2)}, u32[]{:S(2)}) collective-permute-start(f32[144,128]{1,0:T(8,128)S(1)} %add.155), channel_id=1, source_target_pairs={{0,64},{32,96},{64,0},{96,32},{128,192},{160,224},{192,128},{224,1... | collective-permute-start | bytes 221192 | tf_op jit(solution)/shard_map/ppermute | solution.py:304
  50.4 10.4 %collective-permute-start.10 = (f32[144,128]{1,0:T(8,128)S(1)}, f32[144,128]{1,0:T(8,128)S(1)}, u32[]{:S(2)}, u32[]{:S(2)}) collective-permute-start(f32[144,128]{1,0:T(8,128)S(1)} %add.156), channel_id=1, source_target_pairs={{0,128},{32,160},{64,192},{96,224},{128,0},{160,32},{192,64},{224,... | collective-permute-start | bytes 221192 | tf_op jit(solution)/shard_map/ppermute | solution.py:304
  60.8 4.2 %collective-permute-start.11 = (f32[144,128]{1,0:T(8,128)S(1)}, f32[144,128]{1,0:T(8,128)S(1)}, u32[]{:S(2)}, u32[]{:S(2)}) collective-permute-start(f32[144,128]{1,0:T(8,128)S(1)} %get-tuple-element.28), channel_id=1, source_target_pairs={{0,8},{8,16},{16,24},{24,0},{1,9},{9,17},{17,25},{25,1},{2,10},{10... | collective-permute-start | bytes 221192 | tf_op jit(solution)/shard_map/ppermute | solution.py:275
  62.2 5.3 %collective-permute-start.12 = (f32[144,128]{1,0:T(8,128)S(1)}, f32[144,128]{1,0:T(8,128)S(1)}, u32[]{:S(2)}, u32[]{:S(2)}) collective-permute-start(f32[144,128]{1,0:T(8,128)S(1)} %get-tuple-element.28), channel_id=1, source_target_pairs={{0,16},{8,24},{16,0},{24,8},{1,17},{9,25},{17,1},{25,9},{2,18},{10... | collective-permute-start | bytes 221192 | tf_op jit(solution)/shard_map/ppermute | solution.py:275
  63.0 4.5 %collective-permute-start.13 = (f32[144,128]{1,0:T(8,128)S(1)}, f32[144,128]{1,0:T(8,128)S(1)}, u32[]{:S(2)}, u32[]{:S(2)}) collective-permute-start(f32[144,128]{1,0:T(8,128)S(1)} %get-tuple-element.28), channel_id=1, source_target_pairs={{0,24},{8,0},{16,8},{24,16},{1,25},{9,1},{17,9},{25,17},{2,26},{10... | collective-permute-start | bytes 221192 | tf_op jit(solution)/shard_map/ppermute | solution.py:275
  67.5 8.2 %collective-permute-start.14 = (f32[4,144,128]{2,1,0:T(8,128)S(1)}, f32[4,144,128]{2,1,0:T(8,128)S(1)}, u32[]{:S(2)}, u32[]{:S(2)}) collective-permute-start(f32[4,144,128]{2,1,0:T(8,128)S(1)} %bitcast_dynamic-update-slice_fusion.4), channel_id=1, source_target_pairs={{0,1},{1,2},{2,3},{3,0},{4,5},{5,6},{6,7},{7,4},{8,9},{9,10},{10,1... | collective-permute-start | bytes 884744 | tf_op jit(solution)/shard_map/ppermute | solution.py:275
  69.5 9.6 %collective-permute-start.16 = (f32[4,144,128]{2,1,0:T(8,128)S(1)}, f32[4,144,128]{2,1,0:T(8,128)S(1)}, u32[]{:S(2)}, u32[]{:S(2)}) collective-permute-start(f32[4,144,128]{2,1,0:T(8,128)S(1)} %bitcast_dynamic-update-slice_fusion.4), channel_id=1, source_target_pairs={{0,3},{1,0},{2,1},{3,2},{4,7},{5,4},{6,5},{7,6},{8,11},{9,8},{10,9... | collective-permute-start | bytes 884744 | tf_op jit(solution)/shard_map/ppermute | solution.py:275
  70.3 8.8 %collective-permute-start.15 = (f32[4,144,128]{2,1,0:T(8,128)S(1)}, f32[4,144,128]{2,1,0:T(8,128)S(1)}, u32[]{:S(2)}, u32[]{:S(2)}) collective-permute-start(f32[4,144,128]{2,1,0:T(8,128)S(1)} %bitcast_dynamic-update-slice_fusion.4), channel_id=1, source_target_pairs={{0,2},{1,3},{2,0},{3,1},{4,6},{5,7},{6,4},{7,5},{8,10},{9,11},{10,... | collective-permute-start | bytes 884744 | tf_op jit(solution)/shard_map/ppermute | solution.py:275
  79.1 45.4 %copy-start.1 = (f32[1024,1024]{1,0:T(8,128)S(1)}, f32[1024,1024]{1,0:T(8,128)}, u32[]{:S(2)}) copy-start(f32[1024,1024]{1,0:T(8,128)} %t_ref.3) | copy-start | bytes 12582916
  79.2 12.9 %collective-permute-start.17 = (f32[18,128,128]{2,1,0:T(8,128)S(1)}, f32[18,128,128]{2,1,0:T(8,128)S(1)}, u32[]{:S(2)}, u32[]{:S(2)}) collective-permute-start(f32[18,128,128]{2,1,0:T(8,128)S(1)} %bitcast.48), channel_id=1, source_target_pairs={{0,4},{4,0},{1,5},{5,1},{2,6},{6,2},{3,7},{7,3},{8,12},{12,8},{9,1... | collective-permute-start | bytes 3538952 | tf_op jit(solution)/shard_map/ppermute | solution.py:270
  131.4 1.3 copy-start.2
  138.3 1.6 copy-start.3
Sparse Core Ops, SparseCore 0:
  14.2 124.0 all-gather.2

commit v5 on v4

--- a/solution.py
+++ b/solution.py
@@ -261,7 +261,7 @@
             pl.BlockSpec((leads, groups, both, part, features), lambda i: (i, 0, 0, 0, 0)),
         ],
         out_specs=pl.BlockSpec((m, width), lambda i: (0, i)),
-        compiler_params=pltpu.CompilerParams(vmem_limit_bytes=44 * MIB),
+        compiler_params=pltpu.CompilerParams(vmem_limit_bytes=36 * MIB),
         cost_estimate=cost(12 * m * total * groups * part * features, 20 * MIB),
     )(pick, wh, wl, v)
 
@@ -299,10 +299,9 @@
     v = (mine + swap(other)).reshape(ny, nx, -1, 128)
     v, beside = lax.optimization_barrier((scatter(v, "y"), beside))
     v = scatter(v, "x")
-    hop = 1
-    while hop < nz:
-        v = v + lax.ppermute(v, Z, [(i, i ^ hop) for i in range(nz)])
-        hop *= 2
+    across = lambda hop: lax.ppermute(v, Z, [(i, i ^ hop) for i in range(nz)])
+    v = (v + across(nz // 2)) + (across(2) + across(nz - 2)) if nz == 8 else lax.psum(v, "z_high")
+    v = v + across(1)
     return gather(gather(v, "x"), "y").reshape(shape), beside
 
 
@@ -324,8 +323,8 @@
     pick = jnp.where(request >= 0, apart * blocks + request - positions * blocks, -1)
 
     core = lax.axis_index("core").reshape(1)
+    held, core = lax.optimization_barrier((held, core))
     mine, other = gram(core, train_grads, n)
-    mine, other, held = lax.optimization_barrier((mine, other, held))
     val_all = lax.all_gather(held, ("z_high", "x", "core", "y"), tiled=False)
     val_all = val_all.reshape(slabs // 2, group, 2 * blocks, part, features)
     mine, pick = sum_all(mine, other, pick)

time: 164 us -> 184 us (1.12)
  the two profiles are of different devices: /device:TPU:35 before, /device:TPU:1 now
where the time goes in v5:
time: 184 us; the launch traced here: 183 us
  waiting for transfers between devices  63.2 us (34%)
  Pallas kernels  61.4 us (33%)
  starting transfers between devices  34 us (18%)
  between operations  15.7 us (9%)
  local copies, waits for them, and re-layouts  5.42 us (3%)
  other arithmetic  3.16 us (2%)
    ppermute x12, waiting for transfers between devices, ring(): return lax.ppermute(v, axis, [(i, (i + k) % size) for i in range(size)])  38.3 us
    pallas_call x1, Pallas kernels, factor(): pl.pallas_call(functools.partial(factor_kernel, n, scale), out_shape=(jax...  32.5 us
    ppermute x4, waiting for transfers between devices, sum_all(): across = lambda hop: lax.ppermute(v, Z, [(i, i ^ hop) for i in range(nz)])  18.1 us
    pallas_call x1, Pallas kernels, score(): pl.pallas_call(score_kernel, grid=(total // leads,), out_shape=jax.ShapeD...  17.5 us
    ppermute x12, starting transfers between devices, ring(): return lax.ppermute(v, axis, [(i, (i + k) % size) for i in range(size)])  14.1 us
    ppermute x2, starting transfers between devices, swap(): return lax.ppermute(v, 'core', [(0, 1), (1, 0)])  8.76 us
    ppermute x4, starting transfers between devices, sum_all(): across = lambda hop: lax.ppermute(v, Z, [(i, i ^ hop) for i in range(nz)])  8.73 us
    pallas_call x1, Pallas kernels, solve(): pl.pallas_call(functools.partial(solve_kernel, n, features ** (-0.5)), ou...  6.77 us
  transfers between devices with their start and end apart: 20, of which 17 were waited for; matrix products, arithmetic and copies ran while one was open for 1% of the time, Pallas kernels for 24%

profile of v5, /device:TPU:1, one launch (start us, length us, event | category | flops | bytes accessed | tf_op | source)
XLA Modules:
  0.0 182.8 jit_solution(14527703405844574516)
XLA Ops:
  6.5 0.0 all-gather.3.cloned.1.call-start
  6.5 2.5 %collective-permute-start = (f32[2,8,1024]{2,1,0:T(8,128)}, f32[2,8,1024]{2,1,0:T(8,128)S(1)}, u32[]{:S(2)}, u32[]{:S(2)}) collective-permute-start(f32[2,8,1024]{2,1,0:T(8,128)} %param.5), channel_id=1, source_target_pairs={{0,32},{32,0},{1,33},{33,1},{2,34},{34,2},{3,35},{35,3},{4,36},{36... | collective-permute-start | bytes 196616 | tf_op jit(solution)/shard_map/ppermute | solution.py:316
  9.0 1.9 %collective-permute-done = f32[2,8,1024]{2,1,0:T(8,128)S(1)} collective-permute-done((f32[2,8,1024]{2,1,0:T(8,128)}, f32[2,8,1024]{2,1,0:T(8,128)S(1)}, u32[]{:S(2)}, u32[]{:S(2)}) %collective-permute-start) | collective-permute-done | bytes 65568 | tf_op jit(solution)/shard_map/ppermute | solution.py:316
  10.9 1.5 pad_maximum_fusion
  12.4 0.0 all-gather.3.cloned.1.call-update
  12.4 0.0 copy-start
  12.4 2.2 %copy-done = f32[1024,1024]{1,0:T(8,128)S(1)} copy-done((f32[1024,1024]{1,0:T(8,128)S(1)}, f32[1024,1024]{1,0:T(8,128)}, u32[]{:S(2)}) %copy-start) | copy-done | bytes 4194328
  14.6 4.6 %shard_map.46 = (f32[18,128,128]{2,1,0:T(8,128)S(1)}, f32[18,128,128]{2,1,0:T(8,128)S(1)}) custom-call(s32[1]{0:T(128)} %bitcast.core_ref, f32[1024,1024]{1,0:T(8,128)S(1)} %copy-done), custom_call_target="tpu_custom_call" | custom-call | flops 6442450944 | bytes 7340032 | tf_op jit(solution)/shard_map/pallas_call | solution.py:134
  19.2 3.5 %collective-permute-start.1 = (f32[18,128,128]{2,1,0:T(8,128)S(1)}, f32[18,128,128]{2,1,0:T(8,128)S(1)}, u32[]{:S(2)}, u32[]{:S(2)}) collective-permute-start(f32[18,128,128]{2,1,0:T(8,128)S(1)} %get-tuple-element.17), channel_id=1, source_target_pairs={{0,4},{4,0},{1,5},{5,1},{2,6},{6,2},{3,7},{7,3},{8,12},{12,8},{9,1... | collective-permute-start | bytes 3538952 | tf_op jit(solution)/shard_map/ppermute | solution.py:270
  22.7 2.5 %collective-permute-done.1 = f32[18,128,128]{2,1,0:T(8,128)S(1)} collective-permute-done((f32[18,128,128]{2,1,0:T(8,128)S(1)}, f32[18,128,128]{2,1,0:T(8,128)S(1)}, u32[]{:S(2)}, u32[]{:S(2)}) %collective-permute-start.1) | collective-permute-done | bytes 1179680 | tf_op jit(solution)/shard_map/ppermute | solution.py:270
  25.2 0.1 add.132
  25.3 0.0 copy-start.4
  25.3 0.1 dynamic-slice_bitcast_fusion.2
  25.4 0.1 collective-permute-start.2
  25.5 2.7 %collective-permute-start.4 = (f32[4,144,128]{2,1,0:T(8,128)S(1)}, f32[4,144,128]{2,1,0:T(8,128)S(1)}, u32[]{:S(2)}, u32[]{:S(2)}) collective-permute-start(f32[4,144,128]{2,1,0:T(8,128)S(1)} %get-tuple-element.28), channel_id=1, source_target_pairs={{0,3},{1,0},{2,1},{3,2},{4,7},{5,4},{6,5},{7,6},{8,11},{9,8},{10,9... | collective-permute-start | bytes 884744 | tf_op jit(solution)/shard_map/ppermute | solution.py:275
  28.2 0.0 collective-permute-start.3
  28.2 0.0 copy-done.4
  28.2 0.7 fusion.9
  30.9 0.7 compare_select_fusion.pick_ref
  31.6 4.3 %collective-permute-done.2 = f32[4,144,128]{2,1,0:T(8,128)S(1)} collective-permute-done((f32[4,144,128]{2,1,0:T(8,128)S(1)}, f32[4,144,128]{2,1,0:T(8,128)S(1)}, u32[]{:S(2)}, u32[]{:S(2)}) %collective-permute-start.2) | collective-permute-done | bytes 294944 | tf_op jit(solution)/shard_map/ppermute | solution.py:275
  36.0 0.0 collective-permute-done.4
  36.0 5.8 %collective-permute-done.3 = f32[4,144,128]{2,1,0:T(8,128)S(1)} collective-permute-done((f32[4,144,128]{2,1,0:T(8,128)S(1)}, f32[4,144,128]{2,1,0:T(8,128)S(1)}, u32[]{:S(2)}, u32[]{:S(2)}) %collective-permute-start.3) | collective-permute-done | bytes 294944 | tf_op jit(solution)/shard_map/ppermute | solution.py:275
  41.8 0.1 fusion.1
  41.9 1.2 collective-permute-start.5
  43.1 1.6 collective-permute-start.7
  44.6 1.5 collective-permute-start.6
  46.1 0.3 collective-permute-done.5
  46.4 0.3 collective-permute-done.7
  46.7 3.1 %collective-permute-done.6 = f32[144,128]{1,0:T(8,128)S(1)} collective-permute-done((f32[144,128]{1,0:T(8,128)S(1)}, f32[144,128]{1,0:T(8,128)S(1)}, u32[]{:S(2)}, u32[]{:S(2)}) %collective-permute-start.6) | collective-permute-done | bytes 73760 | tf_op jit(solution)/shard_map/ppermute | solution.py:275
  49.9 6.5 %collective-permute-start.10 = (f32[144,128]{1,0:T(8,128)S(1)}, f32[144,128]{1,0:T(8,128)S(1)}, u32[]{:S(2)}, u32[]{:S(2)}) collective-permute-start(f32[144,128]{1,0:T(8,128)S(1)} %fusion.3), channel_id=1, source_target_pairs={{0,192},{32,224},{64,128},{96,160},{128,64},{160,96},{192,0},{224,... | collective-permute-start | bytes 221192 | tf_op jit(solution)/shard_map/ppermute | solution.py:302
  56.3 1.2 collective-permute-start.9
  57.5 0.9 collective-permute-start.8
  58.5 2.6 %collective-permute-done.10 = f32[144,128]{1,0:T(8,128)S(1)} collective-permute-done((f32[144,128]{1,0:T(8,128)S(1)}, f32[144,128]{1,0:T(8,128)S(1)}, u32[]{:S(2)}, u32[]{:S(2)}) %collective-permute-start.10) | collective-permute-done | bytes 73760 | tf_op jit(solution)/shard_map/ppermute | solution.py:302
  61.1 5.7 %collective-permute-done.9 = f32[144,128]{1,0:T(8,128)S(1)} collective-permute-done((f32[144,128]{1,0:T(8,128)S(1)}, f32[144,128]{1,0:T(8,128)S(1)}, u32[]{:S(2)}, u32[]{:S(2)}) %collective-permute-start.9) | collective-permute-done | bytes 73760 | tf_op jit(solution)/shard_map/ppermute | solution.py:302
  66.8 2.5 %collective-permute-done.8 = f32[144,128]{1,0:T(8,128)S(1)} collective-permute-done((f32[144,128]{1,0:T(8,128)S(1)}, f32[144,128]{1,0:T(8,128)S(1)}, u32[]{:S(2)}, u32[]{:S(2)}) %collective-permute-start.8) | collective-permute-done | bytes 73760 | tf_op jit(solution)/shard_map/ppermute | solution.py:302
  69.3 0.1 collective-permute-start.11
  69.4 7.3 %collective-permute-done.11 = f32[144,128]{1,0:T(8,128)S(1)} collective-permute-done((f32[144,128]{1,0:T(8,128)S(1)}, f32[144,128]{1,0:T(8,128)S(1)}, u32[]{:S(2)}, u32[]{:S(2)}) %collective-permute-start.11) | collective-permute-done | bytes 73760 | tf_op jit(solution)/shard_map/ppermute | solution.py:302
  76.7 0.3 collective-permute-start.12
  77.0 4.0 %collective-permute-start.13 = (f32[144,128]{1,0:T(8,128)S(1)}, f32[144,128]{1,0:T(8,128)S(1)}, u32[]{:S(2)}, u32[]{:S(2)}) collective-permute-start(f32[144,128]{1,0:T(8,128)S(1)} %get-tuple-element.26), channel_id=1, source_target_pairs={{0,16},{8,24},{16,0},{24,8},{1,17},{9,25},{17,1},{25,9},{2,18},{10... | collective-permute-start | bytes 221192 | tf_op jit(solution)/shard_map/ppermute | solution.py:275
  81.0 0.0 collective-permute-start.14
  81.0 0.6 collective-permute-done.12
  81.6 2.3 %collective-permute-done.13 = f32[144,128]{1,0:T(8,128)S(1)} collective-permute-done((f32[144,128]{1,0:T(8,128)S(1)}, f32[144,128]{1,0:T(8,128)S(1)}, u32[]{:S(2)}, u32[]{:S(2)}) %collective-permute-start.13) | collective-permute-done | bytes 73760 | tf_op jit(solution)/shard_map/ppermute | solution.py:275
  83.8 1.1 collective-permute-done.14
  85.0 0.9 collective-permute-start.15
  85.9 1.8 %collective-permute-start.17 = (f32[4,144,128]{2,1,0:T(8,128)S(1)}, f32[4,144,128]{2,1,0:T(8,128)S(1)}, u32[]{:S(2)}, u32[]{:S(2)}) collective-permute-start(f32[4,144,128]{2,1,0:T(8,128)S(1)} %bitcast_dynamic-update-slice_fusion.4), channel_id=1, source_target_pairs={{0,3},{1,0},{2,1},{3,2},{4,7},{5,4},{6,5},{7,6},{8,11},{9,8},{10,9... | collective-permute-start | bytes 884744 | tf_op jit(solution)/shard_map/ppermute | solution.py:275
  87.7 0.0 collective-permute-start.16
  87.8 0.1 broadcast_in_dim.38
  87.9 10.1 %collective-permute-done.15 = f32[4,144,128]{2,1,0:T(8,128)S(1)} collective-permute-done((f32[4,144,128]{2,1,0:T(8,128)S(1)}, f32[4,144,128]{2,1,0:T(8,128)S(1)}, u32[]{:S(2)}, u32[]{:S(2)}) %collective-permute-start.15) | collective-permute-done | bytes 294944 | tf_op jit(solution)/shard_map/ppermute | solution.py:275
  98.0 10.4 %collective-permute-done.16 = f32[4,144,128]{2,1,0:T(8,128)S(1)} collective-permute-done((f32[4,144,128]{2,1,0:T(8,128)S(1)}, f32[4,144,128]{2,1,0:T(8,128)S(1)}, u32[]{:S(2)}, u32[]{:S(2)}) %collective-permute-start.16) | collective-permute-done | bytes 294944 | tf_op jit(solution)/shard_map/ppermute | solution.py:275
  108.4 0.0 collective-permute-done.17
  108.5 0.0 copy-start.1
  108.5 5.3 %collective-permute-start.18 = (f32[18,128,128]{2,1,0:T(8,128)S(1)}, f32[18,128,128]{2,1,0:T(8,128)S(1)}, u32[]{:S(2)}, u32[]{:S(2)}) collective-permute-start(f32[18,128,128]{2,1,0:T(8,128)S(1)} %bitcast.48), channel_id=1, source_target_pairs={{0,4},{4,0},{1,5},{5,1},{2,6},{6,2},{3,7},{7,3},{8,12},{12,8},{9,1... | collective-permute-start | bytes 3538952 | tf_op jit(solution)/shard_map/ppermute | solution.py:270
  113.8 2.5 %collective-permute-done.18.other_ref = f32[18,128,128]{2,1,0:T(8,128)S(1)} collective-permute-done((f32[18,128,128]{2,1,0:T(8,128)S(1)}, f32[18,128,128]{2,1,0:T(8,128)S(1)}, u32[]{:S(2)}, u32[]{:S(2)}) %collective-permute-start.18) | collective-permute-done | bytes 1179680 | tf_op jit(solution)/shard_map/ppermute | solution.py:270
  116.3 32.5 %shard_map.47 = (f32[10,256,256]{2,1,0:T(8,128)S(1)}, f32[4,256,256]{2,1,0:T(8,128)S(1)}) custom-call(s32[1]{0:T(128)} %bitcast.core_ref, f32[18,128,128]{2,1,0:T(8,128)S(1)} %bitcast.49, f32[18,128,128]{2,1,0:T(8,128)S(1)} %collective-permute-done.18.other_ref), custom_call_target="tpu_custom_call" | custom-call | flops 34359738368 | bytes 6291456 | tf_op jit(solution)/shard_map/pallas_call | solution.py:190
  148.7 0.0 copy-done.1
  148.7 6.8 %shard_map.48 = (bf16[1024,1024]{1,0:T(8,128)(2,1)S(1)}, bf16[1024,1024]{1,0:T(8,128)(2,1)S(1)}) custom-call(f32[1024,1024]{1,0:T(8,128)S(1)} %copy-done.1, f32[10,256,256]{2,1,0:T(8,128)S(1)} %get-tuple-element.20.l_ref, f32[4,256,256]{2,1,0:T(8,128)S(1)} %get-tuple-element.21.d_ref), custom_call_target="tpu_custom_call" | custom-call | flops 6442450944 | bytes 12582912 | tf_op jit(solution)/shard_map/pallas_call | solution.py:226
  155.5 0.0 copy-start.2
  155.5 1.3 copy-done.2
  156.8 0.0 all-gather.3.cloned.1.call-done
  156.8 0.0 copy-start.3
  156.8 1.6 copy-done.3
  158.4 17.5 %shard_map.49 = f32[1024,2048]{1,0:T(8,128)} custom-call(s32[64]{0:T(128)S(1)} %compare_select_fusion.pick_ref, bf16[1024,1024]{1,0:T(8,128)(2,1)S(1)} %get-tuple-element.22.wh_ref, bf16[1024,1024]{1,0:T(8,128)(2,1)S(1)} %copy-done.3, f32[32,4,4,8,1024]{4,3,2,1,0:T(8,128)} %bitcast.52), custom_call_target="tpu_custom_call" | custom-call | flops 12884901888 | bytes 20971520 | tf_op jit(solution)/shard_map/pallas_call | solution.py:254
  (12 shorter events, 0.2 us)
Async XLA Ops:
  6.5 150.3 %all-gather.3.cloned.1.call-start = ((), (), s32[]{:S(2)}) async-start(), calls=%async_computation | async-start | bytes 16908288 | tf_op jit(solution)/shard_map/all_gather | solution.py:328
  6.5 4.3 %collective-permute-start = (f32[2,8,1024]{2,1,0:T(8,128)}, f32[2,8,1024]{2,1,0:T(8,128)S(1)}, u32[]{:S(2)}, u32[]{:S(2)}) collective-permute-start(f32[2,8,1024]{2,1,0:T(8,128)} %param.5), channel_id=1, source_target_pairs={{0,32},{32,0},{1,33},{33,1},{2,34},{34,2},{3,35},{35,3},{4,36},{36... | collective-permute-start | bytes 196616 | tf_op jit(solution)/shard_map/ppermute | solution.py:316
  12.4 2.2 %copy-start = (f32[1024,1024]{1,0:T(8,128)S(1)}, f32[1024,1024]{1,0:T(8,128)}, u32[]{:S(2)}) copy-start(f32[1024,1024]{1,0:T(8,128)} %t_ref.3) | copy-start | bytes 12582916
  19.2 5.9 %collective-permute-start.1 = (f32[18,128,128]{2,1,0:T(8,128)S(1)}, f32[18,128,128]{2,1,0:T(8,128)S(1)}, u32[]{:S(2)}, u32[]{:S(2)}) collective-permute-start(f32[18,128,128]{2,1,0:T(8,128)S(1)} %get-tuple-element.17), channel_id=1, source_target_pairs={{0,4},{4,0},{1,5},{5,1},{2,6},{6,2},{3,7},{7,3},{8,12},{12,8},{9,1... | collective-permute-start | bytes 3538952 | tf_op jit(solution)/shard_map/ppermute | solution.py:270
  25.3 2.8 %copy-start.4 = (s32[64]{0:T(128)S(1)}, s32[64]{0:T(128)}, u32[]{:S(2)}) copy-start(s32[64]{0:T(128)} %param.7) | copy-start | bytes 772
  25.4 10.6 %collective-permute-start.2 = (f32[4,144,128]{2,1,0:T(8,128)S(1)}, f32[4,144,128]{2,1,0:T(8,128)S(1)}, u32[]{:S(2)}, u32[]{:S(2)}) collective-permute-start(f32[4,144,128]{2,1,0:T(8,128)S(1)} %get-tuple-element.27), channel_id=1, source_target_pairs={{0,1},{1,2},{2,3},{3,0},{4,5},{5,6},{6,7},{7,4},{8,9},{9,10},{10,1... | collective-permute-start | bytes 884744 | tf_op jit(solution)/shard_map/ppermute | solution.py:275
  25.5 10.5 %collective-permute-start.4 = (f32[4,144,128]{2,1,0:T(8,128)S(1)}, f32[4,144,128]{2,1,0:T(8,128)S(1)}, u32[]{:S(2)}, u32[]{:S(2)}) collective-permute-start(f32[4,144,128]{2,1,0:T(8,128)S(1)} %get-tuple-element.28), channel_id=1, source_target_pairs={{0,3},{1,0},{2,1},{3,2},{4,7},{5,4},{6,5},{7,6},{8,11},{9,8},{10,9... | collective-permute-start | bytes 884744 | tf_op jit(solution)/shard_map/ppermute | solution.py:275
  28.2 13.6 %collective-permute-start.3 = (f32[4,144,128]{2,1,0:T(8,128)S(1)}, f32[4,144,128]{2,1,0:T(8,128)S(1)}, u32[]{:S(2)}, u32[]{:S(2)}) collective-permute-start(f32[4,144,128]{2,1,0:T(8,128)S(1)} %get-tuple-element.29), channel_id=1, source_target_pairs={{0,2},{1,3},{2,0},{3,1},{4,6},{5,7},{6,4},{7,5},{8,10},{9,11},{10,... | collective-permute-start | bytes 884744 | tf_op jit(solution)/shard_map/ppermute | solution.py:275
  41.9 4.5 %collective-permute-start.5 = (f32[144,128]{1,0:T(8,128)S(1)}, f32[144,128]{1,0:T(8,128)S(1)}, u32[]{:S(2)}, u32[]{:S(2)}) collective-permute-start(f32[144,128]{1,0:T(8,128)S(1)} %get-tuple-element.30), channel_id=1, source_target_pairs={{0,8},{8,16},{16,24},{24,0},{1,9},{9,17},{17,25},{25,1},{2,10},{10... | collective-permute-start | bytes 221192 | tf_op jit(solution)/shard_map/ppermute | solution.py:275
  43.1 3.6 %collective-permute-start.7 = (f32[144,128]{1,0:T(8,128)S(1)}, f32[144,128]{1,0:T(8,128)S(1)}, u32[]{:S(2)}, u32[]{:S(2)}) collective-permute-start(f32[144,128]{1,0:T(8,128)S(1)} %get-tuple-element.31), channel_id=1, source_target_pairs={{0,24},{8,0},{16,8},{24,16},{1,25},{9,1},{17,9},{25,17},{2,26},{10... | collective-permute-start | bytes 221192 | tf_op jit(solution)/shard_map/ppermute | solution.py:275
  44.6 5.2 %collective-permute-start.6 = (f32[144,128]{1,0:T(8,128)S(1)}, f32[144,128]{1,0:T(8,128)S(1)}, u32[]{:S(2)}, u32[]{:S(2)}) collective-permute-start(f32[144,128]{1,0:T(8,128)S(1)} %get-tuple-element.32), channel_id=1, source_target_pairs={{0,16},{8,24},{16,0},{24,8},{1,17},{9,25},{17,1},{25,9},{2,18},{10... | collective-permute-start | bytes 221192 | tf_op jit(solution)/shard_map/ppermute | solution.py:275
  49.9 11.3 %collective-permute-start.10 = (f32[144,128]{1,0:T(8,128)S(1)}, f32[144,128]{1,0:T(8,128)S(1)}, u32[]{:S(2)}, u32[]{:S(2)}) collective-permute-start(f32[144,128]{1,0:T(8,128)S(1)} %fusion.3), channel_id=1, source_target_pairs={{0,192},{32,224},{64,128},{96,160},{128,64},{160,96},{192,0},{224,... | collective-permute-start | bytes 221192 | tf_op jit(solution)/shard_map/ppermute | solution.py:302
  56.3 10.5 %collective-permute-start.9 = (f32[144,128]{1,0:T(8,128)S(1)}, f32[144,128]{1,0:T(8,128)S(1)}, u32[]{:S(2)}, u32[]{:S(2)}) collective-permute-start(f32[144,128]{1,0:T(8,128)S(1)} %fusion.3), channel_id=1, source_target_pairs={{0,64},{32,96},{64,0},{96,32},{128,192},{160,224},{192,128},{224,1... | collective-permute-start | bytes 221192 | tf_op jit(solution)/shard_map/ppermute | solution.py:302
  57.5 11.7 %collective-permute-start.8 = (f32[144,128]{1,0:T(8,128)S(1)}, f32[144,128]{1,0:T(8,128)S(1)}, u32[]{:S(2)}, u32[]{:S(2)}) collective-permute-start(f32[144,128]{1,0:T(8,128)S(1)} %fusion.3), channel_id=1, source_target_pairs={{0,128},{32,160},{64,192},{96,224},{128,0},{160,32},{192,64},{224,... | collective-permute-start | bytes 221192 | tf_op jit(solution)/shard_map/ppermute | solution.py:302
  69.3 7.4 %collective-permute-start.11 = (f32[144,128]{1,0:T(8,128)S(1)}, f32[144,128]{1,0:T(8,128)S(1)}, u32[]{:S(2)}, u32[]{:S(2)}) collective-permute-start(f32[144,128]{1,0:T(8,128)S(1)} %add_add_fusion), channel_id=1, source_target_pairs={{0,32},{32,0},{64,96},{96,64},{128,160},{160,128},{192,224},{224,1... | collective-permute-start | bytes 221192 | tf_op jit(solution)/shard_map/ppermute | solution.py:302
  76.7 4.9 %collective-permute-start.12 = (f32[144,128]{1,0:T(8,128)S(1)}, f32[144,128]{1,0:T(8,128)S(1)}, u32[]{:S(2)}, u32[]{:S(2)}) collective-permute-start(f32[144,128]{1,0:T(8,128)S(1)} %get-tuple-element.26), channel_id=1, source_target_pairs={{0,8},{8,16},{16,24},{24,0},{1,9},{9,17},{17,25},{25,1},{2,10},{10... | collective-permute-start | bytes 221192 | tf_op jit(solution)/shard_map/ppermute | solution.py:275
  77.0 6.8 %collective-permute-start.13 = (f32[144,128]{1,0:T(8,128)S(1)}, f32[144,128]{1,0:T(8,128)S(1)}, u32[]{:S(2)}, u32[]{:S(2)}) collective-permute-start(f32[144,128]{1,0:T(8,128)S(1)} %get-tuple-element.26), channel_id=1, source_target_pairs={{0,16},{8,24},{16,0},{24,8},{1,17},{9,25},{17,1},{25,9},{2,18},{10... | collective-permute-start | bytes 221192 | tf_op jit(solution)/shard_map/ppermute | solution.py:275
  81.0 3.9 %collective-permute-start.14 = (f32[144,128]{1,0:T(8,128)S(1)}, f32[144,128]{1,0:T(8,128)S(1)}, u32[]{:S(2)}, u32[]{:S(2)}) collective-permute-start(f32[144,128]{1,0:T(8,128)S(1)} %get-tuple-element.26), channel_id=1, source_target_pairs={{0,24},{8,0},{16,8},{24,16},{1,25},{9,1},{17,9},{25,17},{2,26},{10... | collective-permute-start | bytes 221192 | tf_op jit(solution)/shard_map/ppermute | solution.py:275
  85.0 13.0 %collective-permute-start.15 = (f32[4,144,128]{2,1,0:T(8,128)S(1)}, f32[4,144,128]{2,1,0:T(8,128)S(1)}, u32[]{:S(2)}, u32[]{:S(2)}) collective-permute-start(f32[4,144,128]{2,1,0:T(8,128)S(1)} %bitcast_dynamic-update-slice_fusion.4), channel_id=1, source_target_pairs={{0,1},{1,2},{2,3},{3,0},{4,5},{5,6},{6,7},{7,4},{8,9},{9,10},{10,1... | collective-permute-start | bytes 884744 | tf_op jit(solution)/shard_map/ppermute | solution.py:275
  85.9 22.6 %collective-permute-start.17 = (f32[4,144,128]{2,1,0:T(8,128)S(1)}, f32[4,144,128]{2,1,0:T(8,128)S(1)}, u32[]{:S(2)}, u32[]{:S(2)}) collective-permute-start(f32[4,144,128]{2,1,0:T(8,128)S(1)} %bitcast_dynamic-update-slice_fusion.4), channel_id=1, source_target_pairs={{0,3},{1,0},{2,1},{3,2},{4,7},{5,4},{6,5},{7,6},{8,11},{9,8},{10,9... | collective-permute-start | bytes 884744 | tf_op jit(solution)/shard_map/ppermute | solution.py:275
  87.7 20.7 %collective-permute-start.16 = (f32[4,144,128]{2,1,0:T(8,128)S(1)}, f32[4,144,128]{2,1,0:T(8,128)S(1)}, u32[]{:S(2)}, u32[]{:S(2)}) collective-permute-start(f32[4,144,128]{2,1,0:T(8,128)S(1)} %bitcast_dynamic-update-slice_fusion.4), channel_id=1, source_target_pairs={{0,2},{1,3},{2,0},{3,1},{4,6},{5,7},{6,4},{7,5},{8,10},{9,11},{10,... | collective-permute-start | bytes 884744 | tf_op jit(solution)/shard_map/ppermute | solution.py:275
  108.5 40.2 %copy-start.1 = (f32[1024,1024]{1,0:T(8,128)S(1)}, f32[1024,1024]{1,0:T(8,128)}, u32[]{:S(2)}) copy-start(f32[1024,1024]{1,0:T(8,128)} %t_ref.3) | copy-start | bytes 12582916
  108.5 7.8 %collective-permute-start.18 = (f32[18,128,128]{2,1,0:T(8,128)S(1)}, f32[18,128,128]{2,1,0:T(8,128)S(1)}, u32[]{:S(2)}, u32[]{:S(2)}) collective-permute-start(f32[18,128,128]{2,1,0:T(8,128)S(1)} %bitcast.48), channel_id=1, source_target_pairs={{0,4},{4,0},{1,5},{5,1},{2,6},{6,2},{3,7},{7,3},{8,12},{12,8},{9,1... | collective-permute-start | bytes 3538952 | tf_op jit(solution)/shard_map/ppermute | solution.py:270
  155.5 1.3 copy-start.2
  156.8 1.6 copy-start.3
Sparse Core Ops, SparseCore 0:
  12.5 120.1 all-gather.2

commit v6 on v4

--- a/solution.py
+++ b/solution.py
@@ -201,7 +201,7 @@
     )(core, mine, other)
 
 
-def solve_kernel(n, scale, t_ref, l_ref, d_ref, wh_ref, wl_ref):
+def solve_kernel(n, scale, t_ref, l_ref, d_ref, w_ref):
     place = lambda i, j: j * n - j * (j - 1) // 2 + (i - j)
     at = lambda j: slice(256 * j, 256 * j + 256)
     ys = []
@@ -216,8 +216,8 @@
         for i in range(j + 1, n):
             acc = acc - dot3(ws[i], split(l_ref[place(i, j)]), NN)
         ws[j] = split(acc)
-        wh_ref[:, at(j)] = ws[j][0] * jnp.bfloat16(scale)
-        wl_ref[:, at(j)] = ws[j][1] * jnp.bfloat16(scale)
+        w_ref[:, at(j)] = ws[j][0] * jnp.bfloat16(scale)
+        w_ref[:, at(n + j)] = ws[j][1] * jnp.bfloat16(scale)
 
 
 def solve(t, l, d, n):
@@ -225,15 +225,15 @@
     whole = pl.BlockSpec(memory_space=pltpu.VMEM)
     return pl.pallas_call(
         functools.partial(solve_kernel, n, features ** -0.5),
-        out_shape=(jax.ShapeDtypeStruct((m, features), jnp.bfloat16),) * 2,
+        out_shape=jax.ShapeDtypeStruct((m, 2 * features), jnp.bfloat16),
         in_specs=[whole] * 3,
-        out_specs=(whole,) * 2,
+        out_specs=whole,
         compiler_params=pltpu.CompilerParams(vmem_limit_bytes=36 * MIB),
         cost_estimate=cost(6 * m * features * features, 12 * MIB),
     )(t, l, d)
 
 
-def score_kernel(pick_ref, wh_ref, wl_ref, v_ref, out_ref):
+def score_kernel(pick_ref, w_ref, v_ref, out_ref):
     step = pl.program_id(0)
     leads, groups = v_ref.shape[:2]
     rows = []
@@ -243,11 +243,12 @@
         for y in range(groups):
             rows.append(v_ref[s % leads, y, jnp.maximum(pick, 0)] * live)
     v = split(jnp.concatenate(rows, axis=0))
-    out_ref[...] = dot3((wh_ref[...], wl_ref[...]), v, NT)
-
-
-def score(pick, wh, wl, v, leads):
-    m, features = wh.shape
+    features = v_ref.shape[-1]
+    out_ref[...] = dot3((w_ref[:, :features], w_ref[:, features:]), v, NT)
+
+
+def score(pick, w, v, leads):
+    m, features = w.shape[0], v.shape[-1]
     total, groups, both, part, _ = v.shape
     width = 2 * leads * groups * part
     whole = pl.BlockSpec(memory_space=pltpu.VMEM)
@@ -257,13 +258,13 @@
         out_shape=jax.ShapeDtypeStruct((m, total * 2 * groups * part), jnp.float32),
         in_specs=[
             pl.BlockSpec(memory_space=pltpu.SMEM),
-            whole, whole,
+            whole,
             pl.BlockSpec((leads, groups, both, part, features), lambda i: (i, 0, 0, 0, 0)),
         ],
         out_specs=pl.BlockSpec((m, width), lambda i: (0, i)),
-        compiler_params=pltpu.CompilerParams(vmem_limit_bytes=44 * MIB),
+        compiler_params=pltpu.CompilerParams(vmem_limit_bytes=36 * MIB),
         cost_estimate=cost(12 * m * total * groups * part * features, 20 * MIB),
-    )(pick, wh, wl, v)
+    )(pick, w, v)
 
 
 def swap(v):
@@ -299,10 +300,10 @@
     v = (mine + swap(other)).reshape(ny, nx, -1, 128)
     v, beside = lax.optimization_barrier((scatter(v, "y"), beside))
     v = scatter(v, "x")
-    hop = 1
-    while hop < nz:
+    hop = nz // 2
+    while hop:
         v = v + lax.ppermute(v, Z, [(i, i ^ hop) for i in range(nz)])
-        hop *= 2
+        hop //= 2
     return gather(gather(v, "x"), "y").reshape(shape), beside
 
 
@@ -330,8 +331,7 @@
     val_all = val_all.reshape(slabs // 2, group, 2 * blocks, part, features)
     mine, pick = sum_all(mine, other, pick)
     l, d = factor(core, mine, swap(mine), n, 1.0 / (m * slabs * group))
-    wh, wl = solve(train_grads, l, d, n)
-    return score(pick, wh, wl, val_all, plane)
+    return score(pick, solve(train_grads, l, d, n), val_all, plane)
 
 
 def solution(mesh):

time: 164 us -> 171 us (1.043)
  the two profiles are of different devices: /device:TPU:35 before, /device:TPU:1 now
where the time goes in v6:
time: 171 us; the launch traced here: 169 us
  Pallas kernels  61.3 us (36%)
  starting transfers between devices  44.5 us (26%)
  waiting for transfers between devices  39.2 us (23%)
  between operations  15.3 us (9%)
  local copies, waits for them, and re-layouts  6.72 us (4%)
  other arithmetic  2.23 us (1%)
    pallas_call x1, Pallas kernels, factor(): pl.pallas_call(functools.partial(factor_kernel, n, scale), out_shape=(jax...  32.5 us
    ppermute x12, waiting for transfers between devices, ring(): return lax.ppermute(v, axis, [(i, (i + k) % size) for i in range(size)])  26 us
    ppermute x12, starting transfers between devices, ring(): return lax.ppermute(v, axis, [(i, (i + k) % size) for i in range(size)])  18.2 us
    pallas_call x1, Pallas kernels, score(): pl.pallas_call(score_kernel, grid=(total // leads,), out_shape=jax.ShapeD...  17.4 us
    ppermute x2, starting transfers between devices, swap(): return lax.ppermute(v, 'core', [(0, 1), (1, 0)])  14.4 us
    ppermute x3, starting transfers between devices, sum_all(): v = v + lax.ppermute(v, Z, [(i, i ^ hop) for i in range(nz)])  9.42 us
    ppermute x3, waiting for transfers between devices, sum_all(): v = v + lax.ppermute(v, Z, [(i, i ^ hop) for i in range(nz)])  8.23 us
    pallas_call x1, Pallas kernels, solve(): pl.pallas_call(functools.partial(solve_kernel, n, features ** (-0.5)), ou...  6.8 us
  transfers between devices with their start and end apart: 19, of which 14 were waited for; matrix products, arithmetic and copies ran while one was open for 1% of the time, Pallas kernels for 26%

profile of v6, /device:TPU:1, one launch (start us, length us, event | category | flops | bytes accessed | tf_op | source)
XLA Modules:
  0.0 169.2 jit_solution(12010641637503719678)
XLA Ops:
  6.5 0.0 all-gather.3.cloned.1.call-start
  6.5 2.5 %collective-permute-start = (f32[2,8,1024]{2,1,0:T(8,128)}, f32[2,8,1024]{2,1,0:T(8,128)S(1)}, u32[]{:S(2)}, u32[]{:S(2)}) collective-permute-start(f32[2,8,1024]{2,1,0:T(8,128)} %param.5), channel_id=1, source_target_pairs={{0,32},{32,0},{1,33},{33,1},{2,34},{34,2},{3,35},{35,3},{4,36},{36... | collective-permute-start | bytes 196616 | tf_op jit(solution)/shard_map/ppermute | solution.py:318
  9.0 0.0 copy-start
  9.0 2.2 %copy-done = f32[1024,1024]{1,0:T(8,128)S(1)} copy-done((f32[1024,1024]{1,0:T(8,128)S(1)}, f32[1024,1024]{1,0:T(8,128)}, u32[]{:S(2)}) %copy-start) | copy-done | bytes 4194328
  11.2 0.0 copy-start.4
  11.2 4.6 %shard_map.46 = (f32[18,128,128]{2,1,0:T(8,128)S(1)}, f32[18,128,128]{2,1,0:T(8,128)S(1)}) custom-call(s32[1]{0:T(128)} %bitcast.core_ref, f32[1024,1024]{1,0:T(8,128)S(1)} %copy-done), custom_call_target="tpu_custom_call" | custom-call | flops 6442450944 | bytes 7340032 | tf_op jit(solution)/shard_map/pallas_call | solution.py:134
  15.8 0.0 collective-permute-done
  15.8 0.0 copy-done.4
  15.8 0.7 pad_maximum_fusion
  16.5 0.0 all-gather.3.cloned.1.call-update
  16.5 1.0 collective-permute-start.1
  17.6 2.5 %collective-permute-done.1 = f32[18,128,128]{2,1,0:T(8,128)S(1)} collective-permute-done((f32[18,128,128]{2,1,0:T(8,128)S(1)}, f32[18,128,128]{2,1,0:T(8,128)S(1)}, u32[]{:S(2)}, u32[]{:S(2)}) %collective-permute-start.1) | collective-permute-done | bytes 1179680 | tf_op jit(solution)/shard_map/ppermute | solution.py:271
  20.0 0.1 add.129
  20.2 0.0 copy-start.5
  20.2 0.1 dynamic-slice_bitcast_fusion.2
  20.3 1.4 collective-permute-start.2
  21.7 1.5 collective-permute-start.4
  23.2 1.6 collective-permute-start.3
  24.7 0.0 copy-done.5
  24.7 0.6 fusion.9
  27.1 0.7 compare_select_fusion.pick_ref
  27.8 2.1 %collective-permute-done.2 = f32[4,144,128]{2,1,0:T(8,128)S(1)} collective-permute-done((f32[4,144,128]{2,1,0:T(8,128)S(1)}, f32[4,144,128]{2,1,0:T(8,128)S(1)}, u32[]{:S(2)}, u32[]{:S(2)}) %collective-permute-start.2) | collective-permute-done | bytes 294944 | tf_op jit(solution)/shard_map/ppermute | solution.py:276
  29.9 0.0 collective-permute-done.4
  29.9 7.9 %collective-permute-done.3 = f32[4,144,128]{2,1,0:T(8,128)S(1)} collective-permute-done((f32[4,144,128]{2,1,0:T(8,128)S(1)}, f32[4,144,128]{2,1,0:T(8,128)S(1)}, u32[]{:S(2)}, u32[]{:S(2)}) %collective-permute-start.3) | collective-permute-done | bytes 294944 | tf_op jit(solution)/shard_map/ppermute | solution.py:276
  37.8 0.1 fusion.1
  37.9 1.3 collective-permute-start.5
  39.2 1.5 collective-permute-start.7
  40.7 1.5 collective-permute-start.6
  42.2 0.7 collective-permute-done.5
  42.9 0.0 collective-permute-done.7
  42.9 2.9 %collective-permute-done.6 = f32[144,128]{1,0:T(8,128)S(1)} collective-permute-done((f32[144,128]{1,0:T(8,128)S(1)}, f32[144,128]{1,0:T(8,128)S(1)}, u32[]{:S(2)}, u32[]{:S(2)}) %collective-permute-start.6) | collective-permute-done | bytes 73760 | tf_op jit(solution)/shard_map/ppermute | solution.py:276
  45.9 6.3 %collective-permute-start.8 = (f32[144,128]{1,0:T(8,128)S(1)}, f32[144,128]{1,0:T(8,128)S(1)}, u32[]{:S(2)}, u32[]{:S(2)}) collective-permute-start(f32[144,128]{1,0:T(8,128)S(1)} %fusion.3), channel_id=1, source_target_pairs={{0,128},{32,160},{64,192},{96,224},{128,0},{160,32},{192,64},{224,... | collective-permute-start | bytes 221192 | tf_op jit(solution)/shard_map/ppermute | solution.py:305
  52.1 1.8 %collective-permute-done.8 = f32[144,128]{1,0:T(8,128)S(1)} collective-permute-done((f32[144,128]{1,0:T(8,128)S(1)}, f32[144,128]{1,0:T(8,128)S(1)}, u32[]{:S(2)}, u32[]{:S(2)}) %collective-permute-start.8) | collective-permute-done | bytes 73760 | tf_op jit(solution)/shard_map/ppermute | solution.py:305
  53.9 3.0 %collective-permute-start.9 = (f32[144,128]{1,0:T(8,128)S(1)}, f32[144,128]{1,0:T(8,128)S(1)}, u32[]{:S(2)}, u32[]{:S(2)}) collective-permute-start(f32[144,128]{1,0:T(8,128)S(1)} %add.155), channel_id=1, source_target_pairs={{0,64},{32,96},{64,0},{96,32},{128,192},{160,224},{192,128},{224,1... | collective-permute-start | bytes 221192 | tf_op jit(solution)/shard_map/ppermute | solution.py:305
  57.0 2.9 %collective-permute-done.9 = f32[144,128]{1,0:T(8,128)S(1)} collective-permute-done((f32[144,128]{1,0:T(8,128)S(1)}, f32[144,128]{1,0:T(8,128)S(1)}, u32[]{:S(2)}, u32[]{:S(2)}) %collective-permute-start.9) | collective-permute-done | bytes 73760 | tf_op jit(solution)/shard_map/ppermute | solution.py:305
  59.8 0.1 collective-permute-start.10
  59.9 3.6 %collective-permute-done.10 = f32[144,128]{1,0:T(8,128)S(1)} collective-permute-done((f32[144,128]{1,0:T(8,128)S(1)}, f32[144,128]{1,0:T(8,128)S(1)}, u32[]{:S(2)}, u32[]{:S(2)}) %collective-permute-start.10) | collective-permute-done | bytes 73760 | tf_op jit(solution)/shard_map/ppermute | solution.py:305
  63.6 2.7 %collective-permute-start.11 = (f32[144,128]{1,0:T(8,128)S(1)}, f32[144,128]{1,0:T(8,128)S(1)}, u32[]{:S(2)}, u32[]{:S(2)}) collective-permute-start(f32[144,128]{1,0:T(8,128)S(1)} %get-tuple-element.24), channel_id=1, source_target_pairs={{0,8},{8,16},{16,24},{24,0},{1,9},{9,17},{17,25},{25,1},{2,10},{10... | collective-permute-start | bytes 221192 | tf_op jit(solution)/shard_map/ppermute | solution.py:276
  66.3 3.7 %collective-permute-start.12 = (f32[144,128]{1,0:T(8,128)S(1)}, f32[144,128]{1,0:T(8,128)S(1)}, u32[]{:S(2)}, u32[]{:S(2)}) collective-permute-start(f32[144,128]{1,0:T(8,128)S(1)} %get-tuple-element.24), channel_id=1, source_target_pairs={{0,16},{8,24},{16,0},{24,8},{1,17},{9,25},{17,1},{25,9},{2,18},{10... | collective-permute-start | bytes 221192 | tf_op jit(solution)/shard_map/ppermute | solution.py:276
  70.1 0.2 collective-permute-start.13
  70.3 1.1 collective-permute-done.11
  71.4 2.4 %collective-permute-done.12 = f32[144,128]{1,0:T(8,128)S(1)} collective-permute-done((f32[144,128]{1,0:T(8,128)S(1)}, f32[144,128]{1,0:T(8,128)S(1)}, u32[]{:S(2)}, u32[]{:S(2)}) %collective-permute-start.12) | collective-permute-done | bytes 73760 | tf_op jit(solution)/shard_map/ppermute | solution.py:276
  73.8 0.4 collective-permute-done.13
  74.2 0.1 collective-permute-start.14
  74.3 2.7 %collective-permute-start.16 = (f32[4,144,128]{2,1,0:T(8,128)S(1)}, f32[4,144,128]{2,1,0:T(8,128)S(1)}, u32[]{:S(2)}, u32[]{:S(2)}) collective-permute-start(f32[4,144,128]{2,1,0:T(8,128)S(1)} %bitcast_dynamic-update-slice_fusion.4), channel_id=1, source_target_pairs={{0,3},{1,0},{2,1},{3,2},{4,7},{5,4},{6,5},{7,6},{8,11},{9,8},{10,9... | collective-permute-start | bytes 884744 | tf_op jit(solution)/shard_map/ppermute | solution.py:276
  76.9 0.0 collective-permute-start.15
  76.9 0.1 broadcast_in_dim.38
  77.0 4.2 %collective-permute-done.14 = f32[4,144,128]{2,1,0:T(8,128)S(1)} collective-permute-done((f32[4,144,128]{2,1,0:T(8,128)S(1)}, f32[4,144,128]{2,1,0:T(8,128)S(1)}, u32[]{:S(2)}, u32[]{:S(2)}) %collective-permute-start.14) | collective-permute-done | bytes 294944 | tf_op jit(solution)/shard_map/ppermute | solution.py:276
  81.2 4.3 %collective-permute-done.15 = f32[4,144,128]{2,1,0:T(8,128)S(1)} collective-permute-done((f32[4,144,128]{2,1,0:T(8,128)S(1)}, f32[4,144,128]{2,1,0:T(8,128)S(1)}, u32[]{:S(2)}, u32[]{:S(2)}) %collective-permute-start.15) | collective-permute-done | bytes 294944 | tf_op jit(solution)/shard_map/ppermute | solution.py:276
  85.5 0.0 collective-permute-done.16
  85.6 0.0 copy-start.1
  85.6 13.4 %collective-permute-start.17 = (f32[18,128,128]{2,1,0:T(8,128)S(1)}, f32[18,128,128]{2,1,0:T(8,128)S(1)}, u32[]{:S(2)}, u32[]{:S(2)}) collective-permute-start(f32[18,128,128]{2,1,0:T(8,128)S(1)} %bitcast.48), channel_id=1, source_target_pairs={{0,4},{4,0},{1,5},{5,1},{2,6},{6,2},{3,7},{7,3},{8,12},{12,8},{9,1... | collective-permute-start | bytes 3538952 | tf_op jit(solution)/shard_map/ppermute | solution.py:271
  99.0 2.5 %collective-permute-done.17.other_ref = f32[18,128,128]{2,1,0:T(8,128)S(1)} collective-permute-done((f32[18,128,128]{2,1,0:T(8,128)S(1)}, f32[18,128,128]{2,1,0:T(8,128)S(1)}, u32[]{:S(2)}, u32[]{:S(2)}) %collective-permute-start.17) | collective-permute-done | bytes 1179680 | tf_op jit(solution)/shard_map/ppermute | solution.py:271
  101.5 32.5 %shard_map.47 = (f32[10,256,256]{2,1,0:T(8,128)S(1)}, f32[4,256,256]{2,1,0:T(8,128)S(1)}) custom-call(s32[1]{0:T(128)} %bitcast.core_ref, f32[18,128,128]{2,1,0:T(8,128)S(1)} %bitcast.49, f32[18,128,128]{2,1,0:T(8,128)S(1)} %collective-permute-done.17.other_ref), custom_call_target="tpu_custom_call" | custom-call | flops 34359738368 | bytes 6291456 | tf_op jit(solution)/shard_map/pallas_call | solution.py:190
  133.9 0.0 copy-done.1
  133.9 6.8 %shard_map.48.w_ref = bf16[1024,2048]{1,0:T(8,128)(2,1)S(1)} custom-call(f32[1024,1024]{1,0:T(8,128)S(1)} %copy-done.1, f32[10,256,256]{2,1,0:T(8,128)S(1)} %get-tuple-element.20.l_ref, f32[4,256,256]{2,1,0:T(8,128)S(1)} %get-tuple-element.21.d_ref), custom_call_target="tpu_custom_call" | custom-call | flops 6442450944 | bytes 12582912 | tf_op jit(solution)/shard_map/pallas_call | solution.py:226
  140.7 0.0 copy-start.2
  140.8 2.0 %copy-done.2 = bf16[1024,2048]{1,0:T(8,128)(2,1)} copy-done((bf16[1024,2048]{1,0:T(8,128)(2,1)}, bf16[1024,2048]{1,0:T(8,128)(2,1)S(1)}, u32[]{:S(2)}) %copy-start.2) | copy-done | bytes 4194328
  142.8 0.0 all-gather.3.cloned.1.call-done
  142.8 0.0 copy-start.3
  142.8 2.2 %copy-done.3 = bf16[1024,2048]{1,0:T(8,128)(2,1)S(1)} copy-done((bf16[1024,2048]{1,0:T(8,128)(2,1)S(1)}, bf16[1024,2048]{1,0:T(8,128)(2,1)}, u32[]{:S(2)}) %copy-start.3) | copy-done | bytes 4194328
  145.0 17.4 %shard_map.49 = f32[1024,2048]{1,0:T(8,128)} custom-call(s32[64]{0:T(128)S(1)} %compare_select_fusion.pick_ref, bf16[1024,2048]{1,0:T(8,128)(2,1)S(1)} %copy-done.3, f32[32,4,4,8,1024]{4,3,2,1,0:T(8,128)} %bitcast.52), custom_call_target="tpu_custom_call" | custom-call | flops 12884901888 | bytes 20971520 | tf_op jit(solution)/shard_map/pallas_call | solution.py:255
  (13 shorter events, 0.2 us)
Async XLA Ops:
  6.5 136.2 %all-gather.3.cloned.1.call-start = ((), (), s32[]{:S(2)}) async-start(), calls=%async_computation | async-start | bytes 16908288 | tf_op jit(solution)/shard_map/all_gather | solution.py:330
  6.5 9.3 %collective-permute-start = (f32[2,8,1024]{2,1,0:T(8,128)}, f32[2,8,1024]{2,1,0:T(8,128)S(1)}, u32[]{:S(2)}, u32[]{:S(2)}) collective-permute-start(f32[2,8,1024]{2,1,0:T(8,128)} %param.5), channel_id=1, source_target_pairs={{0,32},{32,0},{1,33},{33,1},{2,34},{34,2},{3,35},{35,3},{4,36},{36... | collective-permute-start | bytes 196616 | tf_op jit(solution)/shard_map/ppermute | solution.py:318
  9.0 2.2 %copy-start = (f32[1024,1024]{1,0:T(8,128)S(1)}, f32[1024,1024]{1,0:T(8,128)}, u32[]{:S(2)}) copy-start(f32[1024,1024]{1,0:T(8,128)} %t_ref.3) | copy-start | bytes 12582916
  11.2 4.6 %copy-start.4 = (f32[2,8,1024]{2,1,0:T(8,128)S(1)}, f32[2,8,1024]{2,1,0:T(8,128)}, u32[]{:S(2)}) copy-start(f32[2,8,1024]{2,1,0:T(8,128)} %param.5) | copy-start | bytes 196612
  16.5 3.5 %collective-permute-start.1 = (f32[18,128,128]{2,1,0:T(8,128)S(1)}, f32[18,128,128]{2,1,0:T(8,128)S(1)}, u32[]{:S(2)}, u32[]{:S(2)}) collective-permute-start(f32[18,128,128]{2,1,0:T(8,128)S(1)} %get-tuple-element.17), channel_id=1, source_target_pairs={{0,4},{4,0},{1,5},{5,1},{2,6},{6,2},{3,7},{7,3},{8,12},{12,8},{9,1... | collective-permute-start | bytes 3538952 | tf_op jit(solution)/shard_map/ppermute | solution.py:271
  20.2 4.5 %copy-start.5 = (s32[64]{0:T(128)S(1)}, s32[64]{0:T(128)}, u32[]{:S(2)}) copy-start(s32[64]{0:T(128)} %param.7) | copy-start | bytes 772
  20.3 9.6 %collective-permute-start.2 = (f32[4,144,128]{2,1,0:T(8,128)S(1)}, f32[4,144,128]{2,1,0:T(8,128)S(1)}, u32[]{:S(2)}, u32[]{:S(2)}) collective-permute-start(f32[4,144,128]{2,1,0:T(8,128)S(1)} %get-tuple-element.25), channel_id=1, source_target_pairs={{0,1},{1,2},{2,3},{3,0},{4,5},{5,6},{6,7},{7,4},{8,9},{9,10},{10,1... | collective-permute-start | bytes 884744 | tf_op jit(solution)/shard_map/ppermute | solution.py:276
  21.7 8.3 %collective-permute-start.4 = (f32[4,144,128]{2,1,0:T(8,128)S(1)}, f32[4,144,128]{2,1,0:T(8,128)S(1)}, u32[]{:S(2)}, u32[]{:S(2)}) collective-permute-start(f32[4,144,128]{2,1,0:T(8,128)S(1)} %get-tuple-element.26), channel_id=1, source_target_pairs={{0,3},{1,0},{2,1},{3,2},{4,7},{5,4},{6,5},{7,6},{8,11},{9,8},{10,9... | collective-permute-start | bytes 884744 | tf_op jit(solution)/shard_map/ppermute | solution.py:276
  23.2 14.6 %collective-permute-start.3 = (f32[4,144,128]{2,1,0:T(8,128)S(1)}, f32[4,144,128]{2,1,0:T(8,128)S(1)}, u32[]{:S(2)}, u32[]{:S(2)}) collective-permute-start(f32[4,144,128]{2,1,0:T(8,128)S(1)} %get-tuple-element.27), channel_id=1, source_target_pairs={{0,2},{1,3},{2,0},{3,1},{4,6},{5,7},{6,4},{7,5},{8,10},{9,11},{10,... | collective-permute-start | bytes 884744 | tf_op jit(solution)/shard_map/ppermute | solution.py:276
  37.9 5.0 %collective-permute-start.5 = (f32[144,128]{1,0:T(8,128)S(1)}, f32[144,128]{1,0:T(8,128)S(1)}, u32[]{:S(2)}, u32[]{:S(2)}) collective-permute-start(f32[144,128]{1,0:T(8,128)S(1)} %get-tuple-element.28), channel_id=1, source_target_pairs={{0,8},{8,16},{16,24},{24,0},{1,9},{9,17},{17,25},{25,1},{2,10},{10... | collective-permute-start | bytes 221192 | tf_op jit(solution)/shard_map/ppermute | solution.py:276
  39.2 3.7 %collective-permute-start.7 = (f32[144,128]{1,0:T(8,128)S(1)}, f32[144,128]{1,0:T(8,128)S(1)}, u32[]{:S(2)}, u32[]{:S(2)}) collective-permute-start(f32[144,128]{1,0:T(8,128)S(1)} %get-tuple-element.29), channel_id=1, source_target_pairs={{0,24},{8,0},{16,8},{24,16},{1,25},{9,1},{17,9},{25,17},{2,26},{10... | collective-permute-start | bytes 221192 | tf_op jit(solution)/shard_map/ppermute | solution.py:276
  40.7 5.2 %collective-permute-start.6 = (f32[144,128]{1,0:T(8,128)S(1)}, f32[144,128]{1,0:T(8,128)S(1)}, u32[]{:S(2)}, u32[]{:S(2)}) collective-permute-start(f32[144,128]{1,0:T(8,128)S(1)} %get-tuple-element.30), channel_id=1, source_target_pairs={{0,16},{8,24},{16,0},{24,8},{1,17},{9,25},{17,1},{25,9},{2,18},{10... | collective-permute-start | bytes 221192 | tf_op jit(solution)/shard_map/ppermute | solution.py:276
  45.9 8.0 %collective-permute-start.8 = (f32[144,128]{1,0:T(8,128)S(1)}, f32[144,128]{1,0:T(8,128)S(1)}, u32[]{:S(2)}, u32[]{:S(2)}) collective-permute-start(f32[144,128]{1,0:T(8,128)S(1)} %fusion.3), channel_id=1, source_target_pairs={{0,128},{32,160},{64,192},{96,224},{128,0},{160,32},{192,64},{224,... | collective-permute-start | bytes 221192 | tf_op jit(solution)/shard_map/ppermute | solution.py:305
  53.9 5.9 %collective-permute-start.9 = (f32[144,128]{1,0:T(8,128)S(1)}, f32[144,128]{1,0:T(8,128)S(1)}, u32[]{:S(2)}, u32[]{:S(2)}) collective-permute-start(f32[144,128]{1,0:T(8,128)S(1)} %add.155), channel_id=1, source_target_pairs={{0,64},{32,96},{64,0},{96,32},{128,192},{160,224},{192,128},{224,1... | collective-permute-start | bytes 221192 | tf_op jit(solution)/shard_map/ppermute | solution.py:305
  59.8 3.7 %collective-permute-start.10 = (f32[144,128]{1,0:T(8,128)S(1)}, f32[144,128]{1,0:T(8,128)S(1)}, u32[]{:S(2)}, u32[]{:S(2)}) collective-permute-start(f32[144,128]{1,0:T(8,128)S(1)} %add.156), channel_id=1, source_target_pairs={{0,32},{32,0},{64,96},{96,64},{128,160},{160,128},{192,224},{224,1... | collective-permute-start | bytes 221192 | tf_op jit(solution)/shard_map/ppermute | solution.py:305
  63.6 7.8 %collective-permute-start.11 = (f32[144,128]{1,0:T(8,128)S(1)}, f32[144,128]{1,0:T(8,128)S(1)}, u32[]{:S(2)}, u32[]{:S(2)}) collective-permute-start(f32[144,128]{1,0:T(8,128)S(1)} %get-tuple-element.24), channel_id=1, source_target_pairs={{0,8},{8,16},{16,24},{24,0},{1,9},{9,17},{17,25},{25,1},{2,10},{10... | collective-permute-start | bytes 221192 | tf_op jit(solution)/shard_map/ppermute | solution.py:276
  66.3 7.4 %collective-permute-start.12 = (f32[144,128]{1,0:T(8,128)S(1)}, f32[144,128]{1,0:T(8,128)S(1)}, u32[]{:S(2)}, u32[]{:S(2)}) collective-permute-start(f32[144,128]{1,0:T(8,128)S(1)} %get-tuple-element.24), channel_id=1, source_target_pairs={{0,16},{8,24},{16,0},{24,8},{1,17},{9,25},{17,1},{25,9},{2,18},{10... | collective-permute-start | bytes 221192 | tf_op jit(solution)/shard_map/ppermute | solution.py:276
  70.1 4.1 %collective-permute-start.13 = (f32[144,128]{1,0:T(8,128)S(1)}, f32[144,128]{1,0:T(8,128)S(1)}, u32[]{:S(2)}, u32[]{:S(2)}) collective-permute-start(f32[144,128]{1,0:T(8,128)S(1)} %get-tuple-element.24), channel_id=1, source_target_pairs={{0,24},{8,0},{16,8},{24,16},{1,25},{9,1},{17,9},{25,17},{2,26},{10... | collective-permute-start | bytes 221192 | tf_op jit(solution)/shard_map/ppermute | solution.py:276
  74.2 7.0 %collective-permute-start.14 = (f32[4,144,128]{2,1,0:T(8,128)S(1)}, f32[4,144,128]{2,1,0:T(8,128)S(1)}, u32[]{:S(2)}, u32[]{:S(2)}) collective-permute-start(f32[4,144,128]{2,1,0:T(8,128)S(1)} %bitcast_dynamic-update-slice_fusion.4), channel_id=1, source_target_pairs={{0,1},{1,2},{2,3},{3,0},{4,5},{5,6},{6,7},{7,4},{8,9},{9,10},{10,1... | collective-permute-start | bytes 884744 | tf_op jit(solution)/shard_map/ppermute | solution.py:276
  74.3 11.3 %collective-permute-start.16 = (f32[4,144,128]{2,1,0:T(8,128)S(1)}, f32[4,144,128]{2,1,0:T(8,128)S(1)}, u32[]{:S(2)}, u32[]{:S(2)}) collective-permute-start(f32[4,144,128]{2,1,0:T(8,128)S(1)} %bitcast_dynamic-update-slice_fusion.4), channel_id=1, source_target_pairs={{0,3},{1,0},{2,1},{3,2},{4,7},{5,4},{6,5},{7,6},{8,11},{9,8},{10,9... | collective-permute-start | bytes 884744 | tf_op jit(solution)/shard_map/ppermute | solution.py:276
  76.9 8.6 %collective-permute-start.15 = (f32[4,144,128]{2,1,0:T(8,128)S(1)}, f32[4,144,128]{2,1,0:T(8,128)S(1)}, u32[]{:S(2)}, u32[]{:S(2)}) collective-permute-start(f32[4,144,128]{2,1,0:T(8,128)S(1)} %bitcast_dynamic-update-slice_fusion.4), channel_id=1, source_target_pairs={{0,2},{1,3},{2,0},{3,1},{4,6},{5,7},{6,4},{7,5},{8,10},{9,11},{10,... | collective-permute-start | bytes 884744 | tf_op jit(solution)/shard_map/ppermute | solution.py:276
  85.6 48.3 %copy-start.1 = (f32[1024,1024]{1,0:T(8,128)S(1)}, f32[1024,1024]{1,0:T(8,128)}, u32[]{:S(2)}) copy-start(f32[1024,1024]{1,0:T(8,128)} %t_ref.3) | copy-start | bytes 12582916
  85.6 15.9 %collective-permute-start.17 = (f32[18,128,128]{2,1,0:T(8,128)S(1)}, f32[18,128,128]{2,1,0:T(8,128)S(1)}, u32[]{:S(2)}, u32[]{:S(2)}) collective-permute-start(f32[18,128,128]{2,1,0:T(8,128)S(1)} %bitcast.48), channel_id=1, source_target_pairs={{0,4},{4,0},{1,5},{5,1},{2,6},{6,2},{3,7},{7,3},{8,12},{12,8},{9,1... | collective-permute-start | bytes 3538952 | tf_op jit(solution)/shard_map/ppermute | solution.py:271
  140.7 2.0 %copy-start.2 = (bf16[1024,2048]{1,0:T(8,128)(2,1)}, bf16[1024,2048]{1,0:T(8,128)(2,1)S(1)}, u32[]{:S(2)}) copy-start(bf16[1024,2048]{1,0:T(8,128)(2,1)S(1)} %shard_map.48.w_ref) | copy-start | bytes 12582916
  142.8 2.2 %copy-start.3 = (bf16[1024,2048]{1,0:T(8,128)(2,1)S(1)}, bf16[1024,2048]{1,0:T(8,128)(2,1)}, u32[]{:S(2)}) copy-start(bf16[1024,2048]{1,0:T(8,128)(2,1)} %copy-done.2) | copy-start | bytes 12582916
Sparse Core Ops, SparseCore 0:
  16.7 115.7 all-gather.2

commit v7 on v4

--- a/solution.py
+++ b/solution.py
@@ -296,14 +296,14 @@
 def sum_all(mine, other, beside):
     shape = mine.shape
     ny, nx, nz = lax.axis_size("y"), lax.axis_size("x"), lax.axis_size(Z)
-    v = (mine + swap(other)).reshape(ny, nx, -1, 128)
-    v, beside = lax.optimization_barrier((scatter(v, "y"), beside))
-    v = scatter(v, "x")
+    v = (mine + swap(other)).reshape(nx, ny, -1, 128)
+    v, beside = lax.optimization_barrier((scatter(v, "x"), beside))
+    v = scatter(v, "y")
     hop = 1
     while hop < nz:
         v = v + lax.ppermute(v, Z, [(i, i ^ hop) for i in range(nz)])
         hop *= 2
-    return gather(gather(v, "x"), "y").reshape(shape), beside
+    return gather(gather(v, "y"), "x").reshape(shape), beside
 
 
 def local(train_grads, val_grads, wanted, owner):

time: 164 us -> 164 us (level)
  the two profiles are of different devices: /device:TPU:35 before, /device:TPU:1 now
where the time goes in v7:
time: 164 us; the launch traced here: 163 us
  Pallas kernels  61.4 us (37%)
  starting transfers between devices  40.4 us (25%)
  waiting for transfers between devices  38.1 us (23%)
  between operations  15.7 us (10%)
  local copies, waits for them, and re-layouts  5.43 us (3%)
  other arithmetic  2.32 us (1%)
    pallas_call x1, Pallas kernels, factor(): pl.pallas_call(functools.partial(factor_kernel, n, scale), out_shape=(jax...  32.5 us
    ppermute x12, waiting for transfers between devices, ring(): return lax.ppermute(v, axis, [(i, (i + k) % size) for i in range(size)])  24.6 us
    pallas_call x1, Pallas kernels, score(): pl.pallas_call(score_kernel, grid=(total // leads,), out_shape=jax.ShapeD...  17.5 us
    ppermute x12, starting transfers between devices, ring(): return lax.ppermute(v, axis, [(i, (i + k) % size) for i in range(size)])  16.2 us
    ppermute x2, starting transfers between devices, swap(): return lax.ppermute(v, 'core', [(0, 1), (1, 0)])  13 us
    ppermute x3, starting transfers between devices, sum_all(): v = v + lax.ppermute(v, Z, [(i, i ^ hop) for i in range(nz)])  8.72 us
    ppermute x3, waiting for transfers between devices, sum_all(): v = v + lax.ppermute(v, Z, [(i, i ^ hop) for i in range(nz)])  8.53 us
    pallas_call x1, Pallas kernels, solve(): pl.pallas_call(functools.partial(solve_kernel, n, features ** (-0.5)), ou...  6.77 us
  transfers between devices with their start and end apart: 19, of which 13 were waited for; matrix products, arithmetic and copies ran while one was open for 1% of the time, Pallas kernels for 27%

profile of v7, /device:TPU:1, one launch (start us, length us, event | category | flops | bytes accessed | tf_op | source)
XLA Modules:
  0.0 163.2 jit_solution(14714211985115581481)
XLA Ops:
  6.5 0.0 all-gather.3.cloned.1.call-start
  6.5 2.5 %collective-permute-start = (f32[2,8,1024]{2,1,0:T(8,128)}, f32[2,8,1024]{2,1,0:T(8,128)S(1)}, u32[]{:S(2)}, u32[]{:S(2)}) collective-permute-start(f32[2,8,1024]{2,1,0:T(8,128)} %param.5), channel_id=1, source_target_pairs={{0,32},{32,0},{1,33},{33,1},{2,34},{34,2},{3,35},{35,3},{4,36},{36... | collective-permute-start | bytes 196616 | tf_op jit(solution)/shard_map/ppermute | solution.py:317
  9.0 0.0 copy-start
  9.0 2.2 %copy-done = f32[1024,1024]{1,0:T(8,128)S(1)} copy-done((f32[1024,1024]{1,0:T(8,128)S(1)}, f32[1024,1024]{1,0:T(8,128)}, u32[]{:S(2)}) %copy-start) | copy-done | bytes 4194328
  11.2 0.0 copy-start.4
  11.2 4.6 %shard_map.46 = (f32[18,128,128]{2,1,0:T(8,128)S(1)}, f32[18,128,128]{2,1,0:T(8,128)S(1)}) custom-call(s32[1]{0:T(128)} %bitcast.core_ref, f32[1024,1024]{1,0:T(8,128)S(1)} %copy-done), custom_call_target="tpu_custom_call" | custom-call | flops 6442450944 | bytes 7340032 | tf_op jit(solution)/shard_map/pallas_call | solution.py:134
  15.8 0.0 collective-permute-done
  15.8 0.0 copy-done.4
  15.8 0.7 pad_maximum_fusion
  16.5 0.0 all-gather.3.cloned.1.call-update
  16.5 1.0 collective-permute-start.1
  17.6 2.5 %collective-permute-done.1 = f32[18,128,128]{2,1,0:T(8,128)S(1)} collective-permute-done((f32[18,128,128]{2,1,0:T(8,128)S(1)}, f32[18,128,128]{2,1,0:T(8,128)S(1)}, u32[]{:S(2)}, u32[]{:S(2)}) %collective-permute-start.1) | collective-permute-done | bytes 1179680 | tf_op jit(solution)/shard_map/ppermute | solution.py:270
  20.1 0.1 add.129
  20.2 0.0 copy-start.5
  20.2 0.1 dynamic-slice_bitcast_fusion.2
  20.3 1.3 collective-permute-start.2
  21.6 1.5 collective-permute-start.4
  23.1 1.5 collective-permute-start.3
  24.6 0.0 copy-done.5
  24.6 0.7 fusion.9
  27.4 0.7 compare_select_fusion.pick_ref
  28.1 1.7 %collective-permute-done.2 = f32[4,144,128]{2,1,0:T(8,128)S(1)} collective-permute-done((f32[4,144,128]{2,1,0:T(8,128)S(1)}, f32[4,144,128]{2,1,0:T(8,128)S(1)}, u32[]{:S(2)}, u32[]{:S(2)}) %collective-permute-start.2) | collective-permute-done | bytes 294944 | tf_op jit(solution)/shard_map/ppermute | solution.py:275
  29.8 0.0 collective-permute-done.4
  29.8 7.8 %collective-permute-done.3 = f32[4,144,128]{2,1,0:T(8,128)S(1)} collective-permute-done((f32[4,144,128]{2,1,0:T(8,128)S(1)}, f32[4,144,128]{2,1,0:T(8,128)S(1)}, u32[]{:S(2)}, u32[]{:S(2)}) %collective-permute-start.3) | collective-permute-done | bytes 294944 | tf_op jit(solution)/shard_map/ppermute | solution.py:275
  37.6 0.1 fusion.1
  37.7 1.4 collective-permute-start.5
  39.0 1.5 collective-permute-start.7
  40.6 1.6 collective-permute-start.6
  42.1 0.7 collective-permute-done.5
  42.8 0.0 collective-permute-done.7
  42.8 3.0 %collective-permute-done.6 = f32[144,128]{1,0:T(8,128)S(1)} collective-permute-done((f32[144,128]{1,0:T(8,128)S(1)}, f32[144,128]{1,0:T(8,128)S(1)}, u32[]{:S(2)}, u32[]{:S(2)}) %collective-permute-start.6) | collective-permute-done | bytes 73760 | tf_op jit(solution)/shard_map/ppermute | solution.py:275
  45.9 0.1 collective-permute-start.8
  46.0 3.6 %collective-permute-done.8 = f32[144,128]{1,0:T(8,128)S(1)} collective-permute-done((f32[144,128]{1,0:T(8,128)S(1)}, f32[144,128]{1,0:T(8,128)S(1)}, u32[]{:S(2)}, u32[]{:S(2)}) %collective-permute-start.8) | collective-permute-done | bytes 73760 | tf_op jit(solution)/shard_map/ppermute | solution.py:304
  49.6 3.0 %collective-permute-start.9 = (f32[144,128]{1,0:T(8,128)S(1)}, f32[144,128]{1,0:T(8,128)S(1)}, u32[]{:S(2)}, u32[]{:S(2)}) collective-permute-start(f32[144,128]{1,0:T(8,128)S(1)} %add.155), channel_id=1, source_target_pairs={{0,64},{32,96},{64,0},{96,32},{128,192},{160,224},{192,128},{224,1... | collective-permute-start | bytes 221192 | tf_op jit(solution)/shard_map/ppermute | solution.py:304
  52.5 2.3 %collective-permute-done.9 = f32[144,128]{1,0:T(8,128)S(1)} collective-permute-done((f32[144,128]{1,0:T(8,128)S(1)}, f32[144,128]{1,0:T(8,128)S(1)}, u32[]{:S(2)}, u32[]{:S(2)}) %collective-permute-start.9) | collective-permute-done | bytes 73760 | tf_op jit(solution)/shard_map/ppermute | solution.py:304
  54.8 5.7 %collective-permute-start.10 = (f32[144,128]{1,0:T(8,128)S(1)}, f32[144,128]{1,0:T(8,128)S(1)}, u32[]{:S(2)}, u32[]{:S(2)}) collective-permute-start(f32[144,128]{1,0:T(8,128)S(1)} %add.156), channel_id=1, source_target_pairs={{0,128},{32,160},{64,192},{96,224},{128,0},{160,32},{192,64},{224,... | collective-permute-start | bytes 221192 | tf_op jit(solution)/shard_map/ppermute | solution.py:304
  60.5 2.7 %collective-permute-done.10 = f32[144,128]{1,0:T(8,128)S(1)} collective-permute-done((f32[144,128]{1,0:T(8,128)S(1)}, f32[144,128]{1,0:T(8,128)S(1)}, u32[]{:S(2)}, u32[]{:S(2)}) %collective-permute-start.10) | collective-permute-done | bytes 73760 | tf_op jit(solution)/shard_map/ppermute | solution.py:304
  63.2 0.9 collective-permute-start.11
  64.1 2.7 %collective-permute-start.12 = (f32[144,128]{1,0:T(8,128)S(1)}, f32[144,128]{1,0:T(8,128)S(1)}, u32[]{:S(2)}, u32[]{:S(2)}) collective-permute-start(f32[144,128]{1,0:T(8,128)S(1)} %get-tuple-element.28), channel_id=1, source_target_pairs={{0,2},{1,3},{2,0},{3,1},{4,6},{5,7},{6,4},{7,5},{8,10},{9,11},{10,... | collective-permute-start | bytes 221192 | tf_op jit(solution)/shard_map/ppermute | solution.py:275
  66.8 1.1 collective-permute-start.13
  67.9 0.6 collective-permute-done.11
  68.6 2.7 %collective-permute-done.12 = f32[144,128]{1,0:T(8,128)S(1)} collective-permute-done((f32[144,128]{1,0:T(8,128)S(1)}, f32[144,128]{1,0:T(8,128)S(1)}, u32[]{:S(2)}, u32[]{:S(2)}) %collective-permute-start.12) | collective-permute-done | bytes 73760 | tf_op jit(solution)/shard_map/ppermute | solution.py:275
  71.2 0.0 collective-permute-done.13
  71.3 0.7 collective-permute-start.14
  71.9 2.1 %collective-permute-start.16 = (f32[4,144,128]{2,1,0:T(8,128)S(1)}, f32[4,144,128]{2,1,0:T(8,128)S(1)}, u32[]{:S(2)}, u32[]{:S(2)}) collective-permute-start(f32[4,144,128]{2,1,0:T(8,128)S(1)} %bitcast_dynamic-update-slice_fusion.4), channel_id=1, source_target_pairs={{0,24},{8,0},{16,8},{24,16},{1,25},{9,1},{17,9},{25,17},{2,26},{10... | collective-permute-start | bytes 884744 | tf_op jit(solution)/shard_map/ppermute | solution.py:275
  74.0 0.0 collective-permute-start.15
  74.0 0.1 broadcast_in_dim.38
  74.1 4.9 %collective-permute-done.14 = f32[4,144,128]{2,1,0:T(8,128)S(1)} collective-permute-done((f32[4,144,128]{2,1,0:T(8,128)S(1)}, f32[4,144,128]{2,1,0:T(8,128)S(1)}, u32[]{:S(2)}, u32[]{:S(2)}) %collective-permute-start.14) | collective-permute-done | bytes 294944 | tf_op jit(solution)/shard_map/ppermute | solution.py:275
  79.1 3.1 %collective-permute-done.15 = f32[4,144,128]{2,1,0:T(8,128)S(1)} collective-permute-done((f32[4,144,128]{2,1,0:T(8,128)S(1)}, f32[4,144,128]{2,1,0:T(8,128)S(1)}, u32[]{:S(2)}, u32[]{:S(2)}) %collective-permute-start.15) | collective-permute-done | bytes 294944 | tf_op jit(solution)/shard_map/ppermute | solution.py:275
  82.2 0.0 collective-permute-done.16
  82.2 0.0 copy-start.1
  82.3 12.0 %collective-permute-start.17 = (f32[18,128,128]{2,1,0:T(8,128)S(1)}, f32[18,128,128]{2,1,0:T(8,128)S(1)}, u32[]{:S(2)}, u32[]{:S(2)}) collective-permute-start(f32[18,128,128]{2,1,0:T(8,128)S(1)} %bitcast.48), channel_id=1, source_target_pairs={{0,4},{4,0},{1,5},{5,1},{2,6},{6,2},{3,7},{7,3},{8,12},{12,8},{9,1... | collective-permute-start | bytes 3538952 | tf_op jit(solution)/shard_map/ppermute | solution.py:270
  94.2 2.5 %collective-permute-done.17.other_ref = f32[18,128,128]{2,1,0:T(8,128)S(1)} collective-permute-done((f32[18,128,128]{2,1,0:T(8,128)S(1)}, f32[18,128,128]{2,1,0:T(8,128)S(1)}, u32[]{:S(2)}, u32[]{:S(2)}) %collective-permute-start.17) | collective-permute-done | bytes 1179680 | tf_op jit(solution)/shard_map/ppermute | solution.py:270
  96.7 32.5 %shard_map.47 = (f32[10,256,256]{2,1,0:T(8,128)S(1)}, f32[4,256,256]{2,1,0:T(8,128)S(1)}) custom-call(s32[1]{0:T(128)} %bitcast.core_ref, f32[18,128,128]{2,1,0:T(8,128)S(1)} %bitcast.49, f32[18,128,128]{2,1,0:T(8,128)S(1)} %collective-permute-done.17.other_ref), custom_call_target="tpu_custom_call" | custom-call | flops 34359738368 | bytes 6291456 | tf_op jit(solution)/shard_map/pallas_call | solution.py:190
  129.2 0.0 copy-done.1
  129.2 6.8 %shard_map.48 = (bf16[1024,1024]{1,0:T(8,128)(2,1)S(1)}, bf16[1024,1024]{1,0:T(8,128)(2,1)S(1)}) custom-call(f32[1024,1024]{1,0:T(8,128)S(1)} %copy-done.1, f32[10,256,256]{2,1,0:T(8,128)S(1)} %get-tuple-element.22.l_ref, f32[4,256,256]{2,1,0:T(8,128)S(1)} %get-tuple-element.23.d_ref), custom_call_target="tpu_custom_call" | custom-call | flops 6442450944 | bytes 12582912 | tf_op jit(solution)/shard_map/pallas_call | solution.py:226
  136.0 0.0 copy-start.2
  136.0 1.3 copy-done.2
  137.3 0.0 all-gather.3.cloned.1.call-done
  137.3 0.0 copy-start.3
  137.3 1.6 copy-done.3
  138.9 17.5 %shard_map.49 = f32[1024,2048]{1,0:T(8,128)} custom-call(s32[64]{0:T(128)S(1)} %compare_select_fusion.pick_ref, bf16[1024,1024]{1,0:T(8,128)(2,1)S(1)} %get-tuple-element.24.wh_ref, bf16[1024,1024]{1,0:T(8,128)(2,1)S(1)} %copy-done.3, f32[32,4,4,8,1024]{4,3,2,1,0:T(8,128)} %bitcast.52), custom_call_target="tpu_custom_call" | custom-call | flops 12884901888 | bytes 20971520 | tf_op jit(solution)/shard_map/pallas_call | solution.py:254
  (13 shorter events, 0.2 us)
Async XLA Ops:
  6.5 130.7 %all-gather.3.cloned.1.call-start = ((), (), s32[]{:S(2)}) async-start(), calls=%async_computation | async-start | bytes 16908288 | tf_op jit(solution)/shard_map/all_gather | solution.py:329
  6.5 9.3 %collective-permute-start = (f32[2,8,1024]{2,1,0:T(8,128)}, f32[2,8,1024]{2,1,0:T(8,128)S(1)}, u32[]{:S(2)}, u32[]{:S(2)}) collective-permute-start(f32[2,8,1024]{2,1,0:T(8,128)} %param.5), channel_id=1, source_target_pairs={{0,32},{32,0},{1,33},{33,1},{2,34},{34,2},{3,35},{35,3},{4,36},{36... | collective-permute-start | bytes 196616 | tf_op jit(solution)/shard_map/ppermute | solution.py:317
  9.0 2.2 %copy-start = (f32[1024,1024]{1,0:T(8,128)S(1)}, f32[1024,1024]{1,0:T(8,128)}, u32[]{:S(2)}) copy-start(f32[1024,1024]{1,0:T(8,128)} %t_ref.3) | copy-start | bytes 12582916
  11.2 4.6 %copy-start.4 = (f32[2,8,1024]{2,1,0:T(8,128)S(1)}, f32[2,8,1024]{2,1,0:T(8,128)}, u32[]{:S(2)}) copy-start(f32[2,8,1024]{2,1,0:T(8,128)} %param.5) | copy-start | bytes 196612
  16.5 3.5 %collective-permute-start.1 = (f32[18,128,128]{2,1,0:T(8,128)S(1)}, f32[18,128,128]{2,1,0:T(8,128)S(1)}, u32[]{:S(2)}, u32[]{:S(2)}) collective-permute-start(f32[18,128,128]{2,1,0:T(8,128)S(1)} %get-tuple-element.19), channel_id=1, source_target_pairs={{0,4},{4,0},{1,5},{5,1},{2,6},{6,2},{3,7},{7,3},{8,12},{12,8},{9,1... | collective-permute-start | bytes 3538952 | tf_op jit(solution)/shard_map/ppermute | solution.py:270
  20.2 4.4 %copy-start.5 = (s32[64]{0:T(128)S(1)}, s32[64]{0:T(128)}, u32[]{:S(2)}) copy-start(s32[64]{0:T(128)} %param.7) | copy-start | bytes 772
  20.3 9.5 %collective-permute-start.2 = (f32[4,144,128]{2,1,0:T(8,128)S(1)}, f32[4,144,128]{2,1,0:T(8,128)S(1)}, u32[]{:S(2)}, u32[]{:S(2)}) collective-permute-start(f32[4,144,128]{2,1,0:T(8,128)S(1)} %get-tuple-element.29), channel_id=1, source_target_pairs={{0,8},{8,16},{16,24},{24,0},{1,9},{9,17},{17,25},{25,1},{2,10},{10... | collective-permute-start | bytes 884744 | tf_op jit(solution)/shard_map/ppermute | solution.py:275
  21.6 8.2 %collective-permute-start.4 = (f32[4,144,128]{2,1,0:T(8,128)S(1)}, f32[4,144,128]{2,1,0:T(8,128)S(1)}, u32[]{:S(2)}, u32[]{:S(2)}) collective-permute-start(f32[4,144,128]{2,1,0:T(8,128)S(1)} %get-tuple-element.30), channel_id=1, source_target_pairs={{0,24},{8,0},{16,8},{24,16},{1,25},{9,1},{17,9},{25,17},{2,26},{10... | collective-permute-start | bytes 884744 | tf_op jit(solution)/shard_map/ppermute | solution.py:275
  23.1 14.5 %collective-permute-start.3 = (f32[4,144,128]{2,1,0:T(8,128)S(1)}, f32[4,144,128]{2,1,0:T(8,128)S(1)}, u32[]{:S(2)}, u32[]{:S(2)}) collective-permute-start(f32[4,144,128]{2,1,0:T(8,128)S(1)} %get-tuple-element.31), channel_id=1, source_target_pairs={{0,16},{8,24},{16,0},{24,8},{1,17},{9,25},{17,1},{25,9},{2,18},{10... | collective-permute-start | bytes 884744 | tf_op jit(solution)/shard_map/ppermute | solution.py:275
  37.7 5.1 %collective-permute-start.5 = (f32[144,128]{1,0:T(8,128)S(1)}, f32[144,128]{1,0:T(8,128)S(1)}, u32[]{:S(2)}, u32[]{:S(2)}) collective-permute-start(f32[144,128]{1,0:T(8,128)S(1)} %get-tuple-element.32), channel_id=1, source_target_pairs={{0,1},{1,2},{2,3},{3,0},{4,5},{5,6},{6,7},{7,4},{8,9},{9,10},{10,1... | collective-permute-start | bytes 221192 | tf_op jit(solution)/shard_map/ppermute | solution.py:275
  39.0 3.8 %collective-permute-start.7 = (f32[144,128]{1,0:T(8,128)S(1)}, f32[144,128]{1,0:T(8,128)S(1)}, u32[]{:S(2)}, u32[]{:S(2)}) collective-permute-start(f32[144,128]{1,0:T(8,128)S(1)} %get-tuple-element.33), channel_id=1, source_target_pairs={{0,3},{1,0},{2,1},{3,2},{4,7},{5,4},{6,5},{7,6},{8,11},{9,8},{10,9... | collective-permute-start | bytes 221192 | tf_op jit(solution)/shard_map/ppermute | solution.py:275
  40.6 5.3 %collective-permute-start.6 = (f32[144,128]{1,0:T(8,128)S(1)}, f32[144,128]{1,0:T(8,128)S(1)}, u32[]{:S(2)}, u32[]{:S(2)}) collective-permute-start(f32[144,128]{1,0:T(8,128)S(1)} %get-tuple-element.34), channel_id=1, source_target_pairs={{0,2},{1,3},{2,0},{3,1},{4,6},{5,7},{6,4},{7,5},{8,10},{9,11},{10,... | collective-permute-start | bytes 221192 | tf_op jit(solution)/shard_map/ppermute | solution.py:275
  45.9 3.7 %collective-permute-start.8 = (f32[144,128]{1,0:T(8,128)S(1)}, f32[144,128]{1,0:T(8,128)S(1)}, u32[]{:S(2)}, u32[]{:S(2)}) collective-permute-start(f32[144,128]{1,0:T(8,128)S(1)} %fusion.3), channel_id=1, source_target_pairs={{0,32},{32,0},{64,96},{96,64},{128,160},{160,128},{192,224},{224,1... | collective-permute-start | bytes 221192 | tf_op jit(solution)/shard_map/ppermute | solution.py:304
  49.6 5.2 %collective-permute-start.9 = (f32[144,128]{1,0:T(8,128)S(1)}, f32[144,128]{1,0:T(8,128)S(1)}, u32[]{:S(2)}, u32[]{:S(2)}) collective-permute-start(f32[144,128]{1,0:T(8,128)S(1)} %add.155), channel_id=1, source_target_pairs={{0,64},{32,96},{64,0},{96,32},{128,192},{160,224},{192,128},{224,1... | collective-permute-start | bytes 221192 | tf_op jit(solution)/shard_map/ppermute | solution.py:304
  54.8 8.4 %collective-permute-start.10 = (f32[144,128]{1,0:T(8,128)S(1)}, f32[144,128]{1,0:T(8,128)S(1)}, u32[]{:S(2)}, u32[]{:S(2)}) collective-permute-start(f32[144,128]{1,0:T(8,128)S(1)} %add.156), channel_id=1, source_target_pairs={{0,128},{32,160},{64,192},{96,224},{128,0},{160,32},{192,64},{224,... | collective-permute-start | bytes 221192 | tf_op jit(solution)/shard_map/ppermute | solution.py:304
  63.2 5.3 %collective-permute-start.11 = (f32[144,128]{1,0:T(8,128)S(1)}, f32[144,128]{1,0:T(8,128)S(1)}, u32[]{:S(2)}, u32[]{:S(2)}) collective-permute-start(f32[144,128]{1,0:T(8,128)S(1)} %get-tuple-element.28), channel_id=1, source_target_pairs={{0,1},{1,2},{2,3},{3,0},{4,5},{5,6},{6,7},{7,4},{8,9},{9,10},{10,1... | collective-permute-start | bytes 221192 | tf_op jit(solution)/shard_map/ppermute | solution.py:275
  64.1 7.1 %collective-permute-start.12 = (f32[144,128]{1,0:T(8,128)S(1)}, f32[144,128]{1,0:T(8,128)S(1)}, u32[]{:S(2)}, u32[]{:S(2)}) collective-permute-start(f32[144,128]{1,0:T(8,128)S(1)} %get-tuple-element.28), channel_id=1, source_target_pairs={{0,2},{1,3},{2,0},{3,1},{4,6},{5,7},{6,4},{7,5},{8,10},{9,11},{10,... | collective-permute-start | bytes 221192 | tf_op jit(solution)/shard_map/ppermute | solution.py:275
  66.8 4.4 %collective-permute-start.13 = (f32[144,128]{1,0:T(8,128)S(1)}, f32[144,128]{1,0:T(8,128)S(1)}, u32[]{:S(2)}, u32[]{:S(2)}) collective-permute-start(f32[144,128]{1,0:T(8,128)S(1)} %get-tuple-element.28), channel_id=1, source_target_pairs={{0,3},{1,0},{2,1},{3,2},{4,7},{5,4},{6,5},{7,6},{8,11},{9,8},{10,9... | collective-permute-start | bytes 221192 | tf_op jit(solution)/shard_map/ppermute | solution.py:275
  71.3 7.8 %collective-permute-start.14 = (f32[4,144,128]{2,1,0:T(8,128)S(1)}, f32[4,144,128]{2,1,0:T(8,128)S(1)}, u32[]{:S(2)}, u32[]{:S(2)}) collective-permute-start(f32[4,144,128]{2,1,0:T(8,128)S(1)} %bitcast_dynamic-update-slice_fusion.4), channel_id=1, source_target_pairs={{0,8},{8,16},{16,24},{24,0},{1,9},{9,17},{17,25},{25,1},{2,10},{10... | collective-permute-start | bytes 884744 | tf_op jit(solution)/shard_map/ppermute | solution.py:275
  71.9 10.3 %collective-permute-start.16 = (f32[4,144,128]{2,1,0:T(8,128)S(1)}, f32[4,144,128]{2,1,0:T(8,128)S(1)}, u32[]{:S(2)}, u32[]{:S(2)}) collective-permute-start(f32[4,144,128]{2,1,0:T(8,128)S(1)} %bitcast_dynamic-update-slice_fusion.4), channel_id=1, source_target_pairs={{0,24},{8,0},{16,8},{24,16},{1,25},{9,1},{17,9},{25,17},{2,26},{10... | collective-permute-start | bytes 884744 | tf_op jit(solution)/shard_map/ppermute | solution.py:275
  74.0 8.2 %collective-permute-start.15 = (f32[4,144,128]{2,1,0:T(8,128)S(1)}, f32[4,144,128]{2,1,0:T(8,128)S(1)}, u32[]{:S(2)}, u32[]{:S(2)}) collective-permute-start(f32[4,144,128]{2,1,0:T(8,128)S(1)} %bitcast_dynamic-update-slice_fusion.4), channel_id=1, source_target_pairs={{0,16},{8,24},{16,0},{24,8},{1,17},{9,25},{17,1},{25,9},{2,18},{10... | collective-permute-start | bytes 884744 | tf_op jit(solution)/shard_map/ppermute | solution.py:275
  82.2 46.9 %copy-start.1 = (f32[1024,1024]{1,0:T(8,128)S(1)}, f32[1024,1024]{1,0:T(8,128)}, u32[]{:S(2)}) copy-start(f32[1024,1024]{1,0:T(8,128)} %t_ref.3) | copy-start | bytes 12582916
  82.3 14.4 %collective-permute-start.17 = (f32[18,128,128]{2,1,0:T(8,128)S(1)}, f32[18,128,128]{2,1,0:T(8,128)S(1)}, u32[]{:S(2)}, u32[]{:S(2)}) collective-permute-start(f32[18,128,128]{2,1,0:T(8,128)S(1)} %bitcast.48), channel_id=1, source_target_pairs={{0,4},{4,0},{1,5},{5,1},{2,6},{6,2},{3,7},{7,3},{8,12},{12,8},{9,1... | collective-permute-start | bytes 3538952 | tf_op jit(solution)/shard_map/ppermute | solution.py:270
  136.0 1.3 copy-start.2
  137.3 1.6 copy-start.3
Sparse Core Ops, SparseCore 0:
  16.7 116.1 all-gather.2
